TPU v7x, 512 devices: a whole 4x4x16 slice. The times are simulated.
512 devices in a mesh: vocab: 64 (over x, z), rows: 8 (over y, core).
Axes of the slice: x: 4, y: 4, z: 16, core: 2. Of those that a mesh axis runs over, the one named last changes fastest.
Arguments:
- hidden: bfloat16 [384, 8192], P('vocab', 'rows'), may hold values from -24 to 24
- head: bfloat16 [76032, 8192], P('vocab', 'rows'), may hold values from -0.2 to 0.2
- targets: int32 [384], replicated, may hold values from 0 to 76031
- upstream: float32 [384], replicated, may hold values from 4 to 40
Outputs:
- token_loss: float32 [384], P('rows')
- grad_hidden: bfloat16 [384, 8192], P('vocab', 'rows')
- grad_head: bfloat16 [76032, 8192], P('vocab', 'rows')
All inputs are finite; a program needn't handle non-finite values.
Results may differ from a plain program's by a relative error of at most 0.006.
Values may be sent and summed in bfloat16 or wider, within the bound.
No kernel may reach another device: no remote copies, remote signals or barrier semaphores. Data moves between devices by JAX's collectives and lax.ppermute only.
A program may use at most 64 MiB of HBM per device.

v0:
```python
import jax
import jax.numpy as jnp
from jax import lax
from jax.sharding import PartitionSpec as P


def softmax_grad(logits, row_targets, row_weight, width):
    offset = lax.axis_index("vocab") * width
    columns = lax.broadcasted_iota(jnp.int32, logits.shape, 1) + offset
    target_mask = columns == row_targets[:, None]
    local_top = jnp.max(logits, axis=1)
    target_logit = jnp.sum(jnp.where(target_mask, logits, jnp.float32(0.0)), axis=1)
    global_top = lax.pmax(local_top, "vocab")
    exp_total = jnp.sum(jnp.exp(logits - global_top[:, None]), axis=1)
    exp_total, target_logit = lax.psum((exp_total, target_logit), "vocab")
    lse = global_top + jnp.log(exp_total)
    probability = jnp.exp(logits - lse[:, None])
    grad_logits = ((probability - target_mask.astype(jnp.float32)) * row_weight[:, None]).astype(
        jnp.bfloat16
    )
    return (lse - target_logit, grad_logits)


def per_device(hidden, head, targets, upstream):
    width = head.shape[0]
    hidden_all = lax.all_gather(hidden, "vocab", axis=0, tiled=True)
    token_count = hidden_all.shape[0]
    own_rows = token_count // lax.axis_size("rows")
    row_first = lax.axis_index("rows") * own_rows
    window_rows = hidden_all
    logits = lax.psum_scatter(
        lax.dot_general(
            window_rows, head, (((1,), (1,)), ((), ())), preferred_element_type=jnp.float32
        ),
        "rows",
        scatter_dimension=0,
        tiled=True,
    )
    row_targets = lax.dynamic_slice_in_dim(targets, row_first, own_rows, 0)
    row_weight = lax.dynamic_slice_in_dim(upstream, row_first, own_rows, 0)
    token_loss, grad_local = softmax_grad(logits, row_targets, row_weight, width)
    grad_all = lax.all_gather(grad_local, "rows", axis=0, tiled=True)
    window_rows = grad_all
    grad_hidden = lax.psum_scatter(
        jnp.dot(window_rows, head, preferred_element_type=jnp.float32),
        "vocab",
        scatter_dimension=0,
        tiled=True,
    ).astype(jnp.bfloat16)
    grad_head = lax.dot_general(
        grad_all, hidden_all, (((0,), (0,)), ((), ())), preferred_element_type=jnp.float32
    ).astype(jnp.bfloat16)
    return (token_loss, grad_hidden, grad_head)


def solution(mesh):
    return jax.shard_map(
        per_device,
        mesh=mesh,
        in_specs=(P("vocab", "rows"), P("vocab", "rows"), P(), P()),
        out_specs=(P("rows"), P("vocab", "rows"), P("vocab", "rows")),
        check_vma=False,
    )
```

profile of v0, /device:TPU:16, one launch (start us, length us, event | category | flops | bytes accessed | tf_op | source)
XLA Modules:
  0.0 698.1 jit_solution(61981150488511463)
XLA Ops:
  7.2 0.0 copy-start
  7.2 0.0 reduce-scatter.4.cloned.1.call-start
  7.2 107.3 %all-gather = bf16[64,6,1024]{2,1,0:T(8,128)(2,1)S(1)} all-gather(bf16[1,6,1024]{2,1,0:T(8,128)(2,1)} %bitcast.10), channel_id=1, replica_groups=mesh['vocab'=64,'rows'=8] {'vocab'}, dimensions={0}, use_global_device_ids=true | all-gather | bytes 798720 | tf_op jit(solution)/shard_map/all_gather | solution.py:26
  114.5 1.1 reshape.11
  115.7 3.6 fusion.7
  119.3 0.0 reduce-scatter.4.cloned.1.call-update
  119.3 0.8 dynamic_slice.6
  120.1 0.8 dynamic_slice.7
  120.9 30.2 %reduce-scatter.4.cloned.1.call-done = f32[48,1188]{1,0:T(8,128)} async-done(((f32[384,1188]{1,0:T(8,128)}), f32[48,1188]{1,0:T(8,128)}) %reduce-scatter.4.cloned.1.call-update) | async-done | bytes 228112 | tf_op jit(solution)/shard_map/reduce_scatter | solution.py:31
  151.0 1.1 reduce_max.9
  152.1 144.2 %pmax.7 = f32[48]{0:T(128)S(1)} all-reduce(f32[48]{0:T(128)S(1)} %reduce_max.9), channel_id=1, replica_groups=mesh['vocab'=64,'rows'=8] {'vocab'}, use_global_device_ids=true, to_apply=%region_2.3 | all-reduce | flops 48 | bytes 384 | tf_op jit(solution)/shard_map/pmax | solution.py:13
  296.3 1.2 fusion.1
  297.4 138.0 %all-reduce.2 = (f32[48]{0:T(128)S(1)}, f32[48]{0:T(128)S(1)}) all-reduce(f32[48]{0:T(128)S(1)} %get-tuple-element.4, f32[48]{0:T(128)S(1)} %get-tuple-element.3), channel_id=1, replica_groups=mesh['vocab'=64,'rows'=8] {'vocab'}, use_global_device_ids=true, to_apply=%region_4.5 | all-reduce | flops 96 | bytes 768 | tf_op jit(solution)/shard_map/psum | solution.py:15
  435.4 0.5 fusion.5
  435.9 1.1 fusion.4
  437.0 17.1 %all_gather.7 = bf16[384,1188]{1,0:T(8,128)(2,1)S(1)} all-gather(bf16[48,1188]{1,0:T(8,128)(2,1)S(1)} %fusion.4), channel_id=1, replica_groups=mesh['vocab'=64,'rows'=8] {'rows'}, dimensions={0}, use_global_device_ids=true | all-gather | bytes 1026432 | tf_op jit(solution)/shard_map/all_gather | solution.py:42
  454.1 2.3 fusion.8
  456.5 151.1 %fusion = f32[8,1024]{1,0:T(8,128)S(1)} fusion(f32[384,1024]{1,0:T(8,128)} %fusion.8), kind=kCustom, calls=%all-reduce-scatter | all-reduce-scatter fusion | flops 524289 | bytes 1607680
  607.6 1.3 collective-permute-start.15
  608.9 1.3 collective-permute-start.1
  610.2 2.2 collective-permute-start.2
  612.5 1.3 collective-permute-start.3
  613.8 1.7 collective-permute-start.4
  615.4 1.3 collective-permute-start.5
  616.7 0.0 collective-permute-done.1
  616.7 1.9 collective-permute-start.6
  618.6 12.7 %collective-permute-start.7 = (bf16[8,1024]{1,0:T(8,128)(2,1)S(1)}, bf16[8,1024]{1,0:T(8,128)(2,1)}, u32[]{:S(2)}, u32[]{:S(2)}) collective-permute-start(bf16[8,1024]{1,0:T(8,128)(2,1)S(1)} %convert.30), channel_id=1, source_target_pairs={{0,64},{8,72},{16,80},{24,88},{32,96},{40,104},{48,112},{56,120},{... | collective-permute-start | bytes 49160
  631.3 20.8 %collective-permute-start.8 = (bf16[8,1024]{1,0:T(8,128)(2,1)S(1)}, bf16[8,1024]{1,0:T(8,128)(2,1)}, u32[]{:S(2)}, u32[]{:S(2)}) collective-permute-start(bf16[8,1024]{1,0:T(8,128)(2,1)S(1)} %convert.30), channel_id=1, source_target_pairs={{0,72},{8,80},{16,88},{24,96},{32,104},{40,112},{48,120},{56,128},... | collective-permute-start | bytes 49160
  652.1 6.1 collective-permute-start.9
  658.2 0.0 collective-permute-done.5
  658.2 0.6 copy-done.1
  658.9 6.4 collective-permute-start.10
  665.2 1.3 dynamic-slice.4
  667.2 1.3 collective-permute-start.11
  668.5 0.0 collective-permute-done.7
  668.5 1.3 collective-permute-start.12
  669.8 1.3 collective-permute-start.13
  671.1 0.0 collective-permute-done.9
  671.1 1.3 collective-permute-start.14
  672.4 0.0 collective-permute-done.10
  672.4 3.1 collective-permute-start
  675.5 4.0 convolution_convert_fusion
  679.5 0.6 copy-done.2
  680.1 0.0 copy-done.3
  680.1 0.0 copy-done.4
  680.1 0.6 copy-done.5
  680.7 9.8 %concatenate = bf16[134,1024]{1,0:T(8,128)(2,1)S(1)} concatenate(bf16[6,1024]{1,0:T(8,128)(2,1)S(1)} %collective-permute-done.15, bf16[8,1024]{1,0:T(8,128)(2,1)} %copy-done.5, bf16[8,1024]{1,0:T(8,128)(2,1)} %copy-done.4, bf16[8,1024]{1,0:T(8,128)(2,1)} %copy-done.3, bf16[8,1024]{1,0:T(8,128)(2,1)} %copy-done.2, bf16[8,1024]{1,0:T(8,128)(2,1)} %collective-permute-done.10, ...), dimensions={0} | concatenate | bytes 565248
  690.6 0.6 dynamic-slice_convert_fusion
  (20 shorter events, 0.1 us)
Async XLA Ops:
  7.2 108.5 %copy-start = (bf16[1188,1024]{1,0:T(8,128)(2,1)S(1)}, bf16[1188,1024]{1,0:T(8,128)(2,1)}, u32[]{:S(2)}) copy-start(bf16[1188,1024]{1,0:T(8,128)(2,1)} %param.5) | copy-start | bytes 7299076
  7.2 143.9 %reduce-scatter.4.cloned.1.call-start = ((), (), s32[]{:S(2)}) async-start(), calls=%async_computation.1 | async-start | bytes 2211840 | tf_op jit(solution)/shard_map/reduce_scatter | solution.py:31
  607.6 7.8 %collective-permute-start.15 = (bf16[6,1024]{1,0:T(8,128)(2,1)S(1)}, bf16[6,1024]{1,0:T(8,128)(2,1)S(1)}, u32[]{:S(2)}, u32[]{:S(2)}) collective-permute-start(bf16[6,1024]{1,0:T(8,128)(2,1)S(1)} %slice), channel_id=1, source_target_pairs={{0,128},{8,136},{16,144},{24,152},{32,160},{40,168},{48,176},{56,1... | collective-permute-start | bytes 36872
  608.9 7.8 %collective-permute-start.1 = (bf16[8,1024]{1,0:T(8,128)(2,1)S(1)}, bf16[8,1024]{1,0:T(8,128)(2,1)S(1)}, u32[]{:S(2)}, u32[]{:S(2)}) collective-permute-start(bf16[8,1024]{1,0:T(8,128)(2,1)S(1)} %convert.30), channel_id=1, source_target_pairs={{0,16},{8,24},{16,32},{24,40},{32,48},{40,56},{48,64},{56,72},{64,... | collective-permute-start | bytes 49160
  610.2 8.4 %collective-permute-start.2 = (bf16[8,1024]{1,0:T(8,128)(2,1)S(1)}, bf16[8,1024]{1,0:T(8,128)(2,1)S(1)}, u32[]{:S(2)}, u32[]{:S(2)}) collective-permute-start(bf16[8,1024]{1,0:T(8,128)(2,1)S(1)} %convert.30), channel_id=1, source_target_pairs={{0,24},{8,32},{16,40},{24,48},{32,56},{40,64},{48,72},{56,80},{64,... | collective-permute-start | bytes 49160
  612.5 18.9 %collective-permute-start.3 = (bf16[8,1024]{1,0:T(8,128)(2,1)S(1)}, bf16[8,1024]{1,0:T(8,128)(2,1)S(1)}, u32[]{:S(2)}, u32[]{:S(2)}) collective-permute-start(bf16[8,1024]{1,0:T(8,128)(2,1)S(1)} %convert.30), channel_id=1, source_target_pairs={{0,32},{8,40},{16,48},{24,56},{32,64},{40,72},{48,80},{56,88},{64,... | collective-permute-start | bytes 49160
  613.8 38.4 %collective-permute-start.4 = (bf16[8,1024]{1,0:T(8,128)(2,1)S(1)}, bf16[8,1024]{1,0:T(8,128)(2,1)S(1)}, u32[]{:S(2)}, u32[]{:S(2)}) collective-permute-start(bf16[8,1024]{1,0:T(8,128)(2,1)S(1)} %convert.30), channel_id=1, source_target_pairs={{0,40},{8,48},{16,56},{24,64},{32,72},{40,80},{48,88},{56,96},{64,... | collective-permute-start | bytes 49160
  615.4 42.8 %collective-permute-start.5 = (bf16[8,1024]{1,0:T(8,128)(2,1)S(1)}, bf16[8,1024]{1,0:T(8,128)(2,1)S(1)}, u32[]{:S(2)}, u32[]{:S(2)}) collective-permute-start(bf16[8,1024]{1,0:T(8,128)(2,1)S(1)} %convert.30), channel_id=1, source_target_pairs={{0,48},{8,56},{16,64},{24,72},{32,80},{40,88},{48,96},{56,104},{64... | collective-permute-start | bytes 49160
  616.7 50.4 %collective-permute-start.6 = (bf16[8,1024]{1,0:T(8,128)(2,1)S(1)}, bf16[8,1024]{1,0:T(8,128)(2,1)}, u32[]{:S(2)}, u32[]{:S(2)}) collective-permute-start(bf16[8,1024]{1,0:T(8,128)(2,1)S(1)} %convert.30), channel_id=1, source_target_pairs={{0,56},{8,64},{16,72},{24,80},{32,88},{40,96},{48,104},{56,112},{6... | collective-permute-start | bytes 49160
  618.6 49.8 %collective-permute-start.7 = (bf16[8,1024]{1,0:T(8,128)(2,1)S(1)}, bf16[8,1024]{1,0:T(8,128)(2,1)}, u32[]{:S(2)}, u32[]{:S(2)}) collective-permute-start(bf16[8,1024]{1,0:T(8,128)(2,1)S(1)} %convert.30), channel_id=1, source_target_pairs={{0,64},{8,72},{16,80},{24,88},{32,96},{40,104},{48,112},{56,120},{... | collective-permute-start | bytes 49160
  631.3 38.5 %collective-permute-start.8 = (bf16[8,1024]{1,0:T(8,128)(2,1)S(1)}, bf16[8,1024]{1,0:T(8,128)(2,1)}, u32[]{:S(2)}, u32[]{:S(2)}) collective-permute-start(bf16[8,1024]{1,0:T(8,128)(2,1)S(1)} %convert.30), channel_id=1, source_target_pairs={{0,72},{8,80},{16,88},{24,96},{32,104},{40,112},{48,120},{56,128},... | collective-permute-start | bytes 49160
  652.1 18.9 %collective-permute-start.9 = (bf16[8,1024]{1,0:T(8,128)(2,1)S(1)}, bf16[8,1024]{1,0:T(8,128)(2,1)}, u32[]{:S(2)}, u32[]{:S(2)}) collective-permute-start(bf16[8,1024]{1,0:T(8,128)(2,1)S(1)} %convert.30), channel_id=1, source_target_pairs={{0,80},{8,88},{16,96},{24,104},{32,112},{40,120},{48,128},{56,136}... | collective-permute-start | bytes 49160
  658.2 0.6 copy-start.1
  658.9 13.5 %collective-permute-start.10 = (bf16[8,1024]{1,0:T(8,128)(2,1)S(1)}, bf16[8,1024]{1,0:T(8,128)(2,1)}, u32[]{:S(2)}, u32[]{:S(2)}) collective-permute-start(bf16[8,1024]{1,0:T(8,128)(2,1)S(1)} %convert.30), channel_id=1, source_target_pairs={{0,88},{8,96},{16,104},{24,112},{32,120},{40,128},{48,136},{56,144... | collective-permute-start | bytes 49160
  667.2 12.3 %collective-permute-start.11 = (bf16[8,1024]{1,0:T(8,128)(2,1)S(1)}, bf16[8,1024]{1,0:T(8,128)(2,1)S(1)}, u32[]{:S(2)}, u32[]{:S(2)}) collective-permute-start(bf16[8,1024]{1,0:T(8,128)(2,1)S(1)} %convert.30), channel_id=1, source_target_pairs={{0,96},{8,104},{16,112},{24,120},{32,128},{40,136},{48,144},{56,15... | collective-permute-start | bytes 49160
  668.5 11.0 %collective-permute-start.12 = (bf16[8,1024]{1,0:T(8,128)(2,1)S(1)}, bf16[8,1024]{1,0:T(8,128)(2,1)S(1)}, u32[]{:S(2)}, u32[]{:S(2)}) collective-permute-start(bf16[8,1024]{1,0:T(8,128)(2,1)S(1)} %convert.30), channel_id=1, source_target_pairs={{0,104},{8,112},{16,120},{24,128},{32,136},{40,144},{48,152},{56,1... | collective-permute-start | bytes 49160
  669.8 9.7 %collective-permute-start.13 = (bf16[8,1024]{1,0:T(8,128)(2,1)S(1)}, bf16[8,1024]{1,0:T(8,128)(2,1)S(1)}, u32[]{:S(2)}, u32[]{:S(2)}) collective-permute-start(bf16[8,1024]{1,0:T(8,128)(2,1)S(1)} %convert.30), channel_id=1, source_target_pairs={{0,112},{8,120},{16,128},{24,136},{32,144},{40,152},{48,160},{56,1... | collective-permute-start | bytes 49160
  671.1 8.5 %collective-permute-start.14 = (bf16[8,1024]{1,0:T(8,128)(2,1)S(1)}, bf16[8,1024]{1,0:T(8,128)(2,1)S(1)}, u32[]{:S(2)}, u32[]{:S(2)}) collective-permute-start(bf16[8,1024]{1,0:T(8,128)(2,1)S(1)} %convert.30), channel_id=1, source_target_pairs={{0,120},{8,128},{16,136},{24,144},{32,152},{40,160},{48,168},{56,1... | collective-permute-start | bytes 49160
  672.4 8.3 %collective-permute-start = (bf16[8,1024]{1,0:T(8,128)(2,1)S(1)}, bf16[8,1024]{1,0:T(8,128)(2,1)}, u32[]{:S(2)}, u32[]{:S(2)}) collective-permute-start(bf16[8,1024]{1,0:T(8,128)(2,1)S(1)} %convert.30), channel_id=1, source_target_pairs={{0,8},{8,16},{16,24},{24,32},{32,40},{40,48},{48,56},{56,64},{64,7... | collective-permute-start | bytes 49160
  679.5 0.6 copy-start.2
  679.5 0.6 copy-start.3
  679.5 0.6 copy-start.4
  680.1 0.6 copy-start.5
Sparse Core Ops, SparseCore 0:
  119.5 31.5 reduce-scatter.3
where the time goes:
time: 701 us; the launch traced here: 698 us
  blocking collectives  558 us (80%)
  starting transfers between devices  65.2 us (9%)
  waiting for transfers between devices  30.2 us (4%)
  local copies, waits for them, and re-layouts  16.2 us (2%)
  between operations  14.9 us (2%)
  matrix products  9.98 us (1%)
    unnamed x1, blocking collectives  151 us
    pmax x1, blocking collectives, softmax_grad(): global_top = lax.pmax(local_top, 'vocab')  144 us
    psum x1, blocking collectives, softmax_grad(): exp_total, target_logit = lax.psum((exp_total, target_logit), 'vocab')  138 us
    all_gather x1, blocking collectives, per_device(): hidden_all = lax.all_gather(hidden, 'vocab', axis=0, tiled=True)  107 us
    unnamed x16, starting transfers between devices  65.2 us
    reduce_scatter x1, waiting for transfers between devices, per_device(): lax.psum_scatter(lax.dot_general(window_rows, head, (((1,), (1,)), ((), (...  30.2 us
    all_gather x1, blocking collectives, per_device(): grad_all = lax.all_gather(grad_local, 'rows', axis=0, tiled=True)  17.1 us
    unnamed x16, local copies, waits for them, and re-layouts  14.1 us
  transfers between devices with their start and end apart: 17, of which 1 were waited for; matrix products, arithmetic and copies ran while one was open for 1% of the time, Pallas kernels for 0%

commit v1 on v0

v1 whole, which is shorter than its diff:
```python
import jax
import jax.numpy as jnp
from jax import lax
from jax.sharding import Mesh, PartitionSpec as P

X, Z, Y, C = 4, 16, 4, 2
VOCAB_AXES = ("x", "z")
ROW_AXES = ("y", "core")
SWAP = [(0, 1), (1, 0)]


def gather_over(block, axis):
    size = lax.axis_size(axis)
    copies = jnp.broadcast_to(block[None], (size,) + block.shape)
    return lax.all_to_all(copies, axis, 0, 0)


def pick(pair, index):
    return lax.dynamic_index_in_dim(pair, index, 1, keepdims=False)


def per_device(hidden, head, targets, upstream):
    width, slice_width = head.shape
    token_count = targets.shape[0]
    own = token_count // (Y * C)
    core = lax.axis_index("core")
    row_first = lax.axis_index(ROW_AXES) * own

    by_z = gather_over(hidden, "z").reshape(-1, slice_width)
    hidden_all = gather_over(by_z, "x").reshape(Y, C, own, slice_width)
    hidden_own = pick(hidden_all, core).reshape(-1, slice_width)
    hidden_other = pick(hidden_all, 1 - core).reshape(-1, slice_width)

    def logits_of(rows):
        return lax.dot_general(rows, head, (((1,), (1,)), ((), ())), preferred_element_type=jnp.float32)

    from_core = lax.ppermute(logits_of(hidden_other), "core", SWAP)
    chip_logits = (logits_of(hidden_own) + from_core).reshape(Y, own, width)
    logits = jnp.sum(lax.all_to_all(chip_logits, "y", 0, 0), axis=0)

    row_targets = lax.dynamic_slice_in_dim(targets, row_first, own, 0)
    row_weight = lax.dynamic_slice_in_dim(upstream, row_first, own, 0)
    columns = lax.broadcasted_iota(jnp.int32, logits.shape, 1) + lax.axis_index(VOCAB_AXES) * width
    target_mask = columns == row_targets[:, None]
    local_top = jnp.max(logits, axis=1)
    local_total = jnp.sum(jnp.exp(logits - local_top[:, None]), axis=1)
    local_target = jnp.sum(jnp.where(target_mask, logits, jnp.float32(0.0)), axis=1)
    stats = jnp.concatenate([local_top, local_total, local_target])
    stats = gather_over(stats[None], VOCAB_AXES).reshape(X * Z, 3, own)
    top = jnp.max(stats[:, 0], axis=0)
    total = jnp.sum(stats[:, 1] * jnp.exp(stats[:, 0] - top), axis=0)
    lse = top + jnp.log(total)
    token_loss = lse - jnp.sum(stats[:, 2], axis=0)
    probability = jnp.exp(logits - lse[:, None])
    grad_rows = ((probability - target_mask.astype(jnp.float32)) * row_weight[:, None]).astype(jnp.bfloat16)

    grad_own = gather_over(grad_rows, "y").reshape(Y * own, width)
    grad_other = lax.ppermute(grad_own, "core", SWAP)

    def partial_of(grad):
        return jnp.dot(grad, head, preferred_element_type=jnp.float32).astype(jnp.bfloat16).reshape(
            X, own, slice_width
        )

    partial = jnp.stack([partial_of(grad_own), partial_of(grad_other)], axis=1)
    over_x = jnp.sum(lax.all_to_all(partial, "x", 0, 0).astype(jnp.float32), axis=0).astype(jnp.bfloat16)
    over_x = jnp.where(core == 0, over_x, over_x[::-1]).reshape(Z, -1, slice_width)
    over_z = lax.all_to_all(over_x, "z", 0, 0)
    grad_hidden = jnp.sum(over_z.astype(jnp.float32), axis=0).astype(jnp.bfloat16)

    def head_part(grad, rows):
        return lax.dot_general(grad, rows, (((0,), (0,)), ((), ())), preferred_element_type=jnp.float32)

    grad_head = (head_part(grad_own, hidden_own) + head_part(grad_other, hidden_other)).astype(jnp.bfloat16)
    return token_loss, grad_hidden, grad_head


def solution(mesh):
    torus = Mesh(mesh.devices.reshape(X, Z, Y, C), VOCAB_AXES + ROW_AXES)
    return jax.shard_map(
        per_device,
        mesh=torus,
        in_specs=(P(VOCAB_AXES, ROW_AXES), P(VOCAB_AXES, ROW_AXES), P(), P()),
        out_specs=(P(ROW_AXES), P(VOCAB_AXES, ROW_AXES), P(VOCAB_AXES, ROW_AXES)),
        check_vma=False,
    )
```

time: 701 us -> 169 us (0.24)
  the two profiles are of different devices: /device:TPU:16 before, /device:TPU:32 now
where the time goes in v1:
time: 169 us; the launch traced here: 168 us
  waiting for transfers between devices  69.9 us (41%)
  blocking collectives  43.2 us (26%)
  starting transfers between devices  30.2 us (18%)
  other arithmetic  9.55 us (6%)
  matrix products  7.35 us (4%)
  local copies, waits for them, and re-layouts  7.13 us (4%)
    all_to_all x2, blocking collectives, gather_over(): return lax.all_to_all(copies, axis, 0, 0)  43.2 us
    all_to_all x2, waiting for transfers between devices, gather_over(): return lax.all_to_all(copies, axis, 0, 0)  24.5 us
    all_to_all x1, waiting for transfers between devices, per_device(): over_z = lax.all_to_all(over_x, 'z', 0, 0)  14.9 us
    all_to_all x1, waiting for transfers between devices, per_device(): logits = jnp.sum(lax.all_to_all(chip_logits, 'y', 0, 0), axis=0)  13.9 us
    all_to_all x1, waiting for transfers between devices, per_device(): lax.all_to_all(partial, 'x', 0, 0).astype(jnp.float32)  12.9 us
    all_to_all x2, starting transfers between devices, gather_over(): return lax.all_to_all(copies, axis, 0, 0)  12.5 us
    all_to_all x1, starting transfers between devices, per_device(): over_z = lax.all_to_all(over_x, 'z', 0, 0)  5.25 us
    all_to_all x1, starting transfers between devices, per_device(): logits = jnp.sum(lax.all_to_all(chip_logits, 'y', 0, 0), axis=0)  4.47 us
  transfers between devices with their start and end apart: 7, of which 7 were waited for; matrix products, arithmetic and copies ran while one was open for 3% of the time, Pallas kernels for 0%

profile of v1, /device:TPU:32, one launch (start us, length us, event | category | flops | bytes accessed | tf_op | source)
XLA Modules:
  0.0 168.1 jit_solution(13803428532747947881)
XLA Ops:
  0.6 0.0 copy-start
  0.6 0.9 broadcast_in_dim.14
  1.5 32.9 %all_to_all.35 = bf16[16,6,1024]{2,1,0:T(8,128)(2,1)S(1)} all-to-all(bf16[16,6,1024]{2,1,0:T(8,128)(2,1)S(1)} %broadcast_in_dim.14), channel_id=1, replica_groups=mesh['x'=4,'z'=16,'y'=4,'core'=2] {'z'}, dimensions={0} | all-to-all | bytes 393216 | tf_op jit(solution)/shard_map/all_to_all | solution.py:15
  34.5 0.1 broadcast_in_dim.15
  34.5 1.0 broadcast_in_dim.16
  35.5 4.3 %all-to-all-start.1 = ((bf16[4,96,1024]{2,1,0:T(8,128)(2,1)}), bf16[4,96,1024]{2,1,0:T(8,128)(2,1)S(1)}, u32[]{:S(2)}, u32[]{:S(2)}) async-start(bf16[4,96,1024]{2,1,0:T(8,128)(2,1)} %broadcast_in_dim.16), calls=%async_computation.1 | async-start | bytes 1572864 | tf_op jit(solution)/shard_map/all_to_all | solution.py:15
  39.8 11.5 %all-to-all-done.1 = bf16[4,96,1024]{2,1,0:T(8,128)(2,1)S(1)} async-done(((bf16[4,96,1024]{2,1,0:T(8,128)(2,1)}), bf16[4,96,1024]{2,1,0:T(8,128)(2,1)S(1)}, u32[]{:S(2)}, u32[]{:S(2)}) %all-to-all-start.1) | async-done | bytes 786464 | tf_op jit(solution)/shard_map/all_to_all | solution.py:15
  51.2 0.1 constant_dynamic-slice_fusion.1
  51.3 0.7 copy-done.1
  52.1 0.9 fusion.8
  53.0 1.9 %collective-permute-start = (f32[192,1188]{1,0:T(8,128)S(1)}, f32[192,1188]{1,0:T(8,128)S(1)}, u32[]{:S(2)}, u32[]{:S(2)}) collective-permute-start(f32[192,1188]{1,0:T(8,128)S(1)} %fusion.8), channel_id=1, source_target_pairs={{0,1},{1,0},{2,3},{3,2},{4,5},{5,4},{6,7},{7,6},{8,9},{9,8},{10,11... | collective-permute-start | bytes 2737160 | tf_op jit(solution)/shard_map/ppermute | solution.py:37
  54.9 2.5 %collective-permute-done = f32[192,1188]{1,0:T(8,128)S(1)} collective-permute-done((f32[192,1188]{1,0:T(8,128)S(1)}, f32[192,1188]{1,0:T(8,128)S(1)}, u32[]{:S(2)}, u32[]{:S(2)}) %collective-permute-start) | collective-permute-done | bytes 912416 | tf_op jit(solution)/shard_map/ppermute | solution.py:37
  57.5 1.9 %convolution_add_fusion = f32[192,1188]{1,0:T(8,128)} fusion(f32[192,1188]{1,0:T(8,128)S(1)} %collective-permute-done, bf16[192,1024]{1,0:T(8,128)(2,1)S(1)} %bitcast.38, bf16[1188,1024]{1,0:T(8,128)(2,1)S(1)} %copy-done), kind=kOutput, calls=%fused_computation.1 | convolution fusion | flops 467368704 | bytes 4651008 | tf_op jit(solution)/shard_map/dot_general | solution.py:35
  59.4 4.5 %all-to-all-start.2 = ((f32[4,48,1188]{2,1,0:T(8,128)}), f32[4,48,1188]{2,1,0:T(8,128)S(1)}, u32[]{:S(2)}, u32[]{:S(2)}) async-start(f32[4,48,1188]{2,1,0:T(8,128)} %bitcast.3), calls=%async_computation.2 | async-start | bytes 1966080 | tf_op jit(solution)/shard_map/all_to_all | solution.py:39
  63.9 0.8 dynamic_slice.15
  64.6 13.9 %all-to-all-done.2 = f32[4,48,1188]{2,1,0:T(8,128)S(1)} async-done(((f32[4,48,1188]{2,1,0:T(8,128)}), f32[4,48,1188]{2,1,0:T(8,128)S(1)}, u32[]{:S(2)}, u32[]{:S(2)}) %all-to-all-start.2) | async-done | bytes 912416 | tf_op jit(solution)/shard_map/all_to_all | solution.py:39
  78.5 0.8 reduce_sum.69
  79.3 1.1 reduce_max.18
  80.4 1.2 exponential_reduce_fusion
  81.6 0.1 pad_maximum_fusion.1
  81.6 0.7 broadcast_in_dim.18
  82.3 8.2 %all-to-all-start.3 = ((f32[64,1,144]{2,1,0:T(1,128)}), f32[64,1,144]{2,1,0:T(1,128)S(1)}, u32[]{:S(2)}, u32[]{:S(2)}) async-start(f32[64,1,144]{2,1,0:T(1,128)} %broadcast_in_dim.18), calls=%async_computation.3 | async-start | bytes 131072 | tf_op jit(solution)/shard_map/all_to_all | solution.py:15
  90.5 0.8 dynamic_slice.16
  91.2 13.1 %all-to-all-done.3 = f32[64,1,144]{2,1,0:T(1,128)S(1)} async-done(((f32[64,1,144]{2,1,0:T(1,128)}), f32[64,1,144]{2,1,0:T(1,128)S(1)}, u32[]{:S(2)}, u32[]{:S(2)}) %all-to-all-start.3) | async-done | bytes 36896 | tf_op jit(solution)/shard_map/all_to_all | solution.py:15
  104.3 0.1 copy.11
  104.4 0.1 slice_reduce_fusion
  104.5 0.2 fusion.5
  104.7 0.5 fusion.7
  105.2 1.1 fusion.3
  106.3 10.3 %all_to_all.36 = bf16[4,48,1188]{2,1,0:T(8,128)(2,1)S(1)} all-to-all(bf16[4,48,1188]{2,1,0:T(8,128)(2,1)S(1)} %broadcast_in_dim.19), channel_id=1, replica_groups=mesh['x'=4,'z'=16,'y'=4,'core'=2] {'y'}, dimensions={0} | all-to-all | bytes 912384 | tf_op jit(solution)/shard_map/all_to_all | solution.py:15
  116.6 1.9 %collective-permute-start.1 = (bf16[192,1188]{1,0:T(8,128)(2,1)S(1)}, bf16[192,1188]{1,0:T(8,128)(2,1)S(1)}, u32[]{:S(2)}, u32[]{:S(2)}) collective-permute-start(bf16[192,1188]{1,0:T(8,128)(2,1)S(1)} %bitcast.40), channel_id=1, source_target_pairs={{0,1},{1,0},{2,3},{3,2},{4,5},{5,4},{6,7},{7,6},{8,9},{9,8},{10,11... | collective-permute-start | bytes 1368584 | tf_op jit(solution)/shard_map/ppermute | solution.py:58
  118.6 0.7 convolution_convert_fusion.1
  119.3 1.1 collective-permute-done.1
  120.4 0.7 convolution_convert_fusion
  121.1 0.1 copy-done.5
  121.2 1.0 pad_maximum_fusion
  122.1 4.2 %all-to-all-start.5 = ((bf16[4,2,48,1024]{3,2,1,0:T(8,128)(2,1)}), bf16[4,2,48,1024]{3,2,1,0:T(8,128)(2,1)}, u32[]{:S(2)}, u32[]{:S(2)}) async-start(bf16[4,2,48,1024]{3,2,1,0:T(8,128)(2,1)} %pad_maximum_fusion), calls=%async_computation.5 | async-start | bytes 1572864 | tf_op jit(solution)/shard_map/all_to_all | solution.py:66
  126.3 12.9 %all-to-all-done.5 = bf16[4,2,48,1024]{3,2,1,0:T(8,128)(2,1)} async-done(((bf16[4,2,48,1024]{3,2,1,0:T(8,128)(2,1)}), bf16[4,2,48,1024]{3,2,1,0:T(8,128)(2,1)}, u32[]{:S(2)}, u32[]{:S(2)}) %all-to-all-start.5) | async-done | bytes 786464 | tf_op jit(solution)/shard_map/all_to_all | solution.py:66
  139.2 1.3 reduce_sum.74
  140.5 0.7 reverse_select_fusion
  141.2 1.7 %reshape.103 = bf16[16,6,1024]{2,1,0:T(8,128)(2,1)} reshape(bf16[2,48,1024]{2,1,0:T(8,128)(2,1)} %reverse_select_fusion) | data formatting | bytes 393216 | tf_op jit(solution)/shard_map/reshape | solution.py:67
  142.9 5.2 %all-to-all-start.6 = ((bf16[16,6,1024]{2,1,0:T(8,128)(2,1)}), bf16[16,6,1024]{2,1,0:T(8,128)(2,1)}, u32[]{:S(2)}, u32[]{:S(2)}) async-start(bf16[16,6,1024]{2,1,0:T(8,128)(2,1)} %reshape.103), calls=%async_computation.6 | async-start | bytes 524288 | tf_op jit(solution)/shard_map/all_to_all | solution.py:68
  148.2 0.8 fusion.9
  149.0 0.1 copy-done.2
  149.2 0.2 copy-done.6
  149.3 2.3 %add_convert_fusion = bf16[1188,1024]{1,0:T(8,128)(2,1)} fusion(f32[1188,1024]{1,0:T(8,128)S(1)} %fusion.9, bf16[192,1188]{1,0:T(8,128)(2,1)S(1)} %copy-done.6, bf16[192,1024]{1,0:T(8,128)(2,1)S(1)} %bitcast.37), kind=kOutput, calls=%fused_computation | convolution fusion | flops 469573632 | bytes 8148480 | tf_op jit(solution)/shard_map/dot_general | solution.py:72
  151.6 14.9 %all-to-all-done.6 = bf16[16,6,1024]{2,1,0:T(8,128)(2,1)} async-done(((bf16[16,6,1024]{2,1,0:T(8,128)(2,1)}), bf16[16,6,1024]{2,1,0:T(8,128)(2,1)}, u32[]{:S(2)}, u32[]{:S(2)}) %all-to-all-start.6) | async-done | bytes 196640 | tf_op jit(solution)/shard_map/all_to_all | solution.py:68
  166.5 1.6 reduce_sum.75
  (11 shorter events, 0.1 us)
Async XLA Ops:
  0.6 51.4 %copy-start = (bf16[1188,1024]{1,0:T(8,128)(2,1)S(1)}, bf16[1188,1024]{1,0:T(8,128)(2,1)}, u32[]{:S(2)}) copy-start(bf16[1188,1024]{1,0:T(8,128)(2,1)} %param.5) | copy-start | bytes 7299076
  35.5 15.7 %all-to-all-start.1 = ((bf16[4,96,1024]{2,1,0:T(8,128)(2,1)}), bf16[4,96,1024]{2,1,0:T(8,128)(2,1)S(1)}, u32[]{:S(2)}, u32[]{:S(2)}) async-start(bf16[4,96,1024]{2,1,0:T(8,128)(2,1)} %broadcast_in_dim.16), calls=%async_computation.1 | async-start | bytes 1572864 | tf_op jit(solution)/shard_map/all_to_all | solution.py:15
  51.3 0.8 copy-start.1
  51.3 8.1 %copy-start.3 = (bf16[4,1,48,1024]{3,2,1,0:T(8,128)(2,1)}, bf16[4,1,48,1024]{3,2,1,0:T(8,128)(2,1)S(1)}, u32[]{:S(2)}) copy-start(bf16[4,1,48,1024]{3,2,1,0:T(8,128)(2,1)S(1)} %get-tuple-element.9) | copy-start | bytes 1179652
  53.0 4.5 %collective-permute-start = (f32[192,1188]{1,0:T(8,128)S(1)}, f32[192,1188]{1,0:T(8,128)S(1)}, u32[]{:S(2)}, u32[]{:S(2)}) collective-permute-start(f32[192,1188]{1,0:T(8,128)S(1)} %fusion.8), channel_id=1, source_target_pairs={{0,1},{1,0},{2,3},{3,2},{4,5},{5,4},{6,7},{7,6},{8,9},{9,8},{10,11... | collective-permute-start | bytes 2737160 | tf_op jit(solution)/shard_map/ppermute | solution.py:37
  59.4 19.2 %all-to-all-start.2 = ((f32[4,48,1188]{2,1,0:T(8,128)}), f32[4,48,1188]{2,1,0:T(8,128)S(1)}, u32[]{:S(2)}, u32[]{:S(2)}) async-start(f32[4,48,1188]{2,1,0:T(8,128)} %bitcast.3), calls=%async_computation.2 | async-start | bytes 1966080 | tf_op jit(solution)/shard_map/all_to_all | solution.py:39
  82.3 22.0 %all-to-all-start.3 = ((f32[64,1,144]{2,1,0:T(1,128)}), f32[64,1,144]{2,1,0:T(1,128)S(1)}, u32[]{:S(2)}, u32[]{:S(2)}) async-start(f32[64,1,144]{2,1,0:T(1,128)} %broadcast_in_dim.18), calls=%async_computation.3 | async-start | bytes 131072 | tf_op jit(solution)/shard_map/all_to_all | solution.py:15
  116.6 3.7 %collective-permute-start.1 = (bf16[192,1188]{1,0:T(8,128)(2,1)S(1)}, bf16[192,1188]{1,0:T(8,128)(2,1)S(1)}, u32[]{:S(2)}, u32[]{:S(2)}) collective-permute-start(bf16[192,1188]{1,0:T(8,128)(2,1)S(1)} %bitcast.40), channel_id=1, source_target_pairs={{0,1},{1,0},{2,3},{3,2},{4,5},{5,4},{6,7},{7,6},{8,9},{9,8},{10,11... | collective-permute-start | bytes 1368584 | tf_op jit(solution)/shard_map/ppermute | solution.py:58
  120.4 0.8 copy-start.5
  121.2 27.0 %copy-start.4 = (bf16[4,1,48,1024]{3,2,1,0:T(8,128)(2,1)S(1)}, bf16[4,1,48,1024]{3,2,1,0:T(8,128)(2,1)}, u32[]{:S(2)}) copy-start(bf16[4,1,48,1024]{3,2,1,0:T(8,128)(2,1)} %copy-done.3) | copy-start | bytes 1179652
  122.1 17.1 %all-to-all-start.5 = ((bf16[4,2,48,1024]{3,2,1,0:T(8,128)(2,1)}), bf16[4,2,48,1024]{3,2,1,0:T(8,128)(2,1)}, u32[]{:S(2)}, u32[]{:S(2)}) async-start(bf16[4,2,48,1024]{3,2,1,0:T(8,128)(2,1)} %pad_maximum_fusion), calls=%async_computation.5 | async-start | bytes 1572864 | tf_op jit(solution)/shard_map/all_to_all | solution.py:66
  142.9 23.6 %all-to-all-start.6 = ((bf16[16,6,1024]{2,1,0:T(8,128)(2,1)}), bf16[16,6,1024]{2,1,0:T(8,128)(2,1)}, u32[]{:S(2)}, u32[]{:S(2)}) async-start(bf16[16,6,1024]{2,1,0:T(8,128)(2,1)} %reshape.103), calls=%async_computation.6 | async-start | bytes 524288 | tf_op jit(solution)/shard_map/all_to_all | solution.py:68
  148.2 1.0 copy-start.2
  148.2 1.1 copy-start.6

commit v2 on v1

--- a/solution.py
+++ b/solution.py
@@ -26,16 +26,20 @@
     core = lax.axis_index("core")
     row_first = lax.axis_index(ROW_AXES) * own
 
-    by_z = gather_over(hidden, "z").reshape(-1, slice_width)
-    hidden_all = gather_over(by_z, "x").reshape(Y, C, own, slice_width)
-    hidden_own = pick(hidden_all, core).reshape(-1, slice_width)
-    hidden_other = pick(hidden_all, 1 - core).reshape(-1, slice_width)
+    head_other = lax.ppermute(head, "core", SWAP)
 
-    def logits_of(rows):
-        return lax.dot_general(rows, head, (((1,), (1,)), ((), ())), preferred_element_type=jnp.float32)
+    by_z = gather_over(hidden, "z").reshape(1, C, own, slice_width)
+    copies = jnp.broadcast_to(by_z, (X, C, own, slice_width)).reshape(X * C, own, slice_width)
+    both = lax.all_to_all(copies, ("x", "core"), 0, 0).reshape(X, C, own, slice_width)
+    hidden_own = pick(both, core).reshape(-1, slice_width)
+    hidden_other = pick(both, 1 - core).reshape(-1, slice_width)
 
-    from_core = lax.ppermute(logits_of(hidden_other), "core", SWAP)
-    chip_logits = (logits_of(hidden_own) + from_core).reshape(Y, own, width)
+    def logits_of(rows, slice_of_head):
+        return lax.dot_general(
+            rows, slice_of_head, (((1,), (1,)), ((), ())), preferred_element_type=jnp.float32
+        )
+
+    chip_logits = (logits_of(hidden_own, head) + logits_of(hidden_other, head_other)).reshape(Y, own, width)
     logits = jnp.sum(lax.all_to_all(chip_logits, "y", 0, 0), axis=0)
 
     row_targets = lax.dynamic_slice_in_dim(targets, row_first, own, 0)
@@ -54,24 +58,29 @@
     probability = jnp.exp(logits - lse[:, None])
     grad_rows = ((probability - target_mask.astype(jnp.float32)) * row_weight[:, None]).astype(jnp.bfloat16)
 
-    grad_own = gather_over(grad_rows, "y").reshape(Y * own, width)
-    grad_other = lax.ppermute(grad_own, "core", SWAP)
+    grad_half = gather_over(grad_rows, "y").reshape(Y * own, width)
 
-    def partial_of(grad):
-        return jnp.dot(grad, head, preferred_element_type=jnp.float32).astype(jnp.bfloat16).reshape(
+    def partial_of(slice_of_head):
+        return jnp.dot(grad_half, slice_of_head, preferred_element_type=jnp.float32).astype(jnp.bfloat16).reshape(
             X, own, slice_width
         )
 
-    partial = jnp.stack([partial_of(grad_own), partial_of(grad_other)], axis=1)
-    over_x = jnp.sum(lax.all_to_all(partial, "x", 0, 0).astype(jnp.float32), axis=0).astype(jnp.bfloat16)
-    over_x = jnp.where(core == 0, over_x, over_x[::-1]).reshape(Z, -1, slice_width)
+    part_own, part_other = partial_of(head), partial_of(head_other)
+    partial = jnp.stack(
+        [jnp.where(core == 0, part_own, part_other), jnp.where(core == 0, part_other, part_own)], axis=1
+    ).reshape(X * C, own, slice_width)
+    over_x = lax.all_to_all(partial, ("x", "core"), 0, 0).reshape(X, C * own, slice_width)
+    over_x = jnp.sum(over_x.astype(jnp.float32), axis=0).astype(jnp.bfloat16).reshape(Z, -1, slice_width)
     over_z = lax.all_to_all(over_x, "z", 0, 0)
     grad_hidden = jnp.sum(over_z.astype(jnp.float32), axis=0).astype(jnp.bfloat16)
+
+    grad_rest = lax.ppermute(grad_half, "core", SWAP)
+    hidden_rest = lax.ppermute(hidden_other, "core", SWAP)
 
     def head_part(grad, rows):
         return lax.dot_general(grad, rows, (((0,), (0,)), ((), ())), preferred_element_type=jnp.float32)
 
-    grad_head = (head_part(grad_own, hidden_own) + head_part(grad_other, hidden_other)).astype(jnp.bfloat16)
+    grad_head = (head_part(grad_half, hidden_own) + head_part(grad_rest, hidden_rest)).astype(jnp.bfloat16)
     return token_loss, grad_hidden, grad_head
 
 

time: 169 us -> 164 us (0.970)
  blocking collectives: 43.2 us -> 33.8 us
  matrix products: 7.35 us -> 14.1 us
  other arithmetic: 9.55 us -> 3.21 us
  starting transfers between devices: 30.2 us -> 34 us
  waiting for transfers between devices: 69.9 us -> 72 us
    all_to_all x2 -> x1, blocking collectives: 43.2 us -> 33.8 us  [gather_over(): return lax.all_to_all(copies, axis, 0, 0)]
    all_to_all x1 -> x2, waiting for transfers between devices: 12.9 us -> 21.9 us  [the longest x1 13.2 us: per_device(): lax.all_to_all(copies, ('x', 'core'), 0, 0).reshape(X, C, own, slice_width)]
    dot_general x4, matrix products: 4.24 us -> 11 us  [the longest x2 6.21 us: logits_of(): lax.dot_general(rows, slice_of_head, (((1,), (1,)), ((), ())), preferred_...]
    all_to_all x1 -> x2, starting transfers between devices: 4.19 us -> 7.85 us  [the longest x1 4.3 us: per_device(): lax.all_to_all(copies, ('x', 'core'), 0, 0).reshape(X, C, own, slice_width)]
    ppermute x2 -> x3, waiting for transfers between devices: 3.65 us -> 0.01 us  [the longest x1 0.01 us: per_device(): head_other = lax.ppermute(head, 'core', SWAP)]
    all_to_all x2, waiting for transfers between devices: 24.5 us -> 20.9 us  [gather_over(): return lax.all_to_all(copies, axis, 0, 0)]
    ppermute x2 -> x3, starting transfers between devices: 3.83 us -> 6.25 us  [the longest x1 2.3 us: per_device(): hidden_rest = lax.ppermute(hidden_other, 'core', SWAP)]
    all_to_all x2, starting transfers between devices: 12.5 us -> 10.7 us  [gather_over(): return lax.all_to_all(copies, axis, 0, 0)]
  transfers between devices with their start and end apart: 7 -> 9, of which waited for: 7 -> 6; matrix products, arithmetic and copies ran while one was open for 3% -> 6% of each run, Pallas kernels for 0% -> 0%
where the time goes in v2:
time: 164 us; the launch traced here: 163 us
  waiting for transfers between devices  72 us (44%)
  starting transfers between devices  34 us (21%)
  blocking collectives  33.8 us (21%)
  matrix products  14.1 us (9%)
  local copies, waits for them, and re-layouts  5.7 us (3%)
  other arithmetic  3.21 us (2%)
    all_to_all x1, blocking collectives, gather_over(): return lax.all_to_all(copies, axis, 0, 0)  33.8 us
    all_to_all x2, waiting for transfers between devices, gather_over(): return lax.all_to_all(copies, axis, 0, 0)  20.9 us
    all_to_all x1, waiting for transfers between devices, per_device(): over_z = lax.all_to_all(over_x, 'z', 0, 0)  15.7 us
    all_to_all x1, waiting for transfers between devices, per_device(): logits = jnp.sum(lax.all_to_all(chip_logits, 'y', 0, 0), axis=0)  13.4 us
    all_to_all x1, waiting for transfers between devices, per_device(): lax.all_to_all(copies, ('x', 'core'), 0, 0).reshape(X, C, own, slice_width)  13.2 us
    all_to_all x2, starting transfers between devices, gather_over(): return lax.all_to_all(copies, axis, 0, 0)  10.7 us
    all_to_all x1, waiting for transfers between devices, per_device(): lax.all_to_all(partial, ('x', 'core'), 0, 0)  8.73 us
    dot_general x2, matrix products, logits_of(): lax.dot_general(rows, slice_of_head, (((1,), (1,)), ((), ())), preferred_...  6.21 us
  transfers between devices with their start and end apart: 9, of which 6 were waited for; matrix products, arithmetic and copies ran while one was open for 6% of the time, Pallas kernels for 0%

profile of v2, /device:TPU:32, one launch (start us, length us, event | category | flops | bytes accessed | tf_op | source)
XLA Modules:
  0.0 163.5 jit_solution(16552046485537400629)
XLA Ops:
  0.6 1.9 %collective-permute-start = (bf16[1188,1024]{1,0:T(8,128)(2,1)}, bf16[1188,1024]{1,0:T(8,128)(2,1)}, u32[]{:S(2)}, u32[]{:S(2)}) collective-permute-start(bf16[1188,1024]{1,0:T(8,128)(2,1)} %param.5), channel_id=1, source_target_pairs={{0,1},{1,0},{2,3},{3,2},{4,5},{5,4},{6,7},{7,6},{8,9},{9,8},{10,11... | collective-permute-start | bytes 7299080 | tf_op jit(solution)/shard_map/ppermute | solution.py:29
  2.6 0.7 broadcast_in_dim.14
  3.3 33.8 %all_to_all.35 = bf16[16,6,1024]{2,1,0:T(8,128)(2,1)S(1)} all-to-all(bf16[16,6,1024]{2,1,0:T(8,128)(2,1)S(1)} %broadcast_in_dim.14), channel_id=1, replica_groups=mesh['x'=4,'z'=16,'y'=4,'core'=2] {'z'}, dimensions={0} | all-to-all | bytes 393216 | tf_op jit(solution)/shard_map/all_to_all | solution.py:15
  37.1 0.1 broadcast_in_dim.15
  37.1 1.0 broadcast_in_dim.16
  38.1 4.3 %all-to-all-start.1 = ((bf16[8,48,1024]{2,1,0:T(8,128)(2,1)}), bf16[8,48,1024]{2,1,0:T(8,128)(2,1)S(1)}, u32[]{:S(2)}, u32[]{:S(2)}) async-start(bf16[8,48,1024]{2,1,0:T(8,128)(2,1)} %bitcast), calls=%async_computation.1 | async-start | bytes 1572864 | tf_op jit(solution)/shard_map/all_to_all | solution.py:33
  42.4 13.2 %all-to-all-done.1 = bf16[8,48,1024]{2,1,0:T(8,128)(2,1)S(1)} async-done(((bf16[8,48,1024]{2,1,0:T(8,128)(2,1)}), bf16[8,48,1024]{2,1,0:T(8,128)(2,1)S(1)}, u32[]{:S(2)}, u32[]{:S(2)}) %all-to-all-start.1) | async-done | bytes 786464 | tf_op jit(solution)/shard_map/all_to_all | solution.py:33
  55.6 0.1 constant_dynamic-slice_fusion
  55.6 2.6 %fusion.8 = f32[192,1188]{1,0:T(8,128)S(1)} fusion(bf16[192,1024]{1,0:T(8,128)(2,1)S(1)} %bitcast.41, bf16[1188,1024]{1,0:T(8,128)(2,1)} %param.5), kind=kOutput, calls=%fused_computation.28 | convolution fusion | flops 467140608 | bytes 3738624 | tf_op jit(solution)/shard_map/dot_general | solution.py:38
  58.3 0.0 collective-permute-done
  58.3 3.6 %convolution_add_fusion = f32[192,1188]{1,0:T(8,128)} fusion(f32[192,1188]{1,0:T(8,128)S(1)} %fusion.8, bf16[192,1024]{1,0:T(8,128)(2,1)S(1)} %bitcast.49, bf16[1188,1024]{1,0:T(8,128)(2,1)} %collective-permute-done), kind=kOutput, calls=%fused_computation.1 | convolution fusion | flops 467368704 | bytes 4651008 | tf_op jit(solution)/shard_map/dot_general | solution.py:38
  61.9 4.5 %all-to-all-start.2 = ((f32[4,48,1188]{2,1,0:T(8,128)}), f32[4,48,1188]{2,1,0:T(8,128)S(1)}, u32[]{:S(2)}, u32[]{:S(2)}) async-start(f32[4,48,1188]{2,1,0:T(8,128)} %bitcast.4), calls=%async_computation.2 | async-start | bytes 1966080 | tf_op jit(solution)/shard_map/all_to_all | solution.py:43
  66.3 0.8 dynamic_slice.15
  67.1 13.4 %all-to-all-done.2 = f32[4,48,1188]{2,1,0:T(8,128)S(1)} async-done(((f32[4,48,1188]{2,1,0:T(8,128)}), f32[4,48,1188]{2,1,0:T(8,128)S(1)}, u32[]{:S(2)}, u32[]{:S(2)}) %all-to-all-start.2) | async-done | bytes 912416 | tf_op jit(solution)/shard_map/all_to_all | solution.py:43
  80.5 0.1 reduce_sum.69
  80.6 0.1 reduce_max.18
  80.7 0.2 exponential_reduce_fusion
  81.0 0.1 pad_maximum_fusion.1
  81.0 0.7 broadcast_in_dim.18
  81.7 7.2 %all-to-all-start.3 = ((f32[64,1,144]{2,1,0:T(1,128)}), f32[64,1,144]{2,1,0:T(1,128)S(1)}, u32[]{:S(2)}, u32[]{:S(2)}) async-start(f32[64,1,144]{2,1,0:T(1,128)} %broadcast_in_dim.18), calls=%async_computation.3 | async-start | bytes 131072 | tf_op jit(solution)/shard_map/all_to_all | solution.py:15
  88.9 0.8 dynamic_slice.16
  89.7 13.1 %all-to-all-done.3 = f32[64,1,144]{2,1,0:T(1,128)S(1)} async-done(((f32[64,1,144]{2,1,0:T(1,128)}), f32[64,1,144]{2,1,0:T(1,128)S(1)}, u32[]{:S(2)}, u32[]{:S(2)}) %all-to-all-start.3) | async-done | bytes 36896 | tf_op jit(solution)/shard_map/all_to_all | solution.py:15
  102.8 0.1 copy.13
  102.9 0.1 slice_reduce_fusion
  103.0 0.2 fusion.5
  103.2 0.5 fusion.7
  103.7 0.1 fusion.3
  103.8 0.8 broadcast_in_dim.19
  104.7 3.5 %all-to-all-start.4 = ((bf16[4,48,1188]{2,1,0:T(8,128)(2,1)}), bf16[4,48,1188]{2,1,0:T(8,128)(2,1)S(1)}, u32[]{:S(2)}, u32[]{:S(2)}) async-start(bf16[4,48,1188]{2,1,0:T(8,128)(2,1)} %broadcast_in_dim.19), calls=%async_computation.4 | async-start | bytes 983040 | tf_op jit(solution)/shard_map/all_to_all | solution.py:15
  108.1 7.9 %all-to-all-done.4 = bf16[4,48,1188]{2,1,0:T(8,128)(2,1)S(1)} async-done(((bf16[4,48,1188]{2,1,0:T(8,128)(2,1)}), bf16[4,48,1188]{2,1,0:T(8,128)(2,1)S(1)}, u32[]{:S(2)}, u32[]{:S(2)}) %all-to-all-start.4) | async-done | bytes 456224 | tf_op jit(solution)/shard_map/all_to_all | solution.py:15
  116.0 2.4 %convolution_convert_fusion.1 = bf16[192,1024]{1,0:T(8,128)(2,1)S(1)} fusion(bf16[192,1188]{1,0:T(8,128)(2,1)S(1)} %bitcast.43, bf16[1188,1024]{1,0:T(8,128)(2,1)} %param.5), kind=kOutput, calls=%fused_computation.3 | convolution fusion | flops 467337216 | bytes 3282432 | tf_op jit(solution)/shard_map/dot_general | solution.py:64
  118.4 2.4 %broadcast_select_fusion.1 = (bf16[192,1024]{1,0:T(8,128)(2,1)S(1)}, bf16[192,1024]{1,0:T(8,128)(2,1)S(1)}) fusion(bf16[192,1024]{1,0:T(8,128)(2,1)S(1)} %convolution_convert_fusion.1, pred[]{:T(512)S(6)} %eq.18, bf16[192,1188]{1,0:T(8,128)(2,1)S(1)} %bitcast.44, bf16[1188,1024]{1,0:T(8,128)(2,1)} %collective-permute-done), kind=kOutput, calls=%fused_computation.7 | convolution fusion | flops 467730432 | bytes 4068865 | tf_op jit(solution)/shard_map/dot_general | solution.py:64
  120.8 1.0 pad_maximum_fusion
  121.7 3.5 %all-to-all-start.5 = ((bf16[8,48,1024]{2,1,0:T(8,128)(2,1)}), bf16[8,48,1024]{2,1,0:T(8,128)(2,1)S(1)}, u32[]{:S(2)}, u32[]{:S(2)}) async-start(bf16[8,48,1024]{2,1,0:T(8,128)(2,1)} %bitcast.13), calls=%async_computation.5 | async-start | bytes 1572864 | tf_op jit(solution)/shard_map/all_to_all | solution.py:72
  125.3 2.3 %collective-permute-start.2 = (bf16[192,1024]{1,0:T(8,128)(2,1)S(1)}, bf16[192,1024]{1,0:T(8,128)(2,1)S(1)}, u32[]{:S(2)}, u32[]{:S(2)}) collective-permute-start(bf16[192,1024]{1,0:T(8,128)(2,1)S(1)} %bitcast.50), channel_id=1, source_target_pairs={{0,1},{1,0},{2,3},{3,2},{4,5},{5,4},{6,7},{7,6},{8,9},{9,8},{10,11... | collective-permute-start | bytes 1179656 | tf_op jit(solution)/shard_map/ppermute | solution.py:78
  127.6 2.0 %collective-permute-start.1 = (bf16[192,1188]{1,0:T(8,128)(2,1)S(1)}, bf16[192,1188]{1,0:T(8,128)(2,1)S(1)}, u32[]{:S(2)}, u32[]{:S(2)}) collective-permute-start(bf16[192,1188]{1,0:T(8,128)(2,1)S(1)} %bitcast.45), channel_id=1, source_target_pairs={{0,1},{1,0},{2,3},{3,2},{4,5},{5,4},{6,7},{7,6},{8,9},{9,8},{10,11... | collective-permute-start | bytes 1368584 | tf_op jit(solution)/shard_map/ppermute | solution.py:77
  129.6 8.7 %all-to-all-done.5 = bf16[8,48,1024]{2,1,0:T(8,128)(2,1)S(1)} async-done(((bf16[8,48,1024]{2,1,0:T(8,128)(2,1)}), bf16[8,48,1024]{2,1,0:T(8,128)(2,1)S(1)}, u32[]{:S(2)}, u32[]{:S(2)}) %all-to-all-start.5) | async-done | bytes 786464 | tf_op jit(solution)/shard_map/all_to_all | solution.py:72
  138.4 0.1 bitcast_reduce_fusion
  138.5 0.8 reshape.156
  139.3 4.7 %all-to-all-start.6 = ((bf16[16,6,1024]{2,1,0:T(8,128)(2,1)}), bf16[16,6,1024]{2,1,0:T(8,128)(2,1)S(1)}, u32[]{:S(2)}, u32[]{:S(2)}) async-start(bf16[16,6,1024]{2,1,0:T(8,128)(2,1)} %reshape.156), calls=%async_computation.6 | async-start | bytes 524288 | tf_op jit(solution)/shard_map/all_to_all | solution.py:74
  144.0 0.8 fusion.9
  144.8 0.0 collective-permute-done.2
  144.8 0.0 collective-permute-done.1
  144.8 2.3 %add_convert_fusion = bf16[1188,1024]{1,0:T(8,128)(2,1)} fusion(f32[1188,1024]{1,0:T(8,128)S(1)} %fusion.9, bf16[192,1188]{1,0:T(8,128)(2,1)S(1)} %collective-permute-done.1, bf16[192,1024]{1,0:T(8,128)(2,1)S(1)} %collective-permute-done.2), kind=kOutput, calls=%fused_computation | convolution fusion | flops 469573632 | bytes 8148480 | tf_op jit(solution)/shard_map/dot_general | solution.py:81
  147.1 15.7 %all-to-all-done.6 = bf16[16,6,1024]{2,1,0:T(8,128)(2,1)S(1)} async-done(((bf16[16,6,1024]{2,1,0:T(8,128)(2,1)}), bf16[16,6,1024]{2,1,0:T(8,128)(2,1)S(1)}, u32[]{:S(2)}, u32[]{:S(2)}) %all-to-all-start.6) | async-done | bytes 196640 | tf_op jit(solution)/shard_map/all_to_all | solution.py:74
  162.8 0.7 reduce_sum.75
  (1 shorter events, 0.0 us)
Async XLA Ops:
  0.6 57.6 %collective-permute-start = (bf16[1188,1024]{1,0:T(8,128)(2,1)}, bf16[1188,1024]{1,0:T(8,128)(2,1)}, u32[]{:S(2)}, u32[]{:S(2)}) collective-permute-start(bf16[1188,1024]{1,0:T(8,128)(2,1)} %param.5), channel_id=1, source_target_pairs={{0,1},{1,0},{2,3},{3,2},{4,5},{5,4},{6,7},{7,6},{8,9},{9,8},{10,11... | collective-permute-start | bytes 7299080 | tf_op jit(solution)/shard_map/ppermute | solution.py:29
  38.1 17.5 %all-to-all-start.1 = ((bf16[8,48,1024]{2,1,0:T(8,128)(2,1)}), bf16[8,48,1024]{2,1,0:T(8,128)(2,1)S(1)}, u32[]{:S(2)}, u32[]{:S(2)}) async-start(bf16[8,48,1024]{2,1,0:T(8,128)(2,1)} %bitcast), calls=%async_computation.1 | async-start | bytes 1572864 | tf_op jit(solution)/shard_map/all_to_all | solution.py:33
  61.9 18.7 %all-to-all-start.2 = ((f32[4,48,1188]{2,1,0:T(8,128)}), f32[4,48,1188]{2,1,0:T(8,128)S(1)}, u32[]{:S(2)}, u32[]{:S(2)}) async-start(f32[4,48,1188]{2,1,0:T(8,128)} %bitcast.4), calls=%async_computation.2 | async-start | bytes 1966080 | tf_op jit(solution)/shard_map/all_to_all | solution.py:43
  81.7 21.0 %all-to-all-start.3 = ((f32[64,1,144]{2,1,0:T(1,128)}), f32[64,1,144]{2,1,0:T(1,128)S(1)}, u32[]{:S(2)}, u32[]{:S(2)}) async-start(f32[64,1,144]{2,1,0:T(1,128)} %broadcast_in_dim.18), calls=%async_computation.3 | async-start | bytes 131072 | tf_op jit(solution)/shard_map/all_to_all | solution.py:15
  104.7 11.3 %all-to-all-start.4 = ((bf16[4,48,1188]{2,1,0:T(8,128)(2,1)}), bf16[4,48,1188]{2,1,0:T(8,128)(2,1)S(1)}, u32[]{:S(2)}, u32[]{:S(2)}) async-start(bf16[4,48,1188]{2,1,0:T(8,128)(2,1)} %broadcast_in_dim.19), calls=%async_computation.4 | async-start | bytes 983040 | tf_op jit(solution)/shard_map/all_to_all | solution.py:15
  121.7 16.6 %all-to-all-start.5 = ((bf16[8,48,1024]{2,1,0:T(8,128)(2,1)}), bf16[8,48,1024]{2,1,0:T(8,128)(2,1)S(1)}, u32[]{:S(2)}, u32[]{:S(2)}) async-start(bf16[8,48,1024]{2,1,0:T(8,128)(2,1)} %bitcast.13), calls=%async_computation.5 | async-start | bytes 1572864 | tf_op jit(solution)/shard_map/all_to_all | solution.py:72
  125.3 19.5 %collective-permute-start.2 = (bf16[192,1024]{1,0:T(8,128)(2,1)S(1)}, bf16[192,1024]{1,0:T(8,128)(2,1)S(1)}, u32[]{:S(2)}, u32[]{:S(2)}) collective-permute-start(bf16[192,1024]{1,0:T(8,128)(2,1)S(1)} %bitcast.50), channel_id=1, source_target_pairs={{0,1},{1,0},{2,3},{3,2},{4,5},{5,4},{6,7},{7,6},{8,9},{9,8},{10,11... | collective-permute-start | bytes 1179656 | tf_op jit(solution)/shard_map/ppermute | solution.py:78
  127.6 17.2 %collective-permute-start.1 = (bf16[192,1188]{1,0:T(8,128)(2,1)S(1)}, bf16[192,1188]{1,0:T(8,128)(2,1)S(1)}, u32[]{:S(2)}, u32[]{:S(2)}) collective-permute-start(bf16[192,1188]{1,0:T(8,128)(2,1)S(1)} %bitcast.45), channel_id=1, source_target_pairs={{0,1},{1,0},{2,3},{3,2},{4,5},{5,4},{6,7},{7,6},{8,9},{9,8},{10,11... | collective-permute-start | bytes 1368584 | tf_op jit(solution)/shard_map/ppermute | solution.py:77
  139.3 23.6 %all-to-all-start.6 = ((bf16[16,6,1024]{2,1,0:T(8,128)(2,1)}), bf16[16,6,1024]{2,1,0:T(8,128)(2,1)S(1)}, u32[]{:S(2)}, u32[]{:S(2)}) async-start(bf16[16,6,1024]{2,1,0:T(8,128)(2,1)} %reshape.156), calls=%async_computation.6 | async-start | bytes 524288 | tf_op jit(solution)/shard_map/all_to_all | solution.py:74

commit v3 on v2

v3 whole, which is shorter than its diff:
```python
import jax
import jax.numpy as jnp
from jax import lax
from jax.experimental import pallas as pl
from jax.experimental.pallas import tpu as pltpu
from jax.sharding import Mesh, PartitionSpec as P

X, Z, Y, C = 4, 16, 4, 2
VOCAB_AXES = ("x", "z")
ROW_AXES = ("y", "core")
SWAP = [(0, 1), (1, 0)]
TILE = 256
BF16, F32 = jnp.bfloat16, jnp.float32
IN_VMEM = pl.BlockSpec(memory_space=pltpu.VMEM)
IN_SMEM = pl.BlockSpec(memory_space=pltpu.SMEM)


def call(kernel, out_shape, core_index, *operands):
    return pl.pallas_call(
        kernel,
        out_shape=out_shape,
        in_specs=[IN_SMEM] + [IN_VMEM] * len(operands),
        out_specs=IN_VMEM,
        compiler_params=pltpu.CompilerParams(vmem_limit_bytes=24 * 2**20),
    )(core_index, *operands)


def gather_over(block, axis):
    size = lax.axis_size(axis)
    copies = jnp.broadcast_to(block[None], (size,) + block.shape)
    return lax.all_to_all(copies, axis, 0, 0)


def logits_kernel(core_ref, rows_ref, head_ref, other_ref, out_ref):
    core = core_ref[0]
    slice_width = rows_ref.shape[-1]
    own = rows_ref[:, pl.ds(core, 1)].reshape(-1, slice_width)
    rest = rows_ref[:, pl.ds(1 - core, 1)].reshape(-1, slice_width)

    def dot(rows, part):
        return lax.dot_general(rows, part, (((1,), (1,)), ((), ())), preferred_element_type=F32)

    for first in range(0, head_ref.shape[0], TILE):
        span = pl.ds(first, TILE)
        tile = dot(own, head_ref[span, :]) + dot(rest, other_ref[span, :])
        out_ref[:, :, span] = tile.reshape(out_ref.shape[:2] + (TILE,))


def partial_kernel(core_ref, grad_ref, head_ref, other_ref, out_ref):
    core = core_ref[0]
    grad = grad_ref[...]
    blocks, _, own, slice_width = out_ref.shape
    for place, part in ((core, head_ref), (1 - core, other_ref)):
        for first in range(0, slice_width, TILE):
            span = pl.ds(first, TILE)
            tile = jnp.dot(grad, part[:, span], preferred_element_type=F32).astype(BF16)
            out_ref[:, pl.ds(place, 1), :, span] = tile.reshape(blocks, 1, own, TILE)


def per_device(hidden, head, targets, upstream):
    width, slice_width = head.shape
    token_count = targets.shape[0]
    own = token_count // (Y * C)
    padded = -(-width // TILE) * TILE
    core = lax.axis_index("core")
    core_index = core[None]
    row_first = lax.axis_index(ROW_AXES) * own

    head_other = lax.ppermute(head, "core", SWAP)
    pad = lambda a: jnp.pad(a, ((0, padded - width), (0, 0)))
    own_target = lax.dynamic_slice_in_dim(targets, row_first, own, 0) - lax.axis_index(VOCAB_AXES) * width
    own_weight = lax.dynamic_slice_in_dim(upstream, row_first, own, 0)

    by_z = gather_over(hidden, "z").reshape(1, C, own, slice_width)
    by_z, head, head_other, own_target, own_weight = lax.optimization_barrier(
        (by_z, pad(head), pad(head_other), own_target, own_weight)
    )
    copies = jnp.broadcast_to(by_z, (X, C, own, slice_width)).reshape(X * C, own, slice_width)
    both = lax.all_to_all(copies, ("x", "core"), 0, 0).reshape(X, C, own, slice_width)

    out = jax.ShapeDtypeStruct((Y, own, padded), F32)
    chip_logits = call(logits_kernel, out, core_index, both, head, head_other)
    logits = jnp.sum(lax.all_to_all(chip_logits, "y", 0, 0), axis=0)

    column = lax.broadcasted_iota(jnp.int32, logits.shape, 1)
    valid = column < width
    target_mask = (column == own_target[:, None]) & valid
    local_top = jnp.max(jnp.where(valid, logits, -jnp.inf), axis=1)
    local_total = jnp.sum(jnp.where(valid, jnp.exp(logits - local_top[:, None]), 0.0), axis=1)
    local_target = jnp.sum(jnp.where(target_mask, logits, 0.0), axis=1)
    stats = jnp.concatenate([local_top, local_total, local_target])
    stats = gather_over(stats[None], VOCAB_AXES).reshape(X * Z, 3, own)
    top = jnp.max(stats[:, 0], axis=0)
    total = jnp.sum(stats[:, 1] * jnp.exp(stats[:, 0] - top), axis=0)
    lse = top + jnp.log(total)
    token_loss = lse - jnp.sum(stats[:, 2], axis=0)
    probability = jnp.where(valid, jnp.exp(logits - lse[:, None]), 0.0)
    grad_rows = ((probability - target_mask.astype(F32)) * own_weight[:, None]).astype(BF16)

    grad_rows, token_loss = lax.optimization_barrier((grad_rows, token_loss))
    grad_half = gather_over(grad_rows, "y").reshape(Y * own, padded)

    out = jax.ShapeDtypeStruct((X, C, own, slice_width), BF16)
    partial = call(partial_kernel, out, core_index, grad_half, head, head_other)
    over_x = lax.all_to_all(partial.reshape(X * C, own, slice_width), ("x", "core"), 0, 0)
    over_x, both, grad_half = lax.optimization_barrier((over_x, both, grad_half))
    over_x = jnp.sum(over_x.reshape(X, C * own, slice_width).astype(F32), axis=0).astype(BF16)
    over_z = lax.all_to_all(over_x.reshape(Z, -1, slice_width), "z", 0, 0)
    grad_hidden = jnp.sum(over_z.astype(F32), axis=0).astype(BF16)

    pick = lambda index: lax.dynamic_index_in_dim(both, index, 1, keepdims=False).reshape(-1, slice_width)
    hidden_own, hidden_other = pick(core), pick(1 - core)
    grad_rest = lax.ppermute(grad_half, "core", SWAP)
    hidden_rest = lax.ppermute(hidden_other, "core", SWAP)

    def head_part(grad, rows):
        return lax.dot_general(grad[:, :width], rows, (((0,), (0,)), ((), ())), preferred_element_type=F32)

    grad_head = (head_part(grad_half, hidden_own) + head_part(grad_rest, hidden_rest)).astype(BF16)
    return token_loss, grad_hidden, grad_head


def solution(mesh):
    torus = Mesh(mesh.devices.reshape(X, Z, Y, C), VOCAB_AXES + ROW_AXES)
    return jax.shard_map(
        per_device,
        mesh=torus,
        in_specs=(P(VOCAB_AXES, ROW_AXES), P(VOCAB_AXES, ROW_AXES), P(), P()),
        out_specs=(P(ROW_AXES), P(VOCAB_AXES, ROW_AXES), P(VOCAB_AXES, ROW_AXES)),
        check_vma=False,
    )
```

time: 164 us -> 167 us (1.018)
  blocking collectives: 33.8 us -> 48.5 us
  waiting for transfers between devices: 72 us -> 58 us
  matrix products: 14.1 us -> 3.11 us
  local copies, waits for them, and re-layouts: 5.7 us -> 14.3 us
  Pallas kernels: 0 us -> 3.04 us
    all_to_all x0 -> x1, blocking collectives: none -> 17.3 us  [per_device(): lax.all_to_all(copies, ('x', 'core'), 0, 0).reshape(X, C, own, slice_width)]
    dot_general x6 -> x2, matrix products: 14.1 us -> 3.11 us  [head_part(): lax.dot_general(grad[:, :width], rows, (((0,), (0,)), ((), ())), preferre...]
    all_to_all x3 -> x2, waiting for transfers between devices: 37.6 us -> 28.6 us  [the longest x1 15.5 us: per_device(): over_z = lax.all_to_all(over_x.reshape(Z, -1, slice_width), 'z', 0, 0)]
    unnamed x0 -> x10, local copies, waits for them, and re-layouts: none -> 5.96 us
    all_to_all x2 -> x1, waiting for transfers between devices: 20.9 us -> 15.3 us  [gather_over(): return lax.all_to_all(copies, axis, 0, 0)]
    all_to_all x2 -> x1, starting transfers between devices: 10.7 us -> 15.2 us  [gather_over(): return lax.all_to_all(copies, axis, 0, 0)]
    all_to_all x3 -> x2, starting transfers between devices: 12.6 us -> 8.25 us  [the longest x1 4.71 us: per_device(): over_z = lax.all_to_all(over_x.reshape(Z, -1, slice_width), 'z', 0, 0)]
    pad x0 -> x2, local copies, waits for them, and re-layouts: none -> 3.88 us  [per_device(): pad = lambda a: jnp.pad(a, ((0, padded - width), (0, 0)))]
  transfers between devices with their start and end apart: 9 -> 7, of which waited for: 6 -> 4; matrix products, arithmetic and copies ran while one was open for 6% -> 6% of each run, Pallas kernels for 0% -> 0%
where the time goes in v3:
time: 167 us; the launch traced here: 166 us
  waiting for transfers between devices  58 us (35%)
  blocking collectives  48.5 us (29%)
  starting transfers between devices  34.2 us (20%)
  local copies, waits for them, and re-layouts  14.3 us (9%)
  other arithmetic  4.3 us (3%)
  matrix products  3.11 us (2%)
  Pallas kernels  3.04 us (2%)
    all_to_all x2, blocking collectives, gather_over(): return lax.all_to_all(copies, axis, 0, 0)  31.1 us
    all_to_all x1, blocking collectives, per_device(): lax.all_to_all(copies, ('x', 'core'), 0, 0).reshape(X, C, own, slice_width)  17.3 us
    all_to_all x1, waiting for transfers between devices, per_device(): over_z = lax.all_to_all(over_x.reshape(Z, -1, slice_width), 'z', 0, 0)  15.5 us
    all_to_all x1, waiting for transfers between devices, gather_over(): return lax.all_to_all(copies, axis, 0, 0)  15.3 us
    all_to_all x1, starting transfers between devices, gather_over(): return lax.all_to_all(copies, axis, 0, 0)  15.2 us
    all_to_all x1, waiting for transfers between devices, per_device(): logits = jnp.sum(lax.all_to_all(chip_logits, 'y', 0, 0), axis=0)  14.1 us
    all_to_all x1, waiting for transfers between devices, per_device(): lax.all_to_all(partial.reshape(X * C, own, slice_width), ('x', 'core'), 0...  13.1 us
    unnamed x10, local copies, waits for them, and re-layouts  5.96 us
  transfers between devices with their start and end apart: 7, of which 4 were waited for; matrix products, arithmetic and copies ran while one was open for 6% of the time, Pallas kernels for 0%

profile of v3, /device:TPU:32, one launch (start us, length us, event | category | flops | bytes accessed | tf_op | source)
XLA Modules:
  0.0 166.3 jit_solution(8130776693575998887)
XLA Ops:
  0.6 1.9 %collective-permute-start = (bf16[1188,1024]{1,0:T(8,128)(2,1)}, bf16[1188,1024]{1,0:T(8,128)(2,1)}, u32[]{:S(2)}, u32[]{:S(2)}) collective-permute-start(bf16[1188,1024]{1,0:T(8,128)(2,1)} %param.5), channel_id=1, source_target_pairs={{0,1},{1,0},{2,3},{3,2},{4,5},{5,4},{6,7},{7,6},{8,9},{9,8},{10,11... | collective-permute-start | bytes 7299080 | tf_op jit(solution)/shard_map/ppermute | solution.py:69
  2.6 1.4 broadcast_in_dim.42
  4.0 15.2 %all-to-all-start = ((bf16[16,6,1024]{2,1,0:T(8,128)(2,1)}), bf16[16,6,1024]{2,1,0:T(8,128)(2,1)S(1)}, u32[]{:S(2)}, u32[]{:S(2)}) async-start(bf16[16,6,1024]{2,1,0:T(8,128)(2,1)} %broadcast_in_dim.42), calls=%async_computation | async-start | bytes 524288 | tf_op jit(solution)/shard_map/all_to_all | solution.py:31
  19.2 1.9 %pad.7.head_ref = bf16[1280,1024]{1,0:T(8,128)(2,1)S(1)} pad(bf16[1188,1024]{1,0:T(8,128)(2,1)} %param.5, bf16[]{:T(256)} %constant.17.clone.1), padding=0_92x0_0 | pad | bytes 5054466 | tf_op jit(solution)/shard_map/jit(_pad)/pad | solution.py:70
  21.2 0.8 dynamic_slice.14
  21.9 0.8 dynamic-slice_subtract_fusion
  22.7 15.3 %all-to-all-done = bf16[16,6,1024]{2,1,0:T(8,128)(2,1)S(1)} async-done(((bf16[16,6,1024]{2,1,0:T(8,128)(2,1)}), bf16[16,6,1024]{2,1,0:T(8,128)(2,1)S(1)}, u32[]{:S(2)}, u32[]{:S(2)}) %all-to-all-start) | async-done | bytes 196640 | tf_op jit(solution)/shard_map/all_to_all | solution.py:31
  38.0 0.1 reshape.53
  38.0 0.0 collective-permute-done
  38.0 1.9 %pad.8.other_ref = bf16[1280,1024]{1,0:T(8,128)(2,1)S(1)} pad(bf16[1188,1024]{1,0:T(8,128)(2,1)} %collective-permute-done, bf16[]{:T(256)} %constant.17.clone.1), padding=0_92x0_0 | pad | bytes 5054466 | tf_op jit(solution)/shard_map/jit(_pad)/pad | solution.py:70
  40.0 0.1 broadcast_in_dim.44
  40.1 17.3 %all_to_all.35 = bf16[8,48,1024]{2,1,0:T(8,128)(2,1)S(1)} all-to-all(bf16[8,48,1024]{2,1,0:T(8,128)(2,1)S(1)} %bitcast.33), channel_id=1, replica_groups=mesh['x'=4,'z'=16,'y'=4,'core'=2] {'x','core'}, dimensions={0} | all-to-all | bytes 1572864 | tf_op jit(solution)/shard_map/all_to_all | solution.py:79
  57.4 1.8 %shard_map.67 = f32[4,48,1280]{2,1,0:T(8,128)S(1)} custom-call(s32[1]{0:T(128)} %bitcast.core_ref, bf16[4,2,48,1024]{3,2,1,0:T(8,128)(2,1)S(1)} %bitcast.29, bf16[1280,1024]{1,0:T(8,128)(2,1)S(1)} %pad.7.head_ref, bf16[1280,1024]{1,0:T(8,128)(2,1)S(1)} %pad.8.other_ref), custom_call_target="tpu_custom_call" | custom-call | tf_op jit(solution)/shard_map/pallas_call | solution.py:19
  59.3 0.0 copy-start
  59.3 1.5 copy-done
  60.8 0.9 copy-done.2
  61.7 0.9 copy-done.3
  62.6 4.5 %all-to-all-start.2 = ((f32[4,48,1280]{2,1,0:T(8,128)}), f32[4,48,1280]{2,1,0:T(8,128)}, u32[]{:S(2)}, u32[]{:S(2)}) async-start(f32[4,48,1280]{2,1,0:T(8,128)} %copy-done.3), calls=%async_computation.2 | async-start | bytes 1966080 | tf_op jit(solution)/shard_map/all_to_all | solution.py:83
  67.1 14.1 %all-to-all-done.2 = f32[4,48,1280]{2,1,0:T(8,128)} async-done(((f32[4,48,1280]{2,1,0:T(8,128)}), f32[4,48,1280]{2,1,0:T(8,128)}, u32[]{:S(2)}, u32[]{:S(2)}) %all-to-all-start.2) | async-done | bytes 983072 | tf_op jit(solution)/shard_map/all_to_all | solution.py:83
  81.3 1.3 reduce_sum.69
  82.5 0.1 select_reduce_fusion.2
  82.7 0.3 select_reduce_fusion.1
  82.9 0.1 pad_maximum_fusion
  83.1 20.8 %all_to_all.36 = f32[64,1,144]{2,1,0:T(1,128)S(1)} all-to-all(f32[64,1,144]{2,1,0:T(1,128)S(1)} %broadcast_in_dim.47), channel_id=1, replica_groups=mesh['x'=4,'z'=16,'y'=4,'core'=2] {'x','z'}, dimensions={0} | all-to-all | bytes 73728 | tf_op jit(solution)/shard_map/all_to_all | solution.py:31
  103.9 0.1 copy.8
  104.0 0.1 slice_reduce_fusion
  104.1 0.2 fusion.5
  104.3 0.5 fusion.7
  104.8 0.2 multiply_convert_fusion
  105.1 10.3 %all_to_all.37 = bf16[4,48,1280]{2,1,0:T(8,128)(2,1)S(1)} all-to-all(bf16[4,48,1280]{2,1,0:T(8,128)(2,1)S(1)} %broadcast_in_dim.48), channel_id=1, replica_groups=mesh['x'=4,'z'=16,'y'=4,'core'=2] {'y'}, dimensions={0} | all-to-all | bytes 983040 | tf_op jit(solution)/shard_map/all_to_all | solution.py:31
  115.4 1.7 %copy-done.1 = bf16[1280,1024]{1,0:T(8,128)(2,1)S(1)} copy-done((bf16[1280,1024]{1,0:T(8,128)(2,1)S(1)}, bf16[1280,1024]{1,0:T(8,128)(2,1)}, u32[]{:S(2)}) %copy-start.1) | copy-done | bytes 2621464
  117.1 1.2 shard_map.68
  118.3 0.0 copy-start.4
  118.3 0.9 copy-done.4
  119.2 3.5 %all-to-all-start.5 = ((bf16[8,48,1024]{2,1,0:T(8,128)(2,1)}), bf16[8,48,1024]{2,1,0:T(8,128)(2,1)S(1)}, u32[]{:S(2)}, u32[]{:S(2)}) async-start(bf16[8,48,1024]{2,1,0:T(8,128)(2,1)} %bitcast.31), calls=%async_computation.5 | async-start | bytes 1572864 | tf_op jit(solution)/shard_map/all_to_all | solution.py:105
  122.7 13.1 %all-to-all-done.5 = bf16[8,48,1024]{2,1,0:T(8,128)(2,1)S(1)} async-done(((bf16[8,48,1024]{2,1,0:T(8,128)(2,1)}), bf16[8,48,1024]{2,1,0:T(8,128)(2,1)S(1)}, u32[]{:S(2)}, u32[]{:S(2)}) %all-to-all-start.5) | async-done | bytes 786464 | tf_op jit(solution)/shard_map/all_to_all | solution.py:105
  135.8 1.9 %collective-permute-start.1 = (bf16[192,1280]{1,0:T(8,128)(2,1)S(1)}, bf16[192,1280]{1,0:T(8,128)(2,1)S(1)}, u32[]{:S(2)}, u32[]{:S(2)}) collective-permute-start(bf16[192,1280]{1,0:T(8,128)(2,1)S(1)} %bitcast.27), channel_id=1, source_target_pairs={{0,1},{1,0},{2,3},{3,2},{4,5},{5,4},{6,7},{7,6},{8,9},{9,8},{10,11... | collective-permute-start | bytes 1474568 | tf_op jit(solution)/shard_map/ppermute | solution.py:113
  137.7 1.2 constant_dynamic-slice_fusion
  138.9 2.4 %collective-permute-start.2 = (bf16[192,1024]{1,0:T(8,128)(2,1)S(1)}, bf16[192,1024]{1,0:T(8,128)(2,1)S(1)}, u32[]{:S(2)}, u32[]{:S(2)}) collective-permute-start(bf16[192,1024]{1,0:T(8,128)(2,1)S(1)} %bitcast.38), channel_id=1, source_target_pairs={{0,1},{1,0},{2,3},{3,2},{4,5},{5,4},{6,7},{7,6},{8,9},{9,8},{10,11... | collective-permute-start | bytes 1179656 | tf_op jit(solution)/shard_map/ppermute | solution.py:114
  141.3 0.1 bitcast_reduce_fusion
  141.5 0.8 reshape.60
  142.2 4.7 %all-to-all-start.6 = ((bf16[16,6,1024]{2,1,0:T(8,128)(2,1)}), bf16[16,6,1024]{2,1,0:T(8,128)(2,1)S(1)}, u32[]{:S(2)}, u32[]{:S(2)}) async-start(bf16[16,6,1024]{2,1,0:T(8,128)(2,1)} %reshape.60), calls=%async_computation.6 | async-start | bytes 524288 | tf_op jit(solution)/shard_map/all_to_all | solution.py:108
  146.9 0.8 fusion.1
  147.8 0.0 collective-permute-done.2
  147.8 0.0 collective-permute-done.1
  147.8 2.3 %add_convert_fusion = bf16[1188,1024]{1,0:T(8,128)(2,1)} fusion(f32[1188,1024]{1,0:T(8,128)S(1)} %fusion.1, bf16[192,1024]{1,0:T(8,128)(2,1)S(1)} %collective-permute-done.2, bf16[192,1280]{1,0:T(8,128)(2,1)S(1)} %collective-permute-done.1), kind=kOutput, calls=%fused_computation | convolution fusion | flops 469573632 | bytes 8183808 | tf_op jit(solution)/shard_map/dot_general | solution.py:117
  150.1 15.5 %all-to-all-done.6 = bf16[16,6,1024]{2,1,0:T(8,128)(2,1)S(1)} async-done(((bf16[16,6,1024]{2,1,0:T(8,128)(2,1)}), bf16[16,6,1024]{2,1,0:T(8,128)(2,1)S(1)}, u32[]{:S(2)}, u32[]{:S(2)}) %all-to-all-start.6) | async-done | bytes 196640 | tf_op jit(solution)/shard_map/all_to_all | solution.py:108
  165.6 0.7 reduce_sum.75
  (6 shorter events, 0.1 us)
Async XLA Ops:
  0.6 37.4 %collective-permute-start = (bf16[1188,1024]{1,0:T(8,128)(2,1)}, bf16[1188,1024]{1,0:T(8,128)(2,1)}, u32[]{:S(2)}, u32[]{:S(2)}) collective-permute-start(bf16[1188,1024]{1,0:T(8,128)(2,1)} %param.5), channel_id=1, source_target_pairs={{0,1},{1,0},{2,3},{3,2},{4,5},{5,4},{6,7},{7,6},{8,9},{9,8},{10,11... | collective-permute-start | bytes 7299080 | tf_op jit(solution)/shard_map/ppermute | solution.py:69
  4.0 34.0 %all-to-all-start = ((bf16[16,6,1024]{2,1,0:T(8,128)(2,1)}), bf16[16,6,1024]{2,1,0:T(8,128)(2,1)S(1)}, u32[]{:S(2)}, u32[]{:S(2)}) async-start(bf16[16,6,1024]{2,1,0:T(8,128)(2,1)} %broadcast_in_dim.42), calls=%async_computation | async-start | bytes 524288 | tf_op jit(solution)/shard_map/all_to_all | solution.py:31
  59.3 1.5 copy-start
  60.8 0.9 copy-start.2
  61.7 0.9 copy-start.3
  62.6 18.6 %all-to-all-start.2 = ((f32[4,48,1280]{2,1,0:T(8,128)}), f32[4,48,1280]{2,1,0:T(8,128)}, u32[]{:S(2)}, u32[]{:S(2)}) async-start(f32[4,48,1280]{2,1,0:T(8,128)} %copy-done.3), calls=%async_computation.2 | async-start | bytes 1966080 | tf_op jit(solution)/shard_map/all_to_all | solution.py:83
  115.3 1.7 %copy-start.1 = (bf16[1280,1024]{1,0:T(8,128)(2,1)S(1)}, bf16[1280,1024]{1,0:T(8,128)(2,1)}, u32[]{:S(2)}) copy-start(bf16[1280,1024]{1,0:T(8,128)(2,1)} %copy-done) | copy-start | bytes 7864324
  118.3 0.9 copy-start.4
  119.2 16.6 %all-to-all-start.5 = ((bf16[8,48,1024]{2,1,0:T(8,128)(2,1)}), bf16[8,48,1024]{2,1,0:T(8,128)(2,1)S(1)}, u32[]{:S(2)}, u32[]{:S(2)}) async-start(bf16[8,48,1024]{2,1,0:T(8,128)(2,1)} %bitcast.31), calls=%async_computation.5 | async-start | bytes 1572864 | tf_op jit(solution)/shard_map/all_to_all | solution.py:105
  135.8 12.0 %collective-permute-start.1 = (bf16[192,1280]{1,0:T(8,128)(2,1)S(1)}, bf16[192,1280]{1,0:T(8,128)(2,1)S(1)}, u32[]{:S(2)}, u32[]{:S(2)}) collective-permute-start(bf16[192,1280]{1,0:T(8,128)(2,1)S(1)} %bitcast.27), channel_id=1, source_target_pairs={{0,1},{1,0},{2,3},{3,2},{4,5},{5,4},{6,7},{7,6},{8,9},{9,8},{10,11... | collective-permute-start | bytes 1474568 | tf_op jit(solution)/shard_map/ppermute | solution.py:113
  138.9 8.9 %collective-permute-start.2 = (bf16[192,1024]{1,0:T(8,128)(2,1)S(1)}, bf16[192,1024]{1,0:T(8,128)(2,1)S(1)}, u32[]{:S(2)}, u32[]{:S(2)}) collective-permute-start(bf16[192,1024]{1,0:T(8,128)(2,1)S(1)} %bitcast.38), channel_id=1, source_target_pairs={{0,1},{1,0},{2,3},{3,2},{4,5},{5,4},{6,7},{7,6},{8,9},{9,8},{10,11... | collective-permute-start | bytes 1179656 | tf_op jit(solution)/shard_map/ppermute | solution.py:114
  142.2 23.4 %all-to-all-start.6 = ((bf16[16,6,1024]{2,1,0:T(8,128)(2,1)}), bf16[16,6,1024]{2,1,0:T(8,128)(2,1)S(1)}, u32[]{:S(2)}, u32[]{:S(2)}) async-start(bf16[16,6,1024]{2,1,0:T(8,128)(2,1)} %reshape.60), calls=%async_computation.6 | async-start | bytes 524288 | tf_op jit(solution)/shard_map/all_to_all | solution.py:108

commit v4 on v3

v4 whole, which is shorter than its diff:
```python
import jax
import jax.numpy as jnp
from jax import lax
from jax.experimental import pallas as pl
from jax.experimental.pallas import tpu as pltpu
from jax.sharding import Mesh, PartitionSpec as P

X, Z, Y, C = 4, 16, 4, 2
VOCAB_AXES = ("x", "z")
ROW_AXES = ("y", "core")
SWAP = [(0, 1), (1, 0)]
TILE = 256
LANES = 128
BF16, F32 = jnp.bfloat16, jnp.float32
IN_VMEM = pl.BlockSpec(memory_space=pltpu.VMEM)
IN_SMEM = pl.BlockSpec(memory_space=pltpu.SMEM)


def call(kernel, out_shape, flops, core_index, *operands):
    moved = sum(a.size * a.dtype.itemsize for a in operands) + out_shape.size * out_shape.dtype.itemsize
    return pl.pallas_call(
        kernel,
        out_shape=out_shape,
        in_specs=[IN_SMEM] + [IN_VMEM] * len(operands),
        out_specs=IN_VMEM,
        cost_estimate=pl.CostEstimate(flops=flops, bytes_accessed=moved, transcendentals=0),
        compiler_params=pltpu.CompilerParams(vmem_limit_bytes=8 * 2**20),
    )(core_index, *operands)


def gather_over(block, axis):
    size = lax.axis_size(axis)
    copies = jnp.broadcast_to(block[None], (size,) + block.shape)
    return lax.all_to_all(copies, axis, 0, 0)


def spans(length):
    return [pl.ds(first, min(TILE, length - first)) for first in range(0, length, TILE)]


def logits_kernel(core_ref, rows_ref, head_ref, other_ref, out_ref):
    core = core_ref[0]
    slice_width = rows_ref.shape[-1]
    own = rows_ref[:, pl.ds(core, 1)].reshape(-1, slice_width)
    rest = rows_ref[:, pl.ds(1 - core, 1)].reshape(-1, slice_width)

    def dot(rows, part):
        return lax.dot_general(rows, part, (((1,), (1,)), ((), ())), preferred_element_type=F32)

    for span in spans(head_ref.shape[0]):
        tile = dot(own, head_ref[span, :]) + dot(rest, other_ref[span, :])
        out_ref[:, :, span] = tile.reshape(out_ref.shape[:2] + (span.size,))


def partial_kernel(core_ref, weight_ref, head_ref, other_ref, out_ref):
    core = core_ref[0]
    blocks, _, own, slice_width = out_ref.shape
    weight = weight_ref[:, : head_ref.shape[0]]
    for place, part in ((core, head_ref), (1 - core, other_ref)):
        for span in spans(slice_width):
            tile = jnp.dot(weight, part[:, span], preferred_element_type=F32).astype(BF16)
            out_ref[:, pl.ds(place, 1), :, span] = tile.reshape(blocks, 1, own, span.size)


def to_pieces(columns):
    pieces = []
    for column in columns:
        for _ in range(3):
            piece = lax.reduce_precision(column, 8, 7)
            pieces.append(piece.astype(BF16))
            column = column - piece
    return jnp.stack(pieces, axis=1)


def from_pieces(pieces):
    return jnp.sum(pieces.astype(F32).reshape(pieces.shape[:-1] + (-1, 3)), axis=-1)


def halve(rows, axis, bit):
    size = lax.axis_size(axis)
    mine = (lax.axis_index(axis) >> bit) & 1
    pair = rows.reshape((2, -1) + rows.shape[1:])
    keep, send = (lax.dynamic_index_in_dim(pair, k, 0, keepdims=False) for k in (mine, 1 - mine))
    return keep + lax.ppermute(send, axis, [(i, i ^ (1 << bit)) for i in range(size)])


def per_device(hidden, head, targets, upstream):
    width, slice_width = head.shape
    block = hidden.shape[0]
    token_count = targets.shape[0]
    own = token_count // (Y * C)
    padded = -(-width // LANES) * LANES
    core = lax.axis_index("core")
    core_index = core[None]
    row_first = lax.axis_index(ROW_AXES) * own
    block_first = lax.axis_index(VOCAB_AXES) * block
    chunk_first = lax.axis_index("x") * block * Z
    barrier = lax.optimization_barrier

    def in_core_order(mine, other, axis):
        return jnp.where(core == 0, jnp.stack([mine, other], axis), jnp.stack([other, mine], axis))

    by_z = gather_over(hidden, "z").reshape(1, C, own, slice_width)
    head_other = lax.ppermute(head, "core", SWAP)
    local_targets = targets - lax.axis_index(VOCAB_AXES) * width
    own_target = lax.dynamic_slice_in_dim(local_targets, row_first, own, 0)
    block_weight = lax.dynamic_slice_in_dim(upstream, block_first, block, 0)
    pick_target = local_targets[:, None] == lax.broadcasted_iota(jnp.int32, (token_count, width), 1)
    target_rows = jnp.dot(pick_target.astype(BF16), head, preferred_element_type=F32).astype(BF16)
    target_rows = halve(target_rows, "x", 1)
    by_z, head_other, own_target, block_weight, target_rows = barrier(
        (by_z, head_other, own_target, block_weight, target_rows)
    )

    copies = jnp.broadcast_to(by_z, (X, C, own, slice_width)).reshape(X * C, own, slice_width)
    both = lax.all_to_all(copies, ("x", "core"), 0, 0).reshape(X, C, own, slice_width)
    target_rows = halve(target_rows, "x", 0)
    both, target_rows = barrier((both, target_rows))

    out = jax.ShapeDtypeStruct((Y, own, width), F32)
    flops = 4 * Y * own * width * slice_width
    chip_logits = call(logits_kernel, out, flops, core_index, both, head, head_other)
    logit_parts = lax.all_to_all(chip_logits, "y", 0, 0)
    target_rows = halve(target_rows, "z", 3)
    logit_parts, target_rows = barrier((logit_parts, target_rows))
    logits = jnp.sum(logit_parts, axis=0)

    target_mask = lax.broadcasted_iota(jnp.int32, logits.shape, 1) == own_target[:, None]
    top = jnp.max(logits, axis=1)
    weight = jnp.exp(logits - top[:, None])
    total = jnp.sum(weight, axis=1)
    target_logit = jnp.sum(jnp.where(target_mask, logits, 0.0), axis=1)
    weight = jnp.where(target_mask, 0.0, weight).astype(BF16)
    tail = to_pieces([top, total, target_logit])
    tail = jnp.pad(tail, ((0, 0), (0, padded - width - tail.shape[1])))
    weights = gather_over(jnp.concatenate([weight, tail], axis=1), "y")
    target_rows = halve(target_rows, "z", 2)
    weights, target_rows = barrier((weights, target_rows))
    weights = weights.reshape(Y * own, padded)

    out = jax.ShapeDtypeStruct((X, C, own, slice_width), BF16)
    partial = call(partial_kernel, out, flops, core_index, weights, head, head_other)
    over_x = lax.all_to_all(partial.reshape(X * C, own, slice_width), ("x", "core"), 0, 0)
    over_x = over_x.reshape(X, C * own, slice_width)
    target_rows = halve(target_rows, "z", 1)

    weights_rest = lax.ppermute(weights, "core", SWAP)
    read = lambda w: from_pieces(w[:, width : width + 9]).reshape(Y, own, 3)
    stats = in_core_order(read(weights), read(weights_rest), 1).reshape(token_count, 3).T
    by_x = lax.all_gather(stats, "x")
    x_top = jnp.max(by_x[:, 0], axis=0)
    x_scale = jnp.exp(by_x[:, 0] - x_top)
    x_stats = jnp.stack([x_top, jnp.sum(x_scale * by_x[:, 1], axis=0), jnp.sum(by_x[:, 2], axis=0)])
    scale = lax.dynamic_slice_in_dim(x_scale, chunk_first, C * own, 1)
    over_x, target_rows, scale = barrier((over_x, target_rows, scale))
    over_x = jnp.sum(over_x.astype(F32) * scale[:, :, None], axis=0).astype(BF16)

    over_z = lax.all_to_all(over_x.reshape(Z, block, slice_width), "z", 0, 0)
    target_rows = halve(target_rows, "z", 0)
    by_z_stats = lax.all_gather(x_stats, "z")
    z_top = jnp.max(by_z_stats[:, 0], axis=0)
    z_scale = jnp.exp(by_z_stats[:, 0] - z_top)
    all_total = jnp.sum(z_scale * by_z_stats[:, 1], axis=0)
    all_target = jnp.sum(by_z_stats[:, 2], axis=0)
    lse = z_top + jnp.log(all_total)
    loss = lse - all_target
    target_grad = jnp.exp(-loss) - 1.0
    of_block = lambda a: lax.dynamic_slice_in_dim(a, block_first, block, a.ndim - 1)
    scale = of_block(z_scale / all_total)[:, :, None]
    grad_hidden = jnp.sum(over_z.astype(F32) * scale, axis=0)
    grad_hidden = grad_hidden + of_block(target_grad)[:, None] * target_rows.astype(F32)
    grad_hidden = (grad_hidden * block_weight[:, None]).astype(BF16)
    token_loss = lax.dynamic_slice_in_dim(loss, row_first, own, 0)

    by_half = lambda a, half: lax.dynamic_index_in_dim(a.reshape(Y, C, own), half, 1, keepdims=False).reshape(-1)
    pick = lambda half: lax.dynamic_index_in_dim(both, half, 1, keepdims=False).reshape(-1, slice_width)
    hidden_rest = lax.ppermute(pick(1 - core), "core", SWAP)
    row_scale = jnp.exp(stats[0] - lse) * upstream
    row_target = target_grad * upstream

    def head_part(half, weights, rows):
        grad = weights[:, :width].astype(F32) * by_half(row_scale, half)[:, None]
        column = lax.broadcasted_iota(jnp.int32, grad.shape, 1)
        at_target = column == by_half(local_targets, half)[:, None]
        grad = jnp.where(at_target, by_half(row_target, half)[:, None], grad).astype(BF16)
        return lax.dot_general(grad, rows, (((0,), (0,)), ((), ())), preferred_element_type=F32)

    grad_head = head_part(core, weights, pick(core)) + head_part(1 - core, weights_rest, hidden_rest)
    return token_loss, grad_hidden, grad_head.astype(BF16)


def solution(mesh):
    torus = Mesh(mesh.devices.reshape(X, Z, Y, C), VOCAB_AXES + ROW_AXES)
    return jax.shard_map(
        per_device,
        mesh=torus,
        in_specs=(P(VOCAB_AXES, ROW_AXES), P(VOCAB_AXES, ROW_AXES), P(), P()),
        out_specs=(P(ROW_AXES), P(VOCAB_AXES, ROW_AXES), P(VOCAB_AXES, ROW_AXES)),
        check_vma=False,
    )
```

time: 167 us -> 206 us (1.23)
  the two profiles are of different devices: /device:TPU:32 before, /device:TPU:40 now
where the time goes in v4:
time: 206 us; the launch traced here: 205 us
  starting transfers between devices  77.2 us (37%)
  blocking collectives  49.7 us (24%)
  waiting for transfers between devices  33.3 us (16%)
  local copies, waits for them, and re-layouts  15.2 us (7%)
  matrix products  11.1 us (5%)
  other arithmetic  10.7 us (5%)
  Pallas kernels  6.54 us (3%)
    all_gather x1, blocking collectives, per_device(): by_z_stats = lax.all_gather(x_stats, 'z')  33.1 us
    ppermute x6, starting transfers between devices, halve(): lax.ppermute(send, axis, [(i, i ^ 1 << bit) for i in range(size)])  30.3 us
    ppermute x6, waiting for transfers between devices, halve(): lax.ppermute(send, axis, [(i, i ^ 1 << bit) for i in range(size)])  25.9 us
    all_to_all x2, starting transfers between devices, gather_over(): return lax.all_to_all(copies, axis, 0, 0)  20 us
    all_gather x1, blocking collectives, per_device(): by_x = lax.all_gather(stats, 'x')  16.7 us
    dot_general x2, matrix products, head_part(): lax.dot_general(grad, rows, (((0,), (0,)), ((), ())), preferred_element_t...  8.21 us
    all_to_all x1, starting transfers between devices, per_device(): over_z = lax.all_to_all(over_x.reshape(Z, block, slice_width), 'z', 0, 0)  7.65 us
    all_to_all x1, waiting for transfers between devices, per_device(): over_z = lax.all_to_all(over_x.reshape(Z, block, slice_width), 'z', 0, 0)  7.37 us
  transfers between devices with their start and end apart: 15, of which 5 were waited for; matrix products, arithmetic and copies ran while one was open for 14% of the time, Pallas kernels for 1%

profile of v4, /device:TPU:40, one launch (start us, length us, event | category | flops | bytes accessed | tf_op | source)
XLA Modules:
  0.0 204.8 jit_solution(13355281157954990119)
XLA Ops:
  0.6 1.9 collective-permute-start
  2.6 1.4 broadcast_in_dim.55
  4.0 15.2 %all-to-all-start = ((bf16[16,6,1024]{2,1,0:T(8,128)(2,1)}), bf16[16,6,1024]{2,1,0:T(8,128)(2,1)S(1)}, u32[]{:S(2)}, u32[]{:S(2)}) async-start(bf16[16,6,1024]{2,1,0:T(8,128)(2,1)} %broadcast_in_dim.55), calls=%async_computation | async-start | bytes 524288 | tf_op jit(solution)/shard_map/all_to_all | solution.py:34
  19.2 0.7 broadcast_subtract_fusion
  19.9 2.9 %fusion.1 = bf16[384,1024]{1,0:T(8,128)(2,1)S(1)} fusion(bf16[1188,1024]{1,0:T(8,128)(2,1)} %head_ref.3, s32[384]{0:T(512)S(1)} %broadcast_subtract_fusion), kind=kOutput, calls=%fused_computation.4 | convolution fusion | flops 935130624 | bytes 3220992 | tf_op jit(solution)/shard_map/dot_general | solution.py:109
  22.8 0.8 dynamic-slice_bitcast_fusion
  23.6 4.9 %collective-permute-start.1 = (bf16[192,1024]{1,0:T(8,128)(2,1)}, bf16[192,1024]{1,0:T(8,128)(2,1)}, u32[]{:S(2)}, u32[]{:S(2)}) collective-permute-start(bf16[192,1024]{1,0:T(8,128)(2,1)} %dynamic-slice_bitcast_fusion), channel_id=1, source_target_pairs={{0,256},{128,384},{256,0},{384,128},{1,257},{129,385},{257,1},{385... | collective-permute-start | bytes 1179656 | tf_op jit(solution)/shard_map/ppermute | solution.py:84
  28.6 1.3 dynamic_slice.88
  29.9 8.4 %collective-permute-done.1 = bf16[192,1024]{1,0:T(8,128)(2,1)} collective-permute-done((bf16[192,1024]{1,0:T(8,128)(2,1)}, bf16[192,1024]{1,0:T(8,128)(2,1)}, u32[]{:S(2)}, u32[]{:S(2)}) %collective-permute-start.1) | collective-permute-done | bytes 393248 | tf_op jit(solution)/shard_map/ppermute | solution.py:84
  38.3 1.8 bitcast_add_fusion
  40.2 1.0 broadcast_in_dim.59
  41.1 4.3 %all-to-all-start.1 = ((bf16[8,48,1024]{2,1,0:T(8,128)(2,1)}), bf16[8,48,1024]{2,1,0:T(8,128)(2,1)S(1)}, u32[]{:S(2)}, u32[]{:S(2)}) async-start(bf16[8,48,1024]{2,1,0:T(8,128)(2,1)} %bitcast.108), calls=%async_computation.1 | async-start | bytes 1572864 | tf_op jit(solution)/shard_map/all_to_all | solution.py:116
  45.4 0.9 dynamic-slice_bitcast_fusion.1
  46.4 3.9 %collective-permute-start.2 = (bf16[96,1024]{1,0:T(8,128)(2,1)S(1)}, bf16[96,1024]{1,0:T(8,128)(2,1)}, u32[]{:S(2)}, u32[]{:S(2)}) collective-permute-start(bf16[96,1024]{1,0:T(8,128)(2,1)S(1)} %dynamic-slice_bitcast_fusion.1), channel_id=1, source_target_pairs={{0,128},{128,0},{256,384},{384,256},{1,129},{129,1},{257,385},{385... | collective-permute-start | bytes 589832 | tf_op jit(solution)/shard_map/ppermute | solution.py:84
  50.3 11.1 %collective-permute-done.2 = bf16[96,1024]{1,0:T(8,128)(2,1)} collective-permute-done((bf16[96,1024]{1,0:T(8,128)(2,1)S(1)}, bf16[96,1024]{1,0:T(8,128)(2,1)}, u32[]{:S(2)}, u32[]{:S(2)}) %collective-permute-start.2) | collective-permute-done | bytes 196640 | tf_op jit(solution)/shard_map/ppermute | solution.py:84
  61.4 1.7 bitcast_add_fusion.1
  63.1 3.7 %shard_map.67 = f32[4,48,1188]{2,1,0:T(8,128)S(1)} custom-call(s32[1]{0:T(128)} %bitcast.3.core_ref, bf16[4,2,48,1024]{3,2,1,0:T(8,128)(2,1)S(1)} %bitcast.104, bf16[1188,1024]{1,0:T(8,128)(2,1)S(1)} %copy-done, bf16[1188,1024]{1,0:T(8,128)(2,1)} %collective-permute-done.other_ref), custom_call_target="tpu_custom_call" | custom-call | flops 934281216 | bytes 6564864 | tf_op jit(solution)/shard_map/pallas_call | solution.py:21
  66.8 0.9 copy-done.2
  67.8 4.9 %all-to-all-start.2 = ((f32[4,48,1188]{2,1,0:T(8,128)}), f32[4,48,1188]{2,1,0:T(8,128)S(1)}, u32[]{:S(2)}, u32[]{:S(2)}) async-start(f32[4,48,1188]{2,1,0:T(8,128)} %copy-done.2), calls=%async_computation.2 | async-start | bytes 1966080 | tf_op jit(solution)/shard_map/all_to_all | solution.py:123
  72.7 0.9 dynamic-slice_bitcast_fusion.2
  73.6 11.2 %collective-permute-start.3 = (bf16[48,1024]{1,0:T(8,128)(2,1)S(1)}, bf16[48,1024]{1,0:T(8,128)(2,1)}, u32[]{:S(2)}, u32[]{:S(2)}) collective-permute-start(bf16[48,1024]{1,0:T(8,128)(2,1)S(1)} %dynamic-slice_bitcast_fusion.2), channel_id=1, source_target_pairs={{0,64},{8,72},{16,80},{24,88},{32,96},{40,104},{48,112},{56,120},{... | collective-permute-start | bytes 294920 | tf_op jit(solution)/shard_map/ppermute | solution.py:84
  84.9 0.6 eq.47
  85.5 0.6 eq.44
  86.1 6.1 %collective-permute-done.3 = bf16[48,1024]{1,0:T(8,128)(2,1)} collective-permute-done((bf16[48,1024]{1,0:T(8,128)(2,1)S(1)}, bf16[48,1024]{1,0:T(8,128)(2,1)}, u32[]{:S(2)}, u32[]{:S(2)}) %collective-permute-start.3) | collective-permute-done | bytes 98336 | tf_op jit(solution)/shard_map/ppermute | solution.py:84
  92.2 1.0 bitcast_add_fusion.2
  93.2 0.8 reduce_sum.103
  93.9 1.1 reduce_max.29
  95.0 1.2 select_reduce_fusion
  96.5 0.8 broadcast_in_dim.60
  97.3 4.8 %all-to-all-start.3 = ((bf16[4,48,1280]{2,1,0:T(8,128)(2,1)}), bf16[4,48,1280]{2,1,0:T(8,128)(2,1)S(1)}, u32[]{:S(2)}, u32[]{:S(2)}) async-start(bf16[4,48,1280]{2,1,0:T(8,128)(2,1)} %broadcast_in_dim.60), calls=%async_computation.3 | async-start | bytes 983040 | tf_op jit(solution)/shard_map/all_to_all | solution.py:34
  102.1 6.2 %collective-permute-start.4 = (bf16[24,1024]{1,0:T(8,128)(2,1)S(1)}, bf16[24,1024]{1,0:T(8,128)(2,1)S(1)}, u32[]{:S(2)}, u32[]{:S(2)}) collective-permute-start(bf16[24,1024]{1,0:T(8,128)(2,1)S(1)} %dynamic-slice_bitcast_fusion.3), channel_id=1, source_target_pairs={{0,32},{8,40},{16,48},{24,56},{32,0},{40,8},{48,16},{56,24},{64,96... | collective-permute-start | bytes 147464 | tf_op jit(solution)/shard_map/ppermute | solution.py:84
  108.3 1.9 constant_dynamic-slice_fusion
  110.2 1.9 collective-permute-start.8
  112.5 2.1 %collective-permute-start.6 = (bf16[12,1024]{1,0:T(8,128)(2,1)S(1)}, bf16[12,1024]{1,0:T(8,128)(2,1)S(1)}, u32[]{:S(2)}, u32[]{:S(2)}) collective-permute-start(bf16[12,1024]{1,0:T(8,128)(2,1)S(1)} %dynamic-slice_bitcast_fusion.4), channel_id=1, source_target_pairs={{0,16},{8,24},{16,0},{24,8},{32,48},{40,56},{48,32},{56,40},{64,80... | collective-permute-start | bytes 73736 | tf_op jit(solution)/shard_map/ppermute | solution.py:84
  114.6 2.1 %collective-permute-start.5 = (bf16[192,1280]{1,0:T(8,128)(2,1)S(1)}, bf16[192,1280]{1,0:T(8,128)(2,1)}, u32[]{:S(2)}, u32[]{:S(2)}) collective-permute-start(bf16[192,1280]{1,0:T(8,128)(2,1)S(1)} %bitcast.100), channel_id=1, source_target_pairs={{0,1},{1,0},{2,3},{3,2},{4,5},{5,4},{6,7},{7,6},{8,9},{9,8},{10,11... | collective-permute-start | bytes 1474568 | tf_op jit(solution)/shard_map/ppermute | solution.py:147
  116.8 2.9 %shard_map.68 = bf16[4,2,48,1024]{3,2,1,0:T(8,128)(2,1)S(1)} custom-call(s32[1]{0:T(128)} %bitcast.3.core_ref, bf16[192,1280]{1,0:T(8,128)(2,1)S(1)} %bitcast.102, bf16[1188,1024]{1,0:T(8,128)(2,1)S(1)} %copy-done, bf16[1188,1024]{1,0:T(8,128)(2,1)} %collective-permute-done.other_ref), custom_call_target="tpu_custom_call" | custom-call | flops 934281216 | bytes 6144000 | tf_op jit(solution)/shard_map/pallas_call | solution.py:21
  119.7 0.9 copy-done.3
  120.6 4.1 %all-to-all-start.4 = ((bf16[8,48,1024]{2,1,0:T(8,128)(2,1)}), bf16[8,48,1024]{2,1,0:T(8,128)(2,1)S(1)}, u32[]{:S(2)}, u32[]{:S(2)}) async-start(bf16[8,48,1024]{2,1,0:T(8,128)(2,1)} %bitcast.106), calls=%async_computation.4 | async-start | bytes 1572864 | tf_op jit(solution)/shard_map/all_to_all | solution.py:143
  124.9 0.9 slice_convert_fusion
  126.2 16.7 %all-gather.2 = f32[4,3,384]{2,1,0:T(4,128)S(1)} all-gather(f32[1,3,384]{2,1,0:T(4,128)S(1)} %bitcast.120), channel_id=2, replica_groups=mesh['x'=4,'z'=16,'y'=4,'core'=2] {'x'}, dimensions={0}, use_global_device_ids=true | all-gather | bytes 23040 | tf_op jit(solution)/shard_map/all_gather | solution.py:150
  143.0 33.1 %all-gather.3 = f32[16,3,384]{2,1,0:T(4,128)S(1)} all-gather(f32[1,3,384]{2,1,0:T(4,128)S(1)} %maximum_bitcast_fusion), channel_id=3, replica_groups=mesh['x'=4,'z'=16,'y'=4,'core'=2] {'z'}, dimensions={0}, use_global_device_ids=true | all-gather | bytes 78336 | tf_op jit(solution)/shard_map/all_gather | solution.py:160
  176.6 3.1 %fusion.3 = f32[1188,1024]{1,0:T(8,128)} fusion(bf16[192,1024]{1,0:T(8,128)(2,1)S(1)} %bitcast.109, bf16[192,1280]{1,0:T(8,128)(2,1)S(1)} %bitcast.103, f32[192]{0:T(256)S(1)} %mul.102, bf16[192]{0:T(256)(128)(2,1)S(1)} %broadcast_in_dim.61, s32[192]{0:T(256)S(1)} %copy-done.4), kind=kOutput, calls=%fused_computation.11 | convolution fusion | flops 468052992 | bytes 5752704 | tf_op jit(solution)/shard_map/dot_general | solution.py:186
  180.9 0.8 convert_element_type.148
  181.7 7.6 %all-to-all-start.5 = ((bf16[16,6,1024]{2,1,0:T(8,128)(2,1)}), bf16[16,6,1024]{2,1,0:T(8,128)(2,1)S(1)}, u32[]{:S(2)}, u32[]{:S(2)}) async-start(bf16[16,6,1024]{2,1,0:T(8,128)(2,1)} %convert_element_type.148), calls=%async_computation.5 | async-start | bytes 524288 | tf_op jit(solution)/shard_map/all_to_all | solution.py:158
  189.4 5.1 %add_convert_fusion = bf16[1188,1024]{1,0:T(8,128)(2,1)} fusion(f32[1188,1024]{1,0:T(8,128)} %fusion.3, bf16[192,1024]{1,0:T(8,128)(2,1)} %collective-permute-done.8, bf16[192,1280]{1,0:T(8,128)(2,1)} %collective-permute-done.5, f32[192]{0:T(256)S(1)} %mul.105, bf16[192]{0:T(256)(128)(2,1)S(1)} %broadcast_in_dim.63, s32[192]{0:T(256)S(1)} %copy-done.5), kind=kOutput, calls=%fused_computation | convolution fusion | flops 470486016 | bytes 8185728 | tf_op jit(solution)/shard_map/dot_general | solution.py:186
  194.6 2.0 collective-permute-start.7
  196.6 7.4 %all-to-all-done.5 = bf16[16,6,1024]{2,1,0:T(8,128)(2,1)S(1)} async-done(((bf16[16,6,1024]{2,1,0:T(8,128)(2,1)}), bf16[16,6,1024]{2,1,0:T(8,128)(2,1)S(1)}, u32[]{:S(2)}, u32[]{:S(2)}) %all-to-all-start.5) | async-done | bytes 196640 | tf_op jit(solution)/shard_map/all_to_all | solution.py:158
  204.1 0.7 multiply_convert_fusion
  (78 shorter events, 3.6 us)
Async XLA Ops:
  0.6 39.5 %collective-permute-start = (bf16[1188,1024]{1,0:T(8,128)(2,1)}, bf16[1188,1024]{1,0:T(8,128)(2,1)}, u32[]{:S(2)}, u32[]{:S(2)}) collective-permute-start(bf16[1188,1024]{1,0:T(8,128)(2,1)} %head_ref.3), channel_id=1, source_target_pairs={{0,1},{1,0},{2,3},{3,2},{4,5},{5,4},{6,7},{7,6},{8,9},{9,8},{10,11... | collective-permute-start | bytes 7299080 | tf_op jit(solution)/shard_map/ppermute | solution.py:104
  4.0 36.1 %all-to-all-start = ((bf16[16,6,1024]{2,1,0:T(8,128)(2,1)}), bf16[16,6,1024]{2,1,0:T(8,128)(2,1)S(1)}, u32[]{:S(2)}, u32[]{:S(2)}) async-start(bf16[16,6,1024]{2,1,0:T(8,128)(2,1)} %broadcast_in_dim.55), calls=%async_computation | async-start | bytes 524288 | tf_op jit(solution)/shard_map/all_to_all | solution.py:34
  23.6 14.7 %collective-permute-start.1 = (bf16[192,1024]{1,0:T(8,128)(2,1)}, bf16[192,1024]{1,0:T(8,128)(2,1)}, u32[]{:S(2)}, u32[]{:S(2)}) collective-permute-start(bf16[192,1024]{1,0:T(8,128)(2,1)} %dynamic-slice_bitcast_fusion), channel_id=1, source_target_pairs={{0,256},{128,384},{256,0},{384,128},{1,257},{129,385},{257,1},{385... | collective-permute-start | bytes 1179656 | tf_op jit(solution)/shard_map/ppermute | solution.py:84
  29.9 33.2 %copy-start = (bf16[1188,1024]{1,0:T(8,128)(2,1)S(1)}, bf16[1188,1024]{1,0:T(8,128)(2,1)}, u32[]{:S(2)}) copy-start(bf16[1188,1024]{1,0:T(8,128)(2,1)} %head_ref.3) | copy-start | bytes 7299076
  41.1 22.0 %all-to-all-start.1 = ((bf16[8,48,1024]{2,1,0:T(8,128)(2,1)}), bf16[8,48,1024]{2,1,0:T(8,128)(2,1)S(1)}, u32[]{:S(2)}, u32[]{:S(2)}) async-start(bf16[8,48,1024]{2,1,0:T(8,128)(2,1)} %bitcast.108), calls=%async_computation.1 | async-start | bytes 1572864 | tf_op jit(solution)/shard_map/all_to_all | solution.py:116
  46.4 15.0 %collective-permute-start.2 = (bf16[96,1024]{1,0:T(8,128)(2,1)S(1)}, bf16[96,1024]{1,0:T(8,128)(2,1)}, u32[]{:S(2)}, u32[]{:S(2)}) collective-permute-start(bf16[96,1024]{1,0:T(8,128)(2,1)S(1)} %dynamic-slice_bitcast_fusion.1), channel_id=1, source_target_pairs={{0,128},{128,0},{256,384},{384,256},{1,129},{129,1},{257,385},{385... | collective-permute-start | bytes 589832 | tf_op jit(solution)/shard_map/ppermute | solution.py:84
  63.1 3.7 %copy-start.1 = (bf16[8,48,1024]{2,1,0:T(8,128)(2,1)}, bf16[8,48,1024]{2,1,0:T(8,128)(2,1)S(1)}, u32[]{:S(2)}) copy-start(bf16[8,48,1024]{2,1,0:T(8,128)(2,1)S(1)} %all-to-all-done.1) | copy-start | bytes 2359300
  66.8 0.9 copy-start.2
  67.8 25.4 %all-to-all-start.2 = ((f32[4,48,1188]{2,1,0:T(8,128)}), f32[4,48,1188]{2,1,0:T(8,128)S(1)}, u32[]{:S(2)}, u32[]{:S(2)}) async-start(f32[4,48,1188]{2,1,0:T(8,128)} %copy-done.2), calls=%async_computation.2 | async-start | bytes 1966080 | tf_op jit(solution)/shard_map/all_to_all | solution.py:123
  73.6 18.7 %collective-permute-start.3 = (bf16[48,1024]{1,0:T(8,128)(2,1)S(1)}, bf16[48,1024]{1,0:T(8,128)(2,1)}, u32[]{:S(2)}, u32[]{:S(2)}) collective-permute-start(bf16[48,1024]{1,0:T(8,128)(2,1)S(1)} %dynamic-slice_bitcast_fusion.2), channel_id=1, source_target_pairs={{0,64},{8,72},{16,80},{24,88},{32,96},{40,104},{48,112},{56,120},{... | collective-permute-start | bytes 294920 | tf_op jit(solution)/shard_map/ppermute | solution.py:84
  97.3 15.1 %all-to-all-start.3 = ((bf16[4,48,1280]{2,1,0:T(8,128)(2,1)}), bf16[4,48,1280]{2,1,0:T(8,128)(2,1)S(1)}, u32[]{:S(2)}, u32[]{:S(2)}) async-start(bf16[4,48,1280]{2,1,0:T(8,128)(2,1)} %broadcast_in_dim.60), calls=%async_computation.3 | async-start | bytes 983040 | tf_op jit(solution)/shard_map/all_to_all | solution.py:34
  102.1 10.3 %collective-permute-start.4 = (bf16[24,1024]{1,0:T(8,128)(2,1)S(1)}, bf16[24,1024]{1,0:T(8,128)(2,1)S(1)}, u32[]{:S(2)}, u32[]{:S(2)}) collective-permute-start(bf16[24,1024]{1,0:T(8,128)(2,1)S(1)} %dynamic-slice_bitcast_fusion.3), channel_id=1, source_target_pairs={{0,32},{8,40},{16,48},{24,56},{32,0},{40,8},{48,16},{56,24},{64,96... | collective-permute-start | bytes 147464 | tf_op jit(solution)/shard_map/ppermute | solution.py:84
  110.2 79.2 %collective-permute-start.8 = (bf16[192,1024]{1,0:T(8,128)(2,1)}, bf16[192,1024]{1,0:T(8,128)(2,1)}, u32[]{:S(2)}, u32[]{:S(2)}) collective-permute-start(bf16[192,1024]{1,0:T(8,128)(2,1)} %bitcast.32), channel_id=1, source_target_pairs={{0,1},{1,0},{2,3},{3,2},{4,5},{5,4},{6,7},{7,6},{8,9},{9,8},{10,11... | collective-permute-start | bytes 1179656 | tf_op jit(solution)/shard_map/ppermute | solution.py:177
  112.5 12.4 %collective-permute-start.6 = (bf16[12,1024]{1,0:T(8,128)(2,1)S(1)}, bf16[12,1024]{1,0:T(8,128)(2,1)S(1)}, u32[]{:S(2)}, u32[]{:S(2)}) collective-permute-start(bf16[12,1024]{1,0:T(8,128)(2,1)S(1)} %dynamic-slice_bitcast_fusion.4), channel_id=1, source_target_pairs={{0,16},{8,24},{16,0},{24,8},{32,48},{40,56},{48,32},{56,40},{64,80... | collective-permute-start | bytes 73736 | tf_op jit(solution)/shard_map/ppermute | solution.py:84
  114.6 10.3 %collective-permute-start.5 = (bf16[192,1280]{1,0:T(8,128)(2,1)S(1)}, bf16[192,1280]{1,0:T(8,128)(2,1)}, u32[]{:S(2)}, u32[]{:S(2)}) collective-permute-start(bf16[192,1280]{1,0:T(8,128)(2,1)S(1)} %bitcast.100), channel_id=1, source_target_pairs={{0,1},{1,0},{2,3},{3,2},{4,5},{5,4},{6,7},{7,6},{8,9},{9,8},{10,11... | collective-permute-start | bytes 1474568 | tf_op jit(solution)/shard_map/ppermute | solution.py:147
  119.7 0.9 copy-start.3
  120.6 55.5 %copy-start.6 = (f32[384]{0:T(512)S(1)}, f32[384]{0:T(512)}, u32[]{:S(2)}) copy-start(f32[384]{0:T(512)} %param.7) | copy-start | bytes 4612
  120.6 56.0 %copy-start.4 = (s32[192]{0:T(256)S(1)}, s32[192]{0:T(256)}, u32[]{:S(2)}) copy-start(s32[192]{0:T(256)} %eq.44) | copy-start | bytes 2308
  120.6 60.1 %all-to-all-start.4 = ((bf16[8,48,1024]{2,1,0:T(8,128)(2,1)}), bf16[8,48,1024]{2,1,0:T(8,128)(2,1)S(1)}, u32[]{:S(2)}, u32[]{:S(2)}) async-start(bf16[8,48,1024]{2,1,0:T(8,128)(2,1)} %bitcast.106), calls=%async_computation.4 | async-start | bytes 1572864 | tf_op jit(solution)/shard_map/all_to_all | solution.py:143
  176.6 12.9 %copy-start.5 = (s32[192]{0:T(256)S(1)}, s32[192]{0:T(256)}, u32[]{:S(2)}) copy-start(s32[192]{0:T(256)} %eq.47) | copy-start | bytes 2308
  181.7 22.2 %all-to-all-start.5 = ((bf16[16,6,1024]{2,1,0:T(8,128)(2,1)}), bf16[16,6,1024]{2,1,0:T(8,128)(2,1)S(1)}, u32[]{:S(2)}, u32[]{:S(2)}) async-start(bf16[16,6,1024]{2,1,0:T(8,128)(2,1)} %convert_element_type.148), calls=%async_computation.5 | async-start | bytes 524288 | tf_op jit(solution)/shard_map/all_to_all | solution.py:158
  189.4 14.7 %copy-start.7 = (f32[6]{0:T(128)S(1)}, f32[6]{0:T(128)}, u32[]{:S(2)}) copy-start(f32[6]{0:T(128)} %dynamic_slice.88) | copy-start | bytes 76
  194.6 9.5 %collective-permute-start.7 = (bf16[6,1024]{1,0:T(8,128)(2,1)S(1)}, bf16[6,1024]{1,0:T(8,128)(2,1)S(1)}, u32[]{:S(2)}, u32[]{:S(2)}) collective-permute-start(bf16[6,1024]{1,0:T(8,128)(2,1)S(1)} %dynamic-slice_bitcast_fusion.5), channel_id=1, source_target_pairs={{0,8},{8,0},{16,24},{24,16},{32,40},{40,32},{48,56},{56,48},{64,72... | collective-permute-start | bytes 36872 | tf_op jit(solution)/shard_map/ppermute | solution.py:84

commit v5 on v3

v5 whole, which is shorter than its diff:
```python
import jax
import jax.numpy as jnp
from jax import lax
from jax.experimental import pallas as pl
from jax.experimental.pallas import tpu as pltpu
from jax.sharding import Mesh, PartitionSpec as P

X, Z, Y, C = 4, 16, 4, 2
VOCAB_AXES = ("x", "z")
ROW_AXES = ("y", "core")
SWAP = [(0, 1), (1, 0)]
TILE = 256
BF16, F32 = jnp.bfloat16, jnp.float32
IN_VMEM = pl.BlockSpec(memory_space=pltpu.VMEM)
IN_SMEM = pl.BlockSpec(memory_space=pltpu.SMEM)


def call(kernel, out_shape, core_index, rows, head, other):
    moved = sum(a.size * a.dtype.itemsize for a in (rows, head, other, out_shape))
    flops = rows.size * head.shape[0] * 2
    return pl.pallas_call(
        kernel,
        out_shape=out_shape,
        in_specs=[IN_SMEM] + [IN_VMEM] * 3,
        out_specs=IN_VMEM,
        scratch_shapes=[pltpu.VMEM((C, TILE, head.shape[1]), BF16)],
        cost_estimate=pl.CostEstimate(flops=flops, bytes_accessed=moved, transcendentals=0),
        compiler_params=pltpu.CompilerParams(vmem_limit_bytes=8 * 2**20),
    )(core_index, rows, head, other)


def gather_over(block, axis):
    size = lax.axis_size(axis)
    copies = jnp.broadcast_to(block[None], (size,) + block.shape)
    return lax.all_to_all(copies, axis, 0, 0)


def pad_last_rows(tail_ref, head_ref):
    rest = head_ref.shape[0] % TILE
    tail_ref[...] = jnp.zeros_like(tail_ref)
    tail_ref[:rest, :] = head_ref[head_ref.shape[0] - rest :, :]


def logits_kernel(core_ref, rows_ref, head_ref, other_ref, out_ref, tail_ref):
    core = core_ref[0]
    slice_width = rows_ref.shape[-1]
    own = rows_ref[:, pl.ds(core, 1)].reshape(-1, slice_width)
    rest = rows_ref[:, pl.ds(1 - core, 1)].reshape(-1, slice_width)
    pad_last_rows(tail_ref.at[0], head_ref)
    pad_last_rows(tail_ref.at[1], other_ref)

    def dot(rows, part):
        return lax.dot_general(rows, part, (((1,), (1,)), ((), ())), preferred_element_type=F32)

    whole = head_ref.shape[0] // TILE
    for k in range(whole + 1):
        span = pl.ds(k * TILE, TILE)
        part, other = (head_ref[span, :], other_ref[span, :]) if k < whole else (tail_ref[0], tail_ref[1])
        tile = dot(own, part) + dot(rest, other)
        out_ref[:, :, span] = tile.reshape(out_ref.shape[:2] + (TILE,))


def partial_kernel(core_ref, grad_ref, head_ref, other_ref, out_ref, tail_ref):
    core = core_ref[0]
    blocks, _, own, slice_width = out_ref.shape
    whole = head_ref.shape[0] // TILE * TILE
    grad, grad_tail = grad_ref[:, :whole], grad_ref[:, whole:]
    for k, (place, part) in enumerate(((core, head_ref), (1 - core, other_ref))):
        pad_last_rows(tail_ref.at[k], part)
        for first in range(0, slice_width, TILE):
            span = pl.ds(first, TILE)
            tile = jnp.dot(grad, part[:whole, span], preferred_element_type=F32)
            tile = tile + jnp.dot(grad_tail, tail_ref[k, :, span], preferred_element_type=F32)
            out_ref[:, pl.ds(place, 1), :, span] = tile.astype(BF16).reshape(blocks, 1, own, TILE)


def per_device(hidden, head, targets, upstream):
    width, slice_width = head.shape
    token_count = targets.shape[0]
    own = token_count // (Y * C)
    padded = -(-width // TILE) * TILE
    barrier = lax.optimization_barrier

    by_z = gather_over(hidden, "z").reshape(1, C, own, slice_width)
    core = lax.axis_index("core")
    row_first = lax.axis_index(ROW_AXES) * own
    own_target = lax.dynamic_slice_in_dim(targets, row_first, own, 0) - lax.axis_index(VOCAB_AXES) * width
    own_weight = lax.dynamic_slice_in_dim(upstream, row_first, own, 0)
    column = lax.broadcasted_iota(jnp.int32, (own, padded), 1)
    valid = jnp.where(column < width, 1.0, 0.0)
    target_mask = jnp.where(column == own_target[:, None], valid, 0.0)
    head, own_weight, target_mask, valid = barrier((head, own_weight, target_mask, valid))
    head_other = lax.ppermute(head, "core", SWAP)
    by_z, own_weight, target_mask, valid, core = barrier((by_z, own_weight, target_mask, valid, core))
    core_index = core[None]

    copies = jnp.broadcast_to(by_z, (X, C, own, slice_width)).reshape(X * C, own, slice_width)
    both = lax.all_to_all(copies, ("x", "core"), 0, 0).reshape(X, C, own, slice_width)

    out = jax.ShapeDtypeStruct((Y, own, padded), F32)
    chip_logits = call(logits_kernel, out, core_index, both, head, head_other)
    logit_parts = lax.all_to_all(chip_logits, "y", 0, 0)
    logit_parts, own_weight, target_mask, valid, core = barrier((logit_parts, own_weight, target_mask, valid, core))
    logits = jnp.sum(logit_parts, axis=0)

    local_top = jnp.max(jnp.where(valid > 0, logits, -jnp.inf), axis=1)
    local_total = jnp.sum(jnp.where(valid > 0, jnp.exp(logits - local_top[:, None]), 0.0), axis=1)
    local_target = jnp.sum(jnp.where(target_mask > 0, logits, 0.0), axis=1)
    stats = jnp.concatenate([local_top, local_total, local_target])
    stats = gather_over(stats[None], VOCAB_AXES).reshape(X * Z, 3, own)
    stats, logits, own_weight, target_mask, valid = barrier((stats, logits, own_weight, target_mask, valid))
    top = jnp.max(stats[:, 0], axis=0)
    total = jnp.sum(stats[:, 1] * jnp.exp(stats[:, 0] - top), axis=0)
    lse = top + jnp.log(total)
    token_loss = lse - jnp.sum(stats[:, 2], axis=0)
    probability = jnp.where(valid > 0, jnp.exp(logits - lse[:, None]), 0.0)
    grad_rows = ((probability - target_mask) * own_weight[:, None]).astype(BF16)

    grad_rows, token_loss = barrier((grad_rows, token_loss))
    grad_half = gather_over(grad_rows, "y").reshape(Y * own, padded)

    grad_half, core = barrier((grad_half, core))
    out = jax.ShapeDtypeStruct((X, C, own, slice_width), BF16)
    partial = call(partial_kernel, out, core_index, grad_half, head, head_other)
    over_x = lax.all_to_all(partial.reshape(X * C, own, slice_width), ("x", "core"), 0, 0)
    over_x, both, grad_half, core = barrier((over_x, both, grad_half, core))
    over_x = jnp.sum(over_x.reshape(X, C * own, slice_width).astype(F32), axis=0).astype(BF16)
    over_z = lax.all_to_all(over_x.reshape(Z, -1, slice_width), "z", 0, 0)
    grad_hidden = jnp.sum(over_z.astype(F32), axis=0).astype(BF16)

    def head_part(grad, rows):
        return lax.dot_general(grad[:, :width], rows, (((0,), (0,)), ((), ())), preferred_element_type=F32)

    pick = lambda index: lax.dynamic_index_in_dim(both, index, 1, keepdims=False).reshape(-1, slice_width)
    part = head_part(grad_half, pick(core))
    part, grad_half, both = barrier((part, grad_half, both))
    grad_rest = lax.ppermute(grad_half, "core", SWAP)
    hidden_rest = lax.ppermute(pick(1 - core), "core", SWAP)
    grad_head = (part + head_part(grad_rest, hidden_rest)).astype(BF16)
    return token_loss, grad_hidden, grad_head


def solution(mesh):
    torus = Mesh(mesh.devices.reshape(X, Z, Y, C), VOCAB_AXES + ROW_AXES)
    return jax.shard_map(
        per_device,
        mesh=torus,
        in_specs=(P(VOCAB_AXES, ROW_AXES), P(VOCAB_AXES, ROW_AXES), P(), P()),
        out_specs=(P(ROW_AXES), P(VOCAB_AXES, ROW_AXES), P(VOCAB_AXES, ROW_AXES)),
        check_vma=False,
    )
```

time: 167 us -> 170 us (1.018)
  blocking collectives: 48.5 us -> 116 us
  waiting for transfers between devices: 58 us -> 14 us
  starting transfers between devices: 34.2 us -> 11 us
  local copies, waits for them, and re-layouts: 14.3 us -> 5.39 us
  matrix products: 3.11 us -> 7.68 us
  other arithmetic: 4.3 us -> 7.85 us
  Pallas kernels: 3.04 us -> 6.43 us
    all_to_all x3 -> x0, waiting for transfers between devices: 42.5 us -> none  [the longest x1 15.3 us: gather_over(): return lax.all_to_all(copies, axis, 0, 0)]
    all_to_all x0 -> x2, blocking collectives: none -> 34.2 us  [the longest x1 18.3 us: per_device(): logit_parts = lax.all_to_all(chip_logits, 'y', 0, 0)]
    all_to_all x2 -> x3, blocking collectives: 31.1 us -> 64.9 us  [gather_over(): return lax.all_to_all(copies, axis, 0, 0)]
    all_to_all x3 -> x0, starting transfers between devices: 23.2 us -> none  [the longest x1 15.2 us: gather_over(): return lax.all_to_all(copies, axis, 0, 0)]
    unnamed x10 -> x6, local copies, waits for them, and re-layouts: 5.96 us -> 0.89 us
    dot_general x2, matrix products: 3.11 us -> 7.68 us  [head_part(): lax.dot_general(grad[:, :width], rows, (((0,), (0,)), ((), ())), preferre...]
    pad x2 -> x0, local copies, waits for them, and re-layouts: 3.88 us -> none  [per_device(): pad = lambda a: jnp.pad(a, ((0, padded - width), (0, 0)))]
    pallas_call x2, Pallas kernels: 3.04 us -> 6.43 us  [call(): pl.pallas_call(kernel, out_shape=out_shape, in_specs=[IN_SMEM] + [IN_VMEM...]
  transfers between devices with their start and end apart: 7 -> 4, of which waited for: 4 -> 1; matrix products, arithmetic and copies ran while one was open for 6% -> 4% of each run, Pallas kernels for 0% -> 0%
where the time goes in v5:
time: 170 us
  blocking collectives  116 us (68%)
  waiting for transfers between devices  14 us (8%)
  starting transfers between devices  11 us (6%)
  other arithmetic  7.85 us (5%)
  matrix products  7.68 us (5%)
  Pallas kernels  6.43 us (4%)
  local copies, waits for them, and re-layouts  5.39 us (3%)
    all_to_all x3, blocking collectives, gather_over(): return lax.all_to_all(copies, axis, 0, 0)  64.9 us
    all_to_all x1, blocking collectives, per_device(): logit_parts = lax.all_to_all(chip_logits, 'y', 0, 0)  18.3 us
    all_to_all x1, blocking collectives, per_device(): lax.all_to_all(copies, ('x', 'core'), 0, 0).reshape(X, C, own, slice_width)  17.3 us
    all_to_all x1, blocking collectives, per_device(): lax.all_to_all(partial.reshape(X * C, own, slice_width), ('x', 'core'), 0...  15.9 us
    all_to_all x1, waiting for transfers between devices, per_device(): over_z = lax.all_to_all(over_x.reshape(Z, -1, slice_width), 'z', 0, 0)  14 us
    dot_general x2, matrix products, head_part(): lax.dot_general(grad[:, :width], rows, (((0,), (0,)), ((), ())), preferre...  7.68 us
    pallas_call x2, Pallas kernels, call(): pl.pallas_call(kernel, out_shape=out_shape, in_specs=[IN_SMEM] + [IN_VMEM...  6.43 us
    all_to_all x1, starting transfers between devices, per_device(): over_z = lax.all_to_all(over_x.reshape(Z, -1, slice_width), 'z', 0, 0)  4.79 us
  transfers between devices with their start and end apart: 4, of which 1 were waited for; matrix products, arithmetic and copies ran while one was open for 4% of the time, Pallas kernels for 0%

profile of v5, /device:TPU:32, one launch (start us, length us, event | category | flops | bytes accessed | tf_op | source)
XLA Modules:
  0.0 169.6 jit_solution(5480669349779036060)
XLA Ops:
  0.6 0.0 copy-start
  0.7 0.9 dynamic_slice.13
  1.6 0.8 dynamic-slice_subtract_fusion
  2.3 0.8 fusion.3
  3.1 0.7 iota.15
  3.8 1.9 %collective-permute-start = (bf16[1188,1024]{1,0:T(8,128)(2,1)}, bf16[1188,1024]{1,0:T(8,128)(2,1)}, u32[]{:S(2)}, u32[]{:S(2)}) collective-permute-start(bf16[1188,1024]{1,0:T(8,128)(2,1)} %head_ref.1), channel_id=1, source_target_pairs={{0,1},{1,0},{2,3},{3,2},{4,5},{5,4},{6,7},{7,6},{8,9},{9,8},{10,11... | collective-permute-start | bytes 7299080 | tf_op jit(solution)/shard_map/ppermute | solution.py:93
  5.7 0.7 broadcast_in_dim.51
  6.5 33.8 %all_to_all.35 = bf16[16,6,1024]{2,1,0:T(8,128)(2,1)S(1)} all-to-all(bf16[16,6,1024]{2,1,0:T(8,128)(2,1)S(1)} %broadcast_in_dim.51), channel_id=1, replica_groups=mesh['x'=4,'z'=16,'y'=4,'core'=2] {'z'}, dimensions={0} | all-to-all | bytes 393216 | tf_op jit(solution)/shard_map/all_to_all | solution.py:35
  40.2 0.1 reshape.53
  40.3 0.1 broadcast_in_dim.57
  40.4 17.3 %all_to_all.36 = bf16[8,48,1024]{2,1,0:T(8,128)(2,1)S(1)} all-to-all(bf16[8,48,1024]{2,1,0:T(8,128)(2,1)S(1)} %bitcast.32), channel_id=1, replica_groups=mesh['x'=4,'z'=16,'y'=4,'core'=2] {'x','core'}, dimensions={0} | all-to-all | bytes 1572864 | tf_op jit(solution)/shard_map/all_to_all | solution.py:98
  57.8 0.0 collective-permute-done.other_ref
  57.8 0.0 copy-done
  57.8 3.5 %shard_map.67 = f32[4,48,1280]{2,1,0:T(8,128)S(1)} custom-call(s32[1]{0:T(128)} %bitcast.core_ref, bf16[4,2,48,1024]{3,2,1,0:T(8,128)(2,1)S(1)} %bitcast.27, bf16[1188,1024]{1,0:T(8,128)(2,1)S(1)} %copy-done, bf16[1188,1024]{1,0:T(8,128)(2,1)} %collective-permute-done.other_ref), custom_call_target="tpu_custom_call" | custom-call | flops 934281216 | bytes 6635520 | tf_op jit(solution)/shard_map/pallas_call | solution.py:21
  61.3 0.0 copy-start.1
  61.3 0.9 copy-done.1
  62.2 18.3 %all_to_all.37 = f32[4,48,1280]{2,1,0:T(8,128)S(1)} all-to-all(f32[4,48,1280]{2,1,0:T(8,128)S(1)} %shard_map.67), channel_id=1, replica_groups=mesh['x'=4,'z'=16,'y'=4,'core'=2] {'y'}, dimensions={0} | all-to-all | bytes 1966080 | tf_op jit(solution)/shard_map/all_to_all | solution.py:102
  80.5 0.8 reduce_sum.69
  81.2 1.2 select_reduce_fusion.2
  82.5 1.3 select_reduce_fusion.1
  83.8 0.1 pad_maximum_fusion
  83.9 20.8 %all_to_all.38 = f32[64,1,144]{2,1,0:T(1,128)S(1)} all-to-all(f32[64,1,144]{2,1,0:T(1,128)S(1)} %broadcast_in_dim.59), channel_id=1, replica_groups=mesh['x'=4,'z'=16,'y'=4,'core'=2] {'x','z'}, dimensions={0} | all-to-all | bytes 73728 | tf_op jit(solution)/shard_map/all_to_all | solution.py:35
  104.7 0.1 copy.8
  104.8 0.1 slice_reduce_fusion
  104.9 0.2 fusion.6
  105.1 0.5 fusion.8
  105.7 1.3 multiply_convert_fusion
  107.0 10.3 %all_to_all.39 = bf16[4,48,1280]{2,1,0:T(8,128)(2,1)S(1)} all-to-all(bf16[4,48,1280]{2,1,0:T(8,128)(2,1)S(1)} %broadcast_in_dim.60), channel_id=1, replica_groups=mesh['x'=4,'z'=16,'y'=4,'core'=2] {'y'}, dimensions={0} | all-to-all | bytes 983040 | tf_op jit(solution)/shard_map/all_to_all | solution.py:35
  117.3 2.9 %shard_map.68 = bf16[4,2,48,1024]{3,2,1,0:T(8,128)(2,1)S(1)} custom-call(s32[1]{0:T(128)} %bitcast.core_ref, bf16[192,1280]{1,0:T(8,128)(2,1)S(1)} %bitcast.24, bf16[1188,1024]{1,0:T(8,128)(2,1)S(1)} %copy-done, bf16[1188,1024]{1,0:T(8,128)(2,1)} %collective-permute-done.other_ref), custom_call_target="tpu_custom_call" | custom-call | flops 583925760 | bytes 6144000 | tf_op jit(solution)/shard_map/pallas_call | solution.py:21
  120.2 15.9 %all_to_all.40 = bf16[8,48,1024]{2,1,0:T(8,128)(2,1)S(1)} all-to-all(bf16[8,48,1024]{2,1,0:T(8,128)(2,1)S(1)} %bitcast.30), channel_id=1, replica_groups=mesh['x'=4,'z'=16,'y'=4,'core'=2] {'x','core'}, dimensions={0} | all-to-all | bytes 1572864 | tf_op jit(solution)/shard_map/all_to_all | solution.py:125
  136.1 1.0 constant_dynamic-slice_fusion.1
  137.1 0.0 copy-start.2
  137.2 3.0 %fusion.1 = f32[1188,1024]{1,0:T(8,128)} fusion(bf16[192,1024]{1,0:T(8,128)(2,1)S(1)} %bitcast.33, bf16[192,1280]{1,0:T(8,128)(2,1)S(1)} %bitcast.25), kind=kOutput, calls=%fused_computation.3 | convolution fusion | flops 467140608 | bytes 5750784 | tf_op jit(solution)/shard_map/dot_general | solution.py:132
  140.2 1.9 %collective-permute-start.1 = (bf16[192,1280]{1,0:T(8,128)(2,1)S(1)}, bf16[192,1280]{1,0:T(8,128)(2,1)S(1)}, u32[]{:S(2)}, u32[]{:S(2)}) collective-permute-start(bf16[192,1280]{1,0:T(8,128)(2,1)S(1)} %bitcast.26), channel_id=1, source_target_pairs={{0,1},{1,0},{2,3},{3,2},{4,5},{5,4},{6,7},{7,6},{8,9},{9,8},{10,11... | collective-permute-start | bytes 1474568 | tf_op jit(solution)/shard_map/ppermute | solution.py:137
  142.1 0.0 copy-done.2
  142.1 2.4 %collective-permute-start.2 = (bf16[192,1024]{1,0:T(8,128)(2,1)S(1)}, bf16[192,1024]{1,0:T(8,128)(2,1)S(1)}, u32[]{:S(2)}, u32[]{:S(2)}) collective-permute-start(bf16[192,1024]{1,0:T(8,128)(2,1)S(1)} %bitcast.37), channel_id=1, source_target_pairs={{0,1},{1,0},{2,3},{3,2},{4,5},{5,4},{6,7},{7,6},{8,9},{9,8},{10,11... | collective-permute-start | bytes 1179656 | tf_op jit(solution)/shard_map/ppermute | solution.py:138
  144.6 0.1 bitcast_reduce_fusion
  144.7 0.8 reshape.60
  145.5 4.8 %all-to-all-start.6 = ((bf16[16,6,1024]{2,1,0:T(8,128)(2,1)}), bf16[16,6,1024]{2,1,0:T(8,128)(2,1)S(1)}, u32[]{:S(2)}, u32[]{:S(2)}) async-start(bf16[16,6,1024]{2,1,0:T(8,128)(2,1)} %reshape.60), calls=%async_computation.6 | async-start | bytes 524288 | tf_op jit(solution)/shard_map/all_to_all | solution.py:128
  150.2 0.0 collective-permute-done.2
  150.3 0.0 collective-permute-done.1
  150.3 4.7 %add_convert_fusion = bf16[1188,1024]{1,0:T(8,128)(2,1)} fusion(f32[1188,1024]{1,0:T(8,128)} %fusion.1, bf16[192,1024]{1,0:T(8,128)(2,1)S(1)} %collective-permute-done.2, bf16[192,1280]{1,0:T(8,128)(2,1)S(1)} %collective-permute-done.1), kind=kOutput, calls=%fused_computation | convolution fusion | flops 469573632 | bytes 8183808 | tf_op jit(solution)/shard_map/dot_general | solution.py:132
  154.9 14.0 %all-to-all-done.6 = bf16[16,6,1024]{2,1,0:T(8,128)(2,1)S(1)} async-done(((bf16[16,6,1024]{2,1,0:T(8,128)(2,1)}), bf16[16,6,1024]{2,1,0:T(8,128)(2,1)S(1)}, u32[]{:S(2)}, u32[]{:S(2)}) %all-to-all-start.6) | async-done | bytes 196640 | tf_op jit(solution)/shard_map/all_to_all | solution.py:128
  168.9 0.7 reduce_sum.75
  (4 shorter events, 0.1 us)
Async XLA Ops:
  0.6 57.1 %copy-start = (bf16[1188,1024]{1,0:T(8,128)(2,1)S(1)}, bf16[1188,1024]{1,0:T(8,128)(2,1)}, u32[]{:S(2)}) copy-start(bf16[1188,1024]{1,0:T(8,128)(2,1)} %head_ref.1) | copy-start | bytes 7299076
  3.8 53.9 %collective-permute-start = (bf16[1188,1024]{1,0:T(8,128)(2,1)}, bf16[1188,1024]{1,0:T(8,128)(2,1)}, u32[]{:S(2)}, u32[]{:S(2)}) collective-permute-start(bf16[1188,1024]{1,0:T(8,128)(2,1)} %head_ref.1), channel_id=1, source_target_pairs={{0,1},{1,0},{2,3},{3,2},{4,5},{5,4},{6,7},{7,6},{8,9},{9,8},{10,11... | collective-permute-start | bytes 7299080 | tf_op jit(solution)/shard_map/ppermute | solution.py:93
  61.3 0.9 copy-start.1
  137.1 4.9 %copy-start.2 = (bf16[8,48,1024]{2,1,0:T(8,128)(2,1)S(1)}, bf16[8,48,1024]{2,1,0:T(8,128)(2,1)}, u32[]{:S(2)}) copy-start(bf16[8,48,1024]{2,1,0:T(8,128)(2,1)} %copy-done.1) | copy-start | bytes 2359300
  140.2 10.1 %collective-permute-start.1 = (bf16[192,1280]{1,0:T(8,128)(2,1)S(1)}, bf16[192,1280]{1,0:T(8,128)(2,1)S(1)}, u32[]{:S(2)}, u32[]{:S(2)}) collective-permute-start(bf16[192,1280]{1,0:T(8,128)(2,1)S(1)} %bitcast.26), channel_id=1, source_target_pairs={{0,1},{1,0},{2,3},{3,2},{4,5},{5,4},{6,7},{7,6},{8,9},{9,8},{10,11... | collective-permute-start | bytes 1474568 | tf_op jit(solution)/shard_map/ppermute | solution.py:137
  142.1 8.1 %collective-permute-start.2 = (bf16[192,1024]{1,0:T(8,128)(2,1)S(1)}, bf16[192,1024]{1,0:T(8,128)(2,1)S(1)}, u32[]{:S(2)}, u32[]{:S(2)}) collective-permute-start(bf16[192,1024]{1,0:T(8,128)(2,1)S(1)} %bitcast.37), channel_id=1, source_target_pairs={{0,1},{1,0},{2,3},{3,2},{4,5},{5,4},{6,7},{7,6},{8,9},{9,8},{10,11... | collective-permute-start | bytes 1179656 | tf_op jit(solution)/shard_map/ppermute | solution.py:138
  145.5 23.4 %all-to-all-start.6 = ((bf16[16,6,1024]{2,1,0:T(8,128)(2,1)}), bf16[16,6,1024]{2,1,0:T(8,128)(2,1)S(1)}, u32[]{:S(2)}, u32[]{:S(2)}) async-start(bf16[16,6,1024]{2,1,0:T(8,128)(2,1)} %reshape.60), calls=%async_computation.6 | async-start | bytes 524288 | tf_op jit(solution)/shard_map/all_to_all | solution.py:128

commit v6 on v1

v6 whole, which is shorter than its diff:
```python
import functools

import jax
import jax.numpy as jnp
from jax import lax
from jax.experimental import pallas as pl
from jax.experimental.pallas import tpu as pltpu
from jax.sharding import Mesh, PartitionSpec as P

X, Z, Y, C = 4, 16, 4, 2
VOCAB_AXES = ("x", "z")
ROW_AXES = ("y", "core")
SWAP = [(0, 1), (1, 0)]
LANES = 128
TILE = 256
BF16, F32 = jnp.bfloat16, jnp.float32
IN_VMEM = pl.BlockSpec(memory_space=pltpu.VMEM)
IN_SMEM = pl.BlockSpec(memory_space=pltpu.SMEM)


def call(kernel, out_shape, place, *operands, aliases=None):
    many = isinstance(out_shape, list)
    moved = sum(a.size * a.dtype.itemsize for a in operands)
    return pl.pallas_call(
        kernel,
        out_shape=out_shape,
        in_specs=[IN_SMEM] + [IN_VMEM] * len(operands),
        out_specs=[IN_VMEM] * len(out_shape) if many else IN_VMEM,
        input_output_aliases=aliases or {},
        cost_estimate=pl.CostEstimate(flops=moved, bytes_accessed=moved, transcendentals=0),
        compiler_params=pltpu.CompilerParams(vmem_limit_bytes=8 * 2**20),
    )(place, *operands)


def gather_over(block, axis):
    size = lax.axis_size(axis)
    copies = jnp.broadcast_to(block[None], (size,) + block.shape)
    return lax.all_to_all(copies, axis, 0, 0)


def to_lanes(column):
    shape = (column.shape[0], LANES)
    row, lane = (lax.broadcasted_iota(jnp.int32, shape, axis) for axis in (0, 1))
    return jnp.sum(jnp.where(row == lane, column, 0.0), axis=0, keepdims=True)


def to_column(lanes, rows, first=0):
    shape = (rows, lanes.shape[1])
    row, lane = (lax.broadcasted_iota(jnp.int32, shape, axis) for axis in (0, 1))
    return jnp.sum(jnp.where(row + first == lane, lanes, jnp.zeros_like(lanes)), axis=1, keepdims=True)


def target_mask(place_ref, targets_ref, shape):
    column = to_column(targets_ref[...], shape[0], place_ref[1]) - place_ref[2]
    return lax.broadcasted_iota(jnp.int32, shape, 1) == column


def spans(length):
    return [pl.ds(first, min(TILE, length - first)) for first in range(0, length, TILE)]


def logits_kernel(shift, place_ref, rows_ref, head_ref, out_ref):
    half = pl.ds(lax.rem(place_ref[0] + shift, C), 1)
    rows = rows_ref[:, half].reshape(-1, rows_ref.shape[-1])
    for span in spans(head_ref.shape[0]):
        tile = lax.dot_general(rows, head_ref[span, :], (((1,), (1,)), ((), ())), preferred_element_type=F32)
        out_ref[:, :, span] = tile.reshape(out_ref.shape[:2] + (span.size,))


def add_kernel(place_ref, a_ref, b_ref, out_ref):
    out_ref[...] = a_ref[...] + b_ref[...]


def partial_kernel(half, place_ref, grad_ref, head_ref, *refs):
    out_ref = refs[-1]
    blocks, _, own, slice_width = out_ref.shape
    grad = grad_ref[...].reshape(blocks * own, -1)
    for span in spans(slice_width):
        tile = jnp.dot(grad, head_ref[:, span], preferred_element_type=F32).astype(BF16)
        out_ref[:, half, :, span] = tile.reshape(blocks, own, span.size)


def statistics_kernel(place_ref, parts_ref, targets_ref, logits_ref, stats_ref):
    logits = parts_ref[0]
    for y in range(1, Y):
        logits = logits + parts_ref[y]
    logits_ref[...] = logits
    top = jnp.max(logits, axis=1, keepdims=True)
    total = jnp.sum(jnp.exp(logits - top), axis=1, keepdims=True)
    mask = target_mask(place_ref, targets_ref, logits.shape)
    target_logit = jnp.sum(jnp.where(mask, logits, 0.0), axis=1, keepdims=True)
    row = jnp.concatenate([to_lanes(a) for a in (top, total, target_logit)], axis=1)
    stats_ref[...] = jnp.broadcast_to(row[None], stats_ref.shape)


def softmax_kernel(place_ref, stats_ref, logits_ref, targets_ref, upstream_ref, loss_ref, grad_ref):
    logits = logits_ref[...]
    rows = logits.shape[0]
    stats = stats_ref[:, 0, :]
    tops, totals, target_logits = (stats[:, k * LANES : (k + 1) * LANES] for k in range(3))
    top = jnp.max(tops, axis=0, keepdims=True)
    total = jnp.sum(totals * jnp.exp(tops - top), axis=0, keepdims=True)
    used = lax.broadcasted_iota(jnp.int32, top.shape, 1) < rows
    lse = top + jnp.log(jnp.where(used, total, 1.0))
    loss = lse - jnp.sum(target_logits, axis=0, keepdims=True)
    loss_ref[...] = loss[:, :rows]
    weight = to_column(upstream_ref[...], rows, place_ref[1])
    mask = target_mask(place_ref, targets_ref, logits.shape)
    probability = jnp.exp(logits - to_column(lse, rows))
    grad = ((probability - jnp.where(mask, 1.0, 0.0)) * weight).astype(BF16)
    grad_ref[...] = jnp.broadcast_to(grad[None], grad_ref.shape)


def over_x_kernel(place_ref, parts_ref, out_ref):
    core = place_ref[0]
    blocks, block, _ = out_ref.shape
    per_half = blocks // C
    for half in range(C):
        where = pl.ds(lax.rem(core + half, C), 1)
        rows = parts_ref[0, where][0].astype(F32)
        for x in range(1, X):
            rows = rows + parts_ref[x, where][0].astype(F32)
        for k in range(per_half):
            out_ref[half * per_half + k] = rows[k * block : (k + 1) * block].astype(BF16)


def per_device(hidden, head, targets, upstream):
    width, slice_width = head.shape
    token_count = targets.shape[0]
    own = token_count // (Y * C)
    barrier = lax.optimization_barrier

    core = lax.axis_index("core")
    row_first = lax.axis_index(ROW_AXES) * own
    first_column = lax.axis_index(VOCAB_AXES) * width
    hidden, core, row_first, first_column = barrier((hidden, core, row_first, first_column))
    by_z = gather_over(hidden, "z").reshape(-1, slice_width)
    by_x = gather_over(by_z, "x").reshape(Y, C, own, slice_width)

    by_x, targets, upstream, core, row_first, first_column = barrier(
        (by_x, targets, upstream, core, row_first, first_column)
    )
    place = jnp.stack([core, row_first, first_column])
    out = jax.ShapeDtypeStruct((Y, own, width), F32)
    sibling_logits = call(functools.partial(logits_kernel, 1), out, place, by_x, head)
    from_core = lax.ppermute(sibling_logits, "core", SWAP)
    sibling_logits, targets, upstream, by_x = barrier((sibling_logits, targets, upstream, by_x))
    own_logits = call(functools.partial(logits_kernel, 0), out, place, by_x, head)
    chip_logits = call(add_kernel, out, place, own_logits, from_core)
    chip_logits, targets, upstream = barrier((chip_logits, targets[None], upstream[None]))
    parts = lax.all_to_all(chip_logits, "y", 0, 0)

    out = [jax.ShapeDtypeStruct((own, width), F32), jax.ShapeDtypeStruct((X * Z, 1, 3 * LANES), F32)]
    logits, stats = call(statistics_kernel, out, place, parts, targets)
    stats = lax.all_to_all(stats, VOCAB_AXES, 0, 0)
    out = [jax.ShapeDtypeStruct((1, own), F32), jax.ShapeDtypeStruct((Y, own, width), BF16)]
    token_loss, grad_rows = call(softmax_kernel, out, place, stats, logits, targets, upstream)

    grad_own = lax.all_to_all(grad_rows, "y", 0, 0)
    grad_other = lax.ppermute(grad_own, "core", SWAP)

    out = jax.ShapeDtypeStruct((X, C, own, slice_width), BF16)
    partial = call(functools.partial(partial_kernel, 0), out, place, grad_own, head)
    partial = call(functools.partial(partial_kernel, 1), out, place, grad_other, head, partial, aliases={3: 0})
    over_x = lax.all_to_all(partial, "x", 0, 0)
    over_x, place, by_x, core, grad_own, grad_other = barrier((over_x, place, by_x, core, grad_own, grad_other))
    out = jax.ShapeDtypeStruct((Z, token_count // (X * Z), slice_width), BF16)
    over_x = call(over_x_kernel, out, place, over_x)
    over_z = lax.all_to_all(over_x, "z", 0, 0)
    grad_hidden = jnp.sum(over_z.astype(F32), axis=0).astype(BF16)

    def head_part(grad, half):
        rows = lax.dynamic_index_in_dim(by_x, half, 1, keepdims=False).reshape(-1, slice_width)
        grad = grad.reshape(-1, width)
        return lax.dot_general(grad, rows, (((0,), (0,)), ((), ())), preferred_element_type=F32)

    grad_head = (head_part(grad_own, core) + head_part(grad_other, 1 - core)).astype(BF16)
    return token_loss[0], grad_hidden, grad_head


def solution(mesh):
    torus = Mesh(mesh.devices.reshape(X, Z, Y, C), VOCAB_AXES + ROW_AXES)
    return jax.shard_map(
        per_device,
        mesh=torus,
        in_specs=(P(VOCAB_AXES, ROW_AXES), P(VOCAB_AXES, ROW_AXES), P(), P()),
        out_specs=(P(ROW_AXES), P(VOCAB_AXES, ROW_AXES), P(VOCAB_AXES, ROW_AXES)),
        check_vma=False,
    )
```

time: 169 us -> 156 us (0.923)
  blocking collectives: 43.2 us -> 115 us
  waiting for transfers between devices: 69.9 us -> 15.3 us
  starting transfers between devices: 30.2 us -> 8.3 us
  Pallas kernels: 0 us -> 9.44 us
  other arithmetic: 9.55 us -> 0.74 us
  local copies, waits for them, and re-layouts: 7.13 us -> 1.12 us
  matrix products: 7.35 us -> 4.21 us
    all_to_all x0 -> x4, blocking collectives: none -> 66.9 us  [the longest x1 22.1 us: per_device(): stats = lax.all_to_all(stats, VOCAB_AXES, 0, 0)]
    all_to_all x4 -> x0, waiting for transfers between devices: 51.4 us -> none  [the longest x2 24.5 us: gather_over(): return lax.all_to_all(copies, axis, 0, 0)]
    all_to_all x4 -> x0, starting transfers between devices: 21.1 us -> none  [the longest x2 12.5 us: gather_over(): return lax.all_to_all(copies, axis, 0, 0)]
    pallas_call x0 -> x8, Pallas kernels: none -> 9.44 us  [call(): pl.pallas_call(kernel, out_shape=out_shape, in_specs=[IN_SMEM] + [IN_VMEM...]
    all_to_all x2, blocking collectives: 43.2 us -> 48.5 us  [gather_over(): return lax.all_to_all(copies, axis, 0, 0)]
    reduce_sum x6 -> x1, other arithmetic: 5.13 us -> 0.67 us  [per_device(): grad_hidden = jnp.sum(over_z.astype(F32), axis=0).astype(BF16)]
    dot_general x4 -> x0, matrix products: 4.24 us -> none  [the longest x2 2.85 us: logits_of(): lax.dot_general(rows, head, (((1,), (1,)), ((), ())), preferred_element_t...]
    reshape x1 -> x0, local copies, waits for them, and re-layouts: 1.69 us -> none  [per_device(): jnp.where(core == 0, over_x, over_x[::-1]).reshape(Z, -1, slice_width)]
  transfers between devices with their start and end apart: 7 -> 3, of which waited for: 7 -> 3; matrix products, arithmetic and copies ran while one was open for 3% -> 3% of each run, Pallas kernels for 0% -> 2%
where the time goes in v6:
time: 156 us; the launch traced here: 155 us
  blocking collectives  115 us (74%)
  waiting for transfers between devices  15.3 us (10%)
  Pallas kernels  9.44 us (6%)
  starting transfers between devices  8.3 us (5%)
  matrix products  4.21 us (3%)
    all_to_all x2, blocking collectives, gather_over(): return lax.all_to_all(copies, axis, 0, 0)  48.5 us
    all_to_all x1, blocking collectives, per_device(): stats = lax.all_to_all(stats, VOCAB_AXES, 0, 0)  22.1 us
    all_to_all x1, blocking collectives, per_device(): parts = lax.all_to_all(chip_logits, 'y', 0, 0)  19 us
    all_to_all x1, blocking collectives, per_device(): over_x = lax.all_to_all(partial, 'x', 0, 0)  15.6 us
    all_to_all x1, waiting for transfers between devices, per_device(): over_z = lax.all_to_all(over_x, 'z', 0, 0)  13.7 us
    all_to_all x1, blocking collectives, per_device(): grad_own = lax.all_to_all(grad_rows, 'y', 0, 0)  10.3 us
    pallas_call x8, Pallas kernels, call(): pl.pallas_call(kernel, out_shape=out_shape, in_specs=[IN_SMEM] + [IN_VMEM...  9.44 us
    all_to_all x1, starting transfers between devices, per_device(): over_z = lax.all_to_all(over_x, 'z', 0, 0)  4.47 us
  transfers between devices with their start and end apart: 3, of which 3 were waited for; matrix products, arithmetic and copies ran while one was open for 3% of the time, Pallas kernels for 2%

profile of v6, /device:TPU:32, one launch (start us, length us, event | category | flops | bytes accessed | tf_op | source)
XLA Modules:
  0.0 155.3 jit_solution(8842831182405847674)
XLA Ops:
  0.6 0.0 copy-start.5
  0.6 0.0 copy-start.4
  0.7 0.0 copy-start
  0.7 0.9 broadcast_in_dim.19
  1.6 32.9 %all_to_all.35 = bf16[16,6,1024]{2,1,0:T(8,128)(2,1)S(1)} all-to-all(bf16[16,6,1024]{2,1,0:T(8,128)(2,1)S(1)} %broadcast_in_dim.19), channel_id=1, replica_groups=mesh['x'=4,'z'=16,'y'=4,'core'=2] {'z'}, dimensions={0} | all-to-all | bytes 393216 | tf_op jit(solution)/shard_map/all_to_all | solution.py:38
  34.5 0.1 broadcast_in_dim.20
  34.6 0.1 broadcast_in_dim.21
  34.6 15.5 %all_to_all.36 = bf16[4,96,1024]{2,1,0:T(8,128)(2,1)S(1)} all-to-all(bf16[4,96,1024]{2,1,0:T(8,128)(2,1)S(1)} %broadcast_in_dim.21), channel_id=1, replica_groups=mesh['x'=4,'z'=16,'y'=4,'core'=2] {'x'}, dimensions={0} | all-to-all | bytes 1572864 | tf_op jit(solution)/shard_map/all_to_all | solution.py:38
  50.2 0.1 pad_add_fusion.place_ref
  50.3 0.0 copy-done
  50.3 1.5 shard_map.67
  51.8 1.9 %collective-permute-start = (f32[4,48,1188]{2,1,0:T(8,128)S(1)}, f32[4,48,1188]{2,1,0:T(8,128)S(1)}, u32[]{:S(2)}, u32[]{:S(2)}) collective-permute-start(f32[4,48,1188]{2,1,0:T(8,128)S(1)} %shard_map.67), channel_id=1, source_target_pairs={{0,1},{1,0},{2,3},{3,2},{4,5},{5,4},{6,7},{7,6},{8,9},{9,8},{10,11... | collective-permute-start | bytes 2737160 | tf_op jit(solution)/shard_map/ppermute | solution.py:146
  53.7 0.0 copy-done.4
  53.7 0.0 copy-done.5
  53.7 1.5 shard_map.68.a_ref
  55.2 1.0 collective-permute-done.b_ref
  56.2 0.7 shard_map.69
  56.9 19.0 %all_to_all.37.parts_ref = f32[4,48,1188]{2,1,0:T(8,128)S(1)} all-to-all(f32[4,48,1188]{2,1,0:T(8,128)S(1)} %shard_map.69), channel_id=1, replica_groups=mesh['x'=4,'z'=16,'y'=4,'core'=2] {'y'}, dimensions={0} | all-to-all | bytes 1824768 | tf_op jit(solution)/shard_map/all_to_all | solution.py:151
  75.8 0.8 shard_map.70
  76.7 22.1 %all_to_all.38.stats_ref = f32[64,1,384]{2,1,0:T(1,128)S(1)} all-to-all(f32[64,1,384]{2,1,0:T(1,128)S(1)} %get-tuple-element.44), channel_id=1, replica_groups=mesh['x'=4,'z'=16,'y'=4,'core'=2] {'x','z'}, dimensions={0} | all-to-all | bytes 196608 | tf_op jit(solution)/shard_map/all_to_all | solution.py:155
  98.8 1.1 shard_map.71
  99.9 10.3 %all_to_all.39.grad_ref = bf16[4,48,1188]{2,1,0:T(8,128)(2,1)S(1)} all-to-all(bf16[4,48,1188]{2,1,0:T(8,128)(2,1)S(1)} %get-tuple-element.48), channel_id=1, replica_groups=mesh['x'=4,'z'=16,'y'=4,'core'=2] {'y'}, dimensions={0} | all-to-all | bytes 912384 | tf_op jit(solution)/shard_map/all_to_all | solution.py:159
  110.2 0.0 copy-start.1
  110.2 1.9 %collective-permute-start.1 = (bf16[4,48,1188]{2,1,0:T(8,128)(2,1)S(1)}, bf16[4,48,1188]{2,1,0:T(8,128)(2,1)S(1)}, u32[]{:S(2)}, u32[]{:S(2)}) collective-permute-start(bf16[4,48,1188]{2,1,0:T(8,128)(2,1)S(1)} %all_to_all.39.grad_ref), channel_id=1, source_target_pairs={{0,1},{1,0},{2,3},{3,2},{4,5},{5,4},{6,7},{7,6},{8,9},{9,8},{10,11... | collective-permute-start | bytes 1368584 | tf_op jit(solution)/shard_map/ppermute | solution.py:160
  112.1 1.2 shard_map.72.refs_0_
  113.4 0.6 collective-permute-done.1.grad_ref
  114.0 0.0 copy-start.3
  114.0 1.2 shard_map.73
  115.2 0.0 copy-done.1
  115.2 0.0 copy-done.3
  115.2 15.6 %all_to_all.40.parts_ref = bf16[4,2,48,1024]{3,2,1,0:T(8,128)(2,1)S(1)} all-to-all(bf16[4,2,48,1024]{3,2,1,0:T(8,128)(2,1)S(1)} %shard_map.73), channel_id=1, replica_groups=mesh['x'=4,'z'=16,'y'=4,'core'=2] {'x'}, dimensions={0} | all-to-all | bytes 1572864 | tf_op jit(solution)/shard_map/all_to_all | solution.py:165
  130.8 1.4 shard_map.74
  132.2 4.5 %all-to-all-start.6 = ((bf16[16,6,1024]{2,1,0:T(8,128)(2,1)}), bf16[16,6,1024]{2,1,0:T(8,128)(2,1)S(1)}, u32[]{:S(2)}, u32[]{:S(2)}) async-start(bf16[16,6,1024]{2,1,0:T(8,128)(2,1)} %shard_map.74), calls=%async_computation.6 | async-start | bytes 524288 | tf_op jit(solution)/shard_map/all_to_all | solution.py:169
  136.7 0.1 constant_dynamic-slice_fusion.1
  136.7 0.0 copy-start.2
  136.7 1.9 %fusion = f32[1188,1024]{1,0:T(8,128)S(1)} fusion(bf16[192,1188]{1,0:T(8,128)(2,1)} %bitcast.17, bf16[192,1024]{1,0:T(8,128)(2,1)S(1)} %bitcast.19), kind=kOutput, calls=%fused_computation.4 | convolution fusion | flops 467140608 | bytes 5715456 | tf_op jit(solution)/shard_map/dot_general | solution.py:175
  138.6 0.0 copy-done.2
  138.7 2.3 %add_convert_fusion = bf16[1188,1024]{1,0:T(8,128)(2,1)} fusion(f32[1188,1024]{1,0:T(8,128)S(1)} %fusion, bf16[192,1188]{1,0:T(8,128)(2,1)S(1)} %bitcast.16, bf16[192,1024]{1,0:T(8,128)(2,1)S(1)} %bitcast.18), kind=kOutput, calls=%fused_computation | convolution fusion | flops 469573632 | bytes 8148480 | tf_op jit(solution)/shard_map/dot_general | solution.py:175
  140.9 13.7 %all-to-all-done.6 = bf16[16,6,1024]{2,1,0:T(8,128)(2,1)S(1)} async-done(((bf16[16,6,1024]{2,1,0:T(8,128)(2,1)}), bf16[16,6,1024]{2,1,0:T(8,128)(2,1)S(1)}, u32[]{:S(2)}, u32[]{:S(2)}) %all-to-all-start.6) | async-done | bytes 196640 | tf_op jit(solution)/shard_map/all_to_all | solution.py:169
  154.6 0.7 reduce_sum.12
  (2 shorter events, 0.0 us)
Async XLA Ops:
  0.6 53.1 %copy-start.5 = (f32[384]{0:T(512)S(1)}, f32[384]{0:T(512)}, u32[]{:S(2)}) copy-start(f32[384]{0:T(512)} %param.7) | copy-start | bytes 4612
  0.6 53.0 %copy-start.4 = (s32[384]{0:T(512)S(1)}, s32[384]{0:T(512)}, u32[]{:S(2)}) copy-start(s32[384]{0:T(512)} %param.6) | copy-start | bytes 4612
  0.7 49.6 %copy-start = (bf16[1188,1024]{1,0:T(8,128)(2,1)S(1)}, bf16[1188,1024]{1,0:T(8,128)(2,1)}, u32[]{:S(2)}) copy-start(bf16[1188,1024]{1,0:T(8,128)(2,1)} %head_ref.7) | copy-start | bytes 7299076
  51.8 4.5 %collective-permute-start = (f32[4,48,1188]{2,1,0:T(8,128)S(1)}, f32[4,48,1188]{2,1,0:T(8,128)S(1)}, u32[]{:S(2)}, u32[]{:S(2)}) collective-permute-start(f32[4,48,1188]{2,1,0:T(8,128)S(1)} %shard_map.67), channel_id=1, source_target_pairs={{0,1},{1,0},{2,3},{3,2},{4,5},{5,4},{6,7},{7,6},{8,9},{9,8},{10,11... | collective-permute-start | bytes 2737160 | tf_op jit(solution)/shard_map/ppermute | solution.py:146
  110.2 5.0 %copy-start.1 = (bf16[4,48,1188]{2,1,0:T(8,128)(2,1)}, bf16[4,48,1188]{2,1,0:T(8,128)(2,1)S(1)}, u32[]{:S(2)}) copy-start(bf16[4,48,1188]{2,1,0:T(8,128)(2,1)S(1)} %all_to_all.39.grad_ref) | copy-start | bytes 1368580
  110.2 3.7 %collective-permute-start.1 = (bf16[4,48,1188]{2,1,0:T(8,128)(2,1)S(1)}, bf16[4,48,1188]{2,1,0:T(8,128)(2,1)S(1)}, u32[]{:S(2)}, u32[]{:S(2)}) collective-permute-start(bf16[4,48,1188]{2,1,0:T(8,128)(2,1)S(1)} %all_to_all.39.grad_ref), channel_id=1, source_target_pairs={{0,1},{1,0},{2,3},{3,2},{4,5},{5,4},{6,7},{7,6},{8,9},{9,8},{10,11... | collective-permute-start | bytes 1368584 | tf_op jit(solution)/shard_map/ppermute | solution.py:160
  114.0 1.3 copy-start.3
  132.2 22.4 %all-to-all-start.6 = ((bf16[16,6,1024]{2,1,0:T(8,128)(2,1)}), bf16[16,6,1024]{2,1,0:T(8,128)(2,1)S(1)}, u32[]{:S(2)}, u32[]{:S(2)}) async-start(bf16[16,6,1024]{2,1,0:T(8,128)(2,1)} %shard_map.74), calls=%async_computation.6 | async-start | bytes 524288 | tf_op jit(solution)/shard_map/all_to_all | solution.py:169
  136.7 1.9 %copy-start.2 = (bf16[4,48,1188]{2,1,0:T(8,128)(2,1)S(1)}, bf16[4,48,1188]{2,1,0:T(8,128)(2,1)}, u32[]{:S(2)}) copy-start(bf16[4,48,1188]{2,1,0:T(8,128)(2,1)} %copy-done.1) | copy-start | bytes 1368580

commit v7 on v6

--- a/solution.py
+++ b/solution.py
@@ -38,10 +38,10 @@
     return lax.all_to_all(copies, axis, 0, 0)
 
 
-def to_lanes(column):
+def to_lanes(column, first):
     shape = (column.shape[0], LANES)
     row, lane = (lax.broadcasted_iota(jnp.int32, shape, axis) for axis in (0, 1))
-    return jnp.sum(jnp.where(row == lane, column, 0.0), axis=0, keepdims=True)
+    return jnp.sum(jnp.where(row + first == lane, column, 0.0), axis=0, keepdims=True)
 
 
 def to_column(lanes, rows, first=0):
@@ -89,7 +89,7 @@
     total = jnp.sum(jnp.exp(logits - top), axis=1, keepdims=True)
     mask = target_mask(place_ref, targets_ref, logits.shape)
     target_logit = jnp.sum(jnp.where(mask, logits, 0.0), axis=1, keepdims=True)
-    row = jnp.concatenate([to_lanes(a) for a in (top, total, target_logit)], axis=1)
+    row = to_lanes(top + jnp.log(total), 0) + to_lanes(target_logit, LANES // 2)
     stats_ref[...] = jnp.broadcast_to(row[None], stats_ref.shape)
 
 
@@ -97,23 +97,22 @@
     logits = logits_ref[...]
     rows = logits.shape[0]
     stats = stats_ref[:, 0, :]
-    tops, totals, target_logits = (stats[:, k * LANES : (k + 1) * LANES] for k in range(3))
-    top = jnp.max(tops, axis=0, keepdims=True)
-    total = jnp.sum(totals * jnp.exp(tops - top), axis=0, keepdims=True)
-    used = lax.broadcasted_iota(jnp.int32, top.shape, 1) < rows
-    lse = top + jnp.log(jnp.where(used, total, 1.0))
-    loss = lse - jnp.sum(target_logits, axis=0, keepdims=True)
-    loss_ref[...] = loss[:, :rows]
+    top = jnp.max(stats, axis=0, keepdims=True)
+    lse = to_column(top + jnp.log(jnp.sum(jnp.exp(stats - top), axis=0, keepdims=True)), rows)
+    target_logit = to_column(jnp.sum(stats, axis=0, keepdims=True), rows, LANES // 2)
+    loss_ref[...] = to_lanes(lse - target_logit, 0)[:, :rows]
     weight = to_column(upstream_ref[...], rows, place_ref[1])
     mask = target_mask(place_ref, targets_ref, logits.shape)
-    probability = jnp.exp(logits - to_column(lse, rows))
+    probability = jnp.exp(logits - lse)
     grad = ((probability - jnp.where(mask, 1.0, 0.0)) * weight).astype(BF16)
     grad_ref[...] = jnp.broadcast_to(grad[None], grad_ref.shape)
 
 
 def over_x_kernel(place_ref, parts_ref, out_ref):
     core = place_ref[0]
-    blocks, block, _ = out_ref.shape
+    slice_width = parts_ref.shape[-1]
+    blocks, pieces, _ = out_ref.shape
+    block = out_ref.shape[2] // slice_width
     per_half = blocks // C
     for half in range(C):
         where = pl.ds(lax.rem(core + half, C), 1)
@@ -121,7 +120,11 @@
         for x in range(1, X):
             rows = rows + parts_ref[x, where][0].astype(F32)
         for k in range(per_half):
-            out_ref[half * per_half + k] = rows[k * block : (k + 1) * block].astype(BF16)
+            for part in range(pieces):
+                for row in range(block):
+                    first = k * pieces * block + part * block + row
+                    span = pl.ds(row * slice_width, slice_width)
+                    out_ref[half * per_half + k, part : part + 1, span] = rows[first : first + 1].astype(BF16)
 
 
 def per_device(hidden, head, targets, upstream):
@@ -134,7 +137,7 @@
     row_first = lax.axis_index(ROW_AXES) * own
     first_column = lax.axis_index(VOCAB_AXES) * width
     hidden, core, row_first, first_column = barrier((hidden, core, row_first, first_column))
-    by_z = gather_over(hidden, "z").reshape(-1, slice_width)
+    by_z = gather_over(hidden.reshape(2, -1), "z").reshape(-1, slice_width)
     by_x = gather_over(by_z, "x").reshape(Y, C, own, slice_width)
 
     by_x, targets, upstream, core, row_first, first_column = barrier(
@@ -150,7 +153,7 @@
     chip_logits, targets, upstream = barrier((chip_logits, targets[None], upstream[None]))
     parts = lax.all_to_all(chip_logits, "y", 0, 0)
 
-    out = [jax.ShapeDtypeStruct((own, width), F32), jax.ShapeDtypeStruct((X * Z, 1, 3 * LANES), F32)]
+    out = [jax.ShapeDtypeStruct((own, width), F32), jax.ShapeDtypeStruct((X * Z, 1, LANES), F32)]
     logits, stats = call(statistics_kernel, out, place, parts, targets)
     stats = lax.all_to_all(stats, VOCAB_AXES, 0, 0)
     out = [jax.ShapeDtypeStruct((1, own), F32), jax.ShapeDtypeStruct((Y, own, width), BF16)]
@@ -164,10 +167,10 @@
     partial = call(functools.partial(partial_kernel, 1), out, place, grad_other, head, partial, aliases={3: 0})
     over_x = lax.all_to_all(partial, "x", 0, 0)
     over_x, place, by_x, core, grad_own, grad_other = barrier((over_x, place, by_x, core, grad_own, grad_other))
-    out = jax.ShapeDtypeStruct((Z, token_count // (X * Z), slice_width), BF16)
+    out = jax.ShapeDtypeStruct((Z, 2, hidden.size // 2), BF16)
     over_x = call(over_x_kernel, out, place, over_x)
     over_z = lax.all_to_all(over_x, "z", 0, 0)
-    grad_hidden = jnp.sum(over_z.astype(F32), axis=0).astype(BF16)
+    grad_hidden = jnp.sum(over_z.astype(F32), axis=0).astype(BF16).reshape(hidden.shape)
 
     def head_part(grad, half):
         rows = lax.dynamic_index_in_dim(by_x, half, 1, keepdims=False).reshape(-1, slice_width)

time: 156 us -> 151 us (0.968)
  blocking collectives: 115 us -> 112 us
  waiting for transfers between devices: 15.3 us -> 13.5 us
    all_to_all x1, waiting for transfers between devices: 13.7 us -> 11.9 us  [per_device(): over_z = lax.all_to_all(over_x, 'z', 0, 0)]
    all_to_all x1, blocking collectives: 22.1 us -> 20.3 us  [per_device(): stats = lax.all_to_all(stats, VOCAB_AXES, 0, 0)]
    all_to_all x2, blocking collectives: 48.5 us -> 46.7 us  [gather_over(): return lax.all_to_all(copies, axis, 0, 0)]
where the time goes in v7:
time: 151 us; the launch traced here: 150 us
  blocking collectives  112 us (74%)
  waiting for transfers between devices  13.5 us (9%)
  Pallas kernels  9.56 us (6%)
  starting transfers between devices  8.71 us (6%)
  matrix products  4.2 us (3%)
  local copies, waits for them, and re-layouts  1.91 us (1%)
    all_to_all x2, blocking collectives, gather_over(): return lax.all_to_all(copies, axis, 0, 0)  46.7 us
    all_to_all x1, blocking collectives, per_device(): stats = lax.all_to_all(stats, VOCAB_AXES, 0, 0)  20.3 us
    all_to_all x1, blocking collectives, per_device(): parts = lax.all_to_all(chip_logits, 'y', 0, 0)  19 us
    all_to_all x1, blocking collectives, per_device(): over_x = lax.all_to_all(partial, 'x', 0, 0)  15.3 us
    all_to_all x1, waiting for transfers between devices, per_device(): over_z = lax.all_to_all(over_x, 'z', 0, 0)  11.9 us
    all_to_all x1, blocking collectives, per_device(): grad_own = lax.all_to_all(grad_rows, 'y', 0, 0)  10.3 us
    pallas_call x8, Pallas kernels, call(): pl.pallas_call(kernel, out_shape=out_shape, in_specs=[IN_SMEM] + [IN_VMEM...  9.56 us
    all_to_all x1, starting transfers between devices, per_device(): over_z = lax.all_to_all(over_x, 'z', 0, 0)  4.88 us
  transfers between devices with their start and end apart: 3, of which 3 were waited for; matrix products, arithmetic and copies ran while one was open for 3% of the time, Pallas kernels for 2%

profile of v7, /device:TPU:32, one launch (start us, length us, event | category | flops | bytes accessed | tf_op | source)
XLA Modules:
  0.0 150.5 jit_solution(5662160096336666071)
XLA Ops:
  0.6 0.0 copy-start.5
  0.6 0.0 copy-start.4
  0.7 0.0 copy-start
  0.7 0.9 broadcast_in_dim.20
  1.6 0.1 broadcast_in_dim.21
  1.7 30.8 %all_to_all.35 = bf16[16,2,3072]{2,1,0:T(2,128)(2,1)S(1)} all-to-all(bf16[16,2,3072]{2,1,0:T(2,128)(2,1)S(1)} %broadcast_in_dim.21), channel_id=1, replica_groups=mesh['x'=4,'z'=16,'y'=4,'core'=2] {'z'}, dimensions={0} | all-to-all | bytes 393216 | tf_op jit(solution)/shard_map/all_to_all | solution.py:38
  32.5 0.1 broadcast_in_dim.22
  32.6 0.1 broadcast_in_dim.23
  32.7 15.9 %all_to_all.36 = bf16[4,96,1024]{2,1,0:T(8,128)(2,1)S(1)} all-to-all(bf16[4,96,1024]{2,1,0:T(8,128)(2,1)S(1)} %broadcast_in_dim.23), channel_id=1, replica_groups=mesh['x'=4,'z'=16,'y'=4,'core'=2] {'x'}, dimensions={0} | all-to-all | bytes 1572864 | tf_op jit(solution)/shard_map/all_to_all | solution.py:38
  48.6 0.1 pad_add_fusion.place_ref
  48.7 0.0 copy-done
  48.7 1.5 shard_map.67
  50.2 1.9 %collective-permute-start = (f32[4,48,1188]{2,1,0:T(8,128)S(1)}, f32[4,48,1188]{2,1,0:T(8,128)S(1)}, u32[]{:S(2)}, u32[]{:S(2)}) collective-permute-start(f32[4,48,1188]{2,1,0:T(8,128)S(1)} %shard_map.67), channel_id=1, source_target_pairs={{0,1},{1,0},{2,3},{3,2},{4,5},{5,4},{6,7},{7,6},{8,9},{9,8},{10,11... | collective-permute-start | bytes 2737160 | tf_op jit(solution)/shard_map/ppermute | solution.py:149
  52.1 0.0 copy-done.4
  52.1 0.0 copy-done.5
  52.1 1.5 shard_map.68.a_ref
  53.6 1.0 collective-permute-done.b_ref
  54.6 0.7 shard_map.69
  55.3 19.0 %all_to_all.37.parts_ref = f32[4,48,1188]{2,1,0:T(8,128)S(1)} all-to-all(f32[4,48,1188]{2,1,0:T(8,128)S(1)} %shard_map.69), channel_id=1, replica_groups=mesh['x'=4,'z'=16,'y'=4,'core'=2] {'y'}, dimensions={0} | all-to-all | bytes 1824768 | tf_op jit(solution)/shard_map/all_to_all | solution.py:154
  74.3 0.8 shard_map.70
  75.1 20.3 %all_to_all.38.stats_ref = f32[64,1,128]{2,1,0:T(1,128)S(1)} all-to-all(f32[64,1,128]{2,1,0:T(1,128)S(1)} %get-tuple-element.44), channel_id=1, replica_groups=mesh['x'=4,'z'=16,'y'=4,'core'=2] {'x','z'}, dimensions={0} | all-to-all | bytes 65536 | tf_op jit(solution)/shard_map/all_to_all | solution.py:158
  95.4 1.3 shard_map.71
  96.7 10.3 %all_to_all.39.grad_ref = bf16[4,48,1188]{2,1,0:T(8,128)(2,1)S(1)} all-to-all(bf16[4,48,1188]{2,1,0:T(8,128)(2,1)S(1)} %get-tuple-element.48), channel_id=1, replica_groups=mesh['x'=4,'z'=16,'y'=4,'core'=2] {'y'}, dimensions={0} | all-to-all | bytes 912384 | tf_op jit(solution)/shard_map/all_to_all | solution.py:162
  107.0 0.0 copy-start.1
  107.0 1.9 %collective-permute-start.1 = (bf16[4,48,1188]{2,1,0:T(8,128)(2,1)S(1)}, bf16[4,48,1188]{2,1,0:T(8,128)(2,1)S(1)}, u32[]{:S(2)}, u32[]{:S(2)}) collective-permute-start(bf16[4,48,1188]{2,1,0:T(8,128)(2,1)S(1)} %all_to_all.39.grad_ref), channel_id=1, source_target_pairs={{0,1},{1,0},{2,3},{3,2},{4,5},{5,4},{6,7},{7,6},{8,9},{9,8},{10,11... | collective-permute-start | bytes 1368584 | tf_op jit(solution)/shard_map/ppermute | solution.py:163
  108.9 1.2 shard_map.72.refs_0_
  110.1 0.6 collective-permute-done.1.grad_ref
  110.7 0.0 copy-start.3
  110.7 1.2 shard_map.73
  112.0 0.0 copy-done.1
  112.0 0.0 copy-done.3
  112.0 15.3 %all_to_all.40.parts_ref = bf16[4,2,48,1024]{3,2,1,0:T(8,128)(2,1)S(1)} all-to-all(bf16[4,2,48,1024]{3,2,1,0:T(8,128)(2,1)S(1)} %shard_map.73), channel_id=1, replica_groups=mesh['x'=4,'z'=16,'y'=4,'core'=2] {'x'}, dimensions={0} | all-to-all | bytes 1572864 | tf_op jit(solution)/shard_map/all_to_all | solution.py:168
  127.3 1.4 shard_map.74
  128.7 4.9 %all-to-all-start.6 = ((bf16[16,2,3072]{2,1,0:T(2,128)(2,1)}), bf16[16,2,3072]{2,1,0:T(2,128)(2,1)S(1)}, u32[]{:S(2)}, u32[]{:S(2)}) async-start(bf16[16,2,3072]{2,1,0:T(2,128)(2,1)} %shard_map.74), calls=%async_computation.6 | async-start | bytes 393216 | tf_op jit(solution)/shard_map/all_to_all | solution.py:172
  133.5 0.1 constant_dynamic-slice_fusion.1
  133.6 0.0 copy-start.2
  133.6 1.9 %fusion = f32[1188,1024]{1,0:T(8,128)S(1)} fusion(bf16[192,1188]{1,0:T(8,128)(2,1)} %bitcast.17, bf16[192,1024]{1,0:T(8,128)(2,1)S(1)} %bitcast.19), kind=kOutput, calls=%fused_computation.4 | convolution fusion | flops 467140608 | bytes 5715456 | tf_op jit(solution)/shard_map/dot_general | solution.py:178
  135.5 0.0 copy-done.2
  135.5 2.3 %add_convert_fusion = bf16[1188,1024]{1,0:T(8,128)(2,1)} fusion(f32[1188,1024]{1,0:T(8,128)S(1)} %fusion, bf16[192,1188]{1,0:T(8,128)(2,1)S(1)} %bitcast.16, bf16[192,1024]{1,0:T(8,128)(2,1)S(1)} %bitcast.18), kind=kOutput, calls=%fused_computation | convolution fusion | flops 469573632 | bytes 8148480 | tf_op jit(solution)/shard_map/dot_general | solution.py:178
  137.8 11.9 %all-to-all-done.6 = bf16[16,2,3072]{2,1,0:T(2,128)(2,1)S(1)} async-done(((bf16[16,2,3072]{2,1,0:T(2,128)(2,1)}), bf16[16,2,3072]{2,1,0:T(2,128)(2,1)S(1)}, u32[]{:S(2)}, u32[]{:S(2)}) %all-to-all-start.6) | async-done | bytes 196640 | tf_op jit(solution)/shard_map/all_to_all | solution.py:172
  149.7 0.2 reduce_sum.12
  149.9 0.6 reshape.29
  (2 shorter events, 0.0 us)
Async XLA Ops:
  0.6 51.5 %copy-start.5 = (f32[384]{0:T(512)S(1)}, f32[384]{0:T(512)}, u32[]{:S(2)}) copy-start(f32[384]{0:T(512)} %param.7) | copy-start | bytes 4612
  0.6 51.4 %copy-start.4 = (s32[384]{0:T(512)S(1)}, s32[384]{0:T(512)}, u32[]{:S(2)}) copy-start(s32[384]{0:T(512)} %param.6) | copy-start | bytes 4612
  0.7 48.0 %copy-start = (bf16[1188,1024]{1,0:T(8,128)(2,1)S(1)}, bf16[1188,1024]{1,0:T(8,128)(2,1)}, u32[]{:S(2)}) copy-start(bf16[1188,1024]{1,0:T(8,128)(2,1)} %head_ref.7) | copy-start | bytes 7299076
  50.2 4.5 %collective-permute-start = (f32[4,48,1188]{2,1,0:T(8,128)S(1)}, f32[4,48,1188]{2,1,0:T(8,128)S(1)}, u32[]{:S(2)}, u32[]{:S(2)}) collective-permute-start(f32[4,48,1188]{2,1,0:T(8,128)S(1)} %shard_map.67), channel_id=1, source_target_pairs={{0,1},{1,0},{2,3},{3,2},{4,5},{5,4},{6,7},{7,6},{8,9},{9,8},{10,11... | collective-permute-start | bytes 2737160 | tf_op jit(solution)/shard_map/ppermute | solution.py:149
  107.0 5.0 %copy-start.1 = (bf16[4,48,1188]{2,1,0:T(8,128)(2,1)}, bf16[4,48,1188]{2,1,0:T(8,128)(2,1)S(1)}, u32[]{:S(2)}) copy-start(bf16[4,48,1188]{2,1,0:T(8,128)(2,1)S(1)} %all_to_all.39.grad_ref) | copy-start | bytes 1368580
  107.0 3.7 %collective-permute-start.1 = (bf16[4,48,1188]{2,1,0:T(8,128)(2,1)S(1)}, bf16[4,48,1188]{2,1,0:T(8,128)(2,1)S(1)}, u32[]{:S(2)}, u32[]{:S(2)}) collective-permute-start(bf16[4,48,1188]{2,1,0:T(8,128)(2,1)S(1)} %all_to_all.39.grad_ref), channel_id=1, source_target_pairs={{0,1},{1,0},{2,3},{3,2},{4,5},{5,4},{6,7},{7,6},{8,9},{9,8},{10,11... | collective-permute-start | bytes 1368584 | tf_op jit(solution)/shard_map/ppermute | solution.py:163
  110.7 1.3 copy-start.3
  128.7 21.0 %all-to-all-start.6 = ((bf16[16,2,3072]{2,1,0:T(2,128)(2,1)}), bf16[16,2,3072]{2,1,0:T(2,128)(2,1)S(1)}, u32[]{:S(2)}, u32[]{:S(2)}) async-start(bf16[16,2,3072]{2,1,0:T(2,128)(2,1)} %shard_map.74), calls=%async_computation.6 | async-start | bytes 393216 | tf_op jit(solution)/shard_map/all_to_all | solution.py:172
  133.6 1.9 %copy-start.2 = (bf16[4,48,1188]{2,1,0:T(8,128)(2,1)S(1)}, bf16[4,48,1188]{2,1,0:T(8,128)(2,1)}, u32[]{:S(2)}) copy-start(bf16[4,48,1188]{2,1,0:T(8,128)(2,1)} %copy-done.1) | copy-start | bytes 1368580

commit v8 on v7

v8 whole, which is shorter than its diff:
```python
import functools

import jax
import jax.numpy as jnp
from jax import lax
from jax.experimental import pallas as pl
from jax.experimental.pallas import tpu as pltpu
from jax.sharding import Mesh, PartitionSpec as P

X, Z, Y, C = 4, 16, 4, 2
VOCAB_AXES = ("x", "z")
ROW_AXES = ("y", "core")
SWAP = [(0, 1), (1, 0)]
LANES = 128
TILE = 256
BF16, F32 = jnp.bfloat16, jnp.float32
IN_VMEM = pl.BlockSpec(memory_space=pltpu.VMEM)
IN_SMEM = pl.BlockSpec(memory_space=pltpu.SMEM)


def call(kernel, out_shape, place, *operands, cost=None):
    many = isinstance(out_shape, list)
    moved = cost or sum(a.size * a.dtype.itemsize for a in operands)
    return pl.pallas_call(
        kernel,
        out_shape=out_shape,
        in_specs=[IN_SMEM] + [IN_VMEM] * len(operands),
        out_specs=[IN_VMEM] * len(out_shape) if many else IN_VMEM,
        cost_estimate=pl.CostEstimate(flops=moved, bytes_accessed=moved, transcendentals=0),
        compiler_params=pltpu.CompilerParams(vmem_limit_bytes=8 * 2**20),
    )(place, *operands)


def gather_over(block, axis):
    size = lax.axis_size(axis)
    copies = jnp.broadcast_to(block[None], (size,) + block.shape)
    return lax.all_to_all(copies, axis, 0, 0)


def to_lanes(column, first):
    shape = (column.shape[0], LANES)
    row, lane = (lax.broadcasted_iota(jnp.int32, shape, axis) for axis in (0, 1))
    return jnp.sum(jnp.where(row + first == lane, column, 0.0), axis=0, keepdims=True)


def to_column(lanes, rows, first=0):
    row, lane = (lax.broadcasted_iota(jnp.int32, (rows, LANES), axis) for axis in (0, 1))
    found = jnp.zeros((rows, LANES), lanes.dtype)
    for k in range(lanes.shape[0]):
        found = jnp.where(row + first == lane + k * LANES, lanes[k : k + 1], found)
    return jnp.sum(found, axis=1, keepdims=True)


def target_mask(place_ref, targets_ref, shape):
    column = to_column(targets_ref[...], shape[0], place_ref[1]) - place_ref[2]
    return lax.broadcasted_iota(jnp.int32, shape, 1) == column


def spans(length):
    return [pl.ds(first, min(TILE, length - first)) for first in range(0, length, TILE)]


def logits_kernel(place_ref, rows_ref, head_ref, other_ref, out_ref):
    mine = place_ref[0]
    own, rest = (
        rows_ref[:, pl.ds(c, 1)].reshape(-1, rows_ref.shape[-1]) for c in (mine, C - 1 - mine)
    )

    def dot(rows, part):
        return lax.dot_general(rows, part, (((1,), (1,)), ((), ())), preferred_element_type=F32)

    for span in spans(head_ref.shape[0]):
        tile = dot(own, head_ref[span, :]) + dot(rest, other_ref[span, :])
        out_ref[:, :, span] = tile.reshape(out_ref.shape[:2] + (span.size,))


def partial_kernel(place_ref, grad_ref, head_ref, other_ref, out_ref):
    mine = place_ref[0]
    blocks, _, own, slice_width = out_ref.shape
    grad = grad_ref[...].reshape(blocks * own, -1)
    for c, part_ref in ((mine, head_ref), (C - 1 - mine, other_ref)):
        for span in spans(slice_width):
            tile = jnp.dot(grad, part_ref[:, span], preferred_element_type=F32).astype(BF16)
            out_ref[:, pl.ds(c, 1), :, span] = tile.reshape(blocks, 1, own, span.size)


def statistics_kernel(place_ref, parts_ref, targets_ref, logits_ref, stats_ref):
    logits = parts_ref[0]
    for y in range(1, Y):
        logits = logits + parts_ref[y]
    logits_ref[...] = logits
    top = jnp.max(logits, axis=1, keepdims=True)
    total = jnp.sum(jnp.exp(logits - top), axis=1, keepdims=True)
    mask = target_mask(place_ref, targets_ref, logits.shape)
    target_logit = jnp.sum(jnp.where(mask, logits, 0.0), axis=1, keepdims=True)
    row = to_lanes(top + jnp.log(total), 0) + to_lanes(target_logit, LANES // 2)
    stats_ref[...] = jnp.broadcast_to(row[None], stats_ref.shape)


def softmax_kernel(place_ref, stats_ref, logits_ref, targets_ref, upstream_ref, loss_ref, grad_ref):
    logits = logits_ref[...]
    rows = logits.shape[0]
    stats = stats_ref[:, 0, :]
    top = jnp.max(stats, axis=0, keepdims=True)
    lse = to_column(top + jnp.log(jnp.sum(jnp.exp(stats - top), axis=0, keepdims=True)), rows)
    target_logit = to_column(jnp.sum(stats, axis=0, keepdims=True), rows, LANES // 2)
    loss_ref[...] = to_lanes(lse - target_logit, 0)[:, :rows]
    weight = to_column(upstream_ref[...], rows, place_ref[1])
    mask = target_mask(place_ref, targets_ref, logits.shape)
    probability = jnp.exp(logits - lse)
    grad = ((probability - jnp.where(mask, 1.0, 0.0)) * weight).astype(BF16)
    grad_ref[...] = jnp.broadcast_to(grad[None], grad_ref.shape)


def over_x_kernel(place_ref, parts_ref, out_ref):
    slice_width = parts_ref.shape[-1]
    blocks, pieces, _ = out_ref.shape
    block = out_ref.shape[2] // slice_width
    per_half = blocks // C
    for half in range(C):
        rows = parts_ref[0, half].astype(F32)
        for x in range(1, X):
            rows = rows + parts_ref[x, half].astype(F32)
        for k in range(per_half):
            for part in range(pieces):
                for row in range(block):
                    first = k * pieces * block + part * block + row
                    span = pl.ds(row * slice_width, slice_width)
                    out_ref[half * per_half + k, part : part + 1, span] = rows[first : first + 1].astype(BF16)


def head_kernel(place_ref, rows_ref, grad_ref, rest_rows_ref, rest_grad_ref, out_ref):
    mine = place_ref[0]
    width, slice_width = out_ref.shape
    rows = rows_ref[:, pl.ds(mine, 1)].reshape(-1, slice_width)
    rest_rows = rest_rows_ref[...].reshape(-1, slice_width)

    def dot(grad_ref, span, rows):
        grad = grad_ref[:, :, span].reshape(-1, span.size)
        return lax.dot_general(grad, rows, (((0,), (0,)), ((), ())), preferred_element_type=F32)

    for span in spans(width):
        out_ref[span, :] = (dot(grad_ref, span, rows) + dot(rest_grad_ref, span, rest_rows)).astype(BF16)


def per_device(hidden, head, targets, upstream):
    width, slice_width = head.shape
    token_count = targets.shape[0]
    own = token_count // (Y * C)
    barrier = lax.optimization_barrier

    core = lax.axis_index("core")
    row_first = lax.axis_index(ROW_AXES) * own
    first_column = lax.axis_index(VOCAB_AXES) * width
    hidden, core, row_first, first_column = barrier((hidden, core, row_first, first_column))
    by_z = gather_over(hidden.reshape(2, -1), "z").reshape(C, own, slice_width)

    by_z, head = barrier((by_z, head))
    head_other = lax.ppermute(head, "core", SWAP)
    copies = jnp.broadcast_to(by_z, (X, C, own, slice_width)).reshape(X * C, own, slice_width)
    by_x = lax.all_to_all(copies, ("x", "core"), 0, 0).reshape(X, C, own, slice_width)

    by_x, targets, upstream, core, row_first, first_column = barrier(
        (by_x, targets, upstream, core, row_first, first_column)
    )
    place = jnp.stack([core, row_first, first_column])
    targets, upstream = targets.reshape(-1, LANES), upstream.reshape(-1, LANES)
    out = jax.ShapeDtypeStruct((Y, own, width), F32)
    chip_logits = call(logits_kernel, out, place, by_x, head, head_other)
    chip_logits, targets, upstream = barrier((chip_logits, targets, upstream))
    parts = lax.all_to_all(chip_logits, "y", 0, 0)

    out = [jax.ShapeDtypeStruct((own, width), F32), jax.ShapeDtypeStruct((X * Z, 1, LANES), F32)]
    logits, stats = call(statistics_kernel, out, place, parts, targets)
    stats = lax.all_to_all(stats, VOCAB_AXES, 0, 0)
    out = [jax.ShapeDtypeStruct((1, own), F32), jax.ShapeDtypeStruct((Y, own, width), BF16)]
    token_loss, grad_rows = call(softmax_kernel, out, place, stats, logits, targets, upstream)

    grad_half = lax.all_to_all(grad_rows, "y", 0, 0)

    out = jax.ShapeDtypeStruct((X, C, own, slice_width), BF16)
    partial = call(partial_kernel, out, place, grad_half, head, head_other)
    over_x = lax.all_to_all(partial.reshape(X * C, own, slice_width), ("x", "core"), 0, 0).reshape(out.shape)
    out = jax.ShapeDtypeStruct((Z, 2, hidden.size // 2), BF16)
    over_x = call(over_x_kernel, out, place, over_x)
    over_x, by_x, core, grad_half, place = barrier((over_x, by_x, core, grad_half, place))
    over_z = lax.all_to_all(over_x, "z", 0, 0)
    grad_hidden = jnp.sum(over_z.astype(F32), axis=0).astype(BF16).reshape(hidden.shape)

    grad_rest = lax.ppermute(grad_half, "core", SWAP)
    rows_rest = lax.dynamic_index_in_dim(by_x, 1 - core, 1)
    rows_rest = lax.ppermute(rows_rest, "core", SWAP)
    out = jax.ShapeDtypeStruct((width, slice_width), BF16)
    grad_head = call(head_kernel, out, place, by_x, grad_half, rows_rest, grad_rest, cost=1)
    return token_loss[0], grad_hidden, grad_head


def solution(mesh):
    torus = Mesh(mesh.devices.reshape(X, Z, Y, C), VOCAB_AXES + ROW_AXES)
    return jax.shard_map(
        per_device,
        mesh=torus,
        in_specs=(P(VOCAB_AXES, ROW_AXES), P(VOCAB_AXES, ROW_AXES), P(), P()),
        out_specs=(P(ROW_AXES), P(VOCAB_AXES, ROW_AXES), P(VOCAB_AXES, ROW_AXES)),
        check_vma=False,
    )
```

time: 151 us -> 146 us (0.967)
  waiting for transfers between devices: 13.5 us -> 8 us
  matrix products: 4.2 us -> 0 us
  starting transfers between devices: 8.71 us -> 11 us
    all_to_all x2 -> x3, blocking collectives: 25.6 us -> 43.8 us  [the longest x1 17.4 us: per_device(): lax.all_to_all(copies, ('x', 'core'), 0, 0).reshape(X, C, own, slice_width)]
    all_to_all x2 -> x1, blocking collectives: 46.7 us -> 30.8 us  [gather_over(): return lax.all_to_all(copies, axis, 0, 0)]
    all_to_all x1, waiting for transfers between devices: 11.9 us -> 6.66 us  [per_device(): over_z = lax.all_to_all(over_x, 'z', 0, 0)]
    dot_general x2 -> x0, matrix products: 4.2 us -> none  [head_part(): lax.dot_general(grad, rows, (((0,), (0,)), ((), ())), preferred_element_t...]
    ppermute x2 -> x3, starting transfers between devices: 3.83 us -> 6.25 us  [the longest x1 2.41 us: per_device(): rows_rest = lax.ppermute(rows_rest, 'core', SWAP)]
    pallas_call x8 -> x6, Pallas kernels: 9.56 us -> 10.9 us  [call(): pl.pallas_call(kernel, out_shape=out_shape, in_specs=[IN_SMEM] + [IN_VMEM...]
  transfers between devices with their start and end apart: 3 -> 4, of which waited for: 3 -> 2; matrix products, arithmetic and copies ran while one was open for 3% -> 0% of each run, Pallas kernels for 2% -> 2%
where the time goes in v8:
time: 146 us; the launch traced here: 145 us
  blocking collectives  113 us (77%)
  starting transfers between devices  11 us (8%)
  Pallas kernels  10.9 us (7%)
  waiting for transfers between devices  8 us (5%)
  local copies, waits for them, and re-layouts  1.89 us (1%)
    all_to_all x1, blocking collectives, gather_over(): return lax.all_to_all(copies, axis, 0, 0)  30.8 us
    all_to_all x1, blocking collectives, per_device(): stats = lax.all_to_all(stats, VOCAB_AXES, 0, 0)  19.8 us
    all_to_all x1, blocking collectives, per_device(): parts = lax.all_to_all(chip_logits, 'y', 0, 0)  18.3 us
    all_to_all x1, blocking collectives, per_device(): lax.all_to_all(copies, ('x', 'core'), 0, 0).reshape(X, C, own, slice_width)  17.4 us
    all_to_all x1, blocking collectives, per_device(): lax.all_to_all(partial.reshape(X * C, own, slice_width), ('x', 'core'), 0...  16.1 us
    pallas_call x6, Pallas kernels, call(): pl.pallas_call(kernel, out_shape=out_shape, in_specs=[IN_SMEM] + [IN_VMEM...  10.9 us
    all_to_all x1, blocking collectives, per_device(): grad_half = lax.all_to_all(grad_rows, 'y', 0, 0)  10.3 us
    all_to_all x1, waiting for transfers between devices, per_device(): over_z = lax.all_to_all(over_x, 'z', 0, 0)  6.66 us
  transfers between devices with their start and end apart: 4, of which 2 were waited for; matrix products, arithmetic and copies ran while one was open for 0% of the time, Pallas kernels for 2%

profile of v8, /device:TPU:32, one launch (start us, length us, event | category | flops | bytes accessed | tf_op | source)
XLA Modules:
  0.0 145.4 jit_solution(5628553183336388406)
XLA Ops:
  0.6 0.0 copy-start
  0.7 0.9 broadcast_in_dim.10
  1.5 0.1 broadcast_in_dim.11
  1.7 30.8 %all_to_all.35 = bf16[16,2,3072]{2,1,0:T(2,128)(2,1)S(1)} all-to-all(bf16[16,2,3072]{2,1,0:T(2,128)(2,1)S(1)} %broadcast_in_dim.11), channel_id=1, replica_groups=mesh['x'=4,'z'=16,'y'=4,'core'=2] {'z'}, dimensions={0} | all-to-all | bytes 393216 | tf_op jit(solution)/shard_map/all_to_all | solution.py:37
  32.5 0.1 reshape.31
  32.6 1.9 %collective-permute-start = (bf16[1188,1024]{1,0:T(8,128)(2,1)}, bf16[1188,1024]{1,0:T(8,128)(2,1)S(1)}, u32[]{:S(2)}, u32[]{:S(2)}) collective-permute-start(bf16[1188,1024]{1,0:T(8,128)(2,1)} %head_ref.1), channel_id=1, source_target_pairs={{0,1},{1,0},{2,3},{3,2},{4,5},{5,4},{6,7},{7,6},{8,9},{9,8},{10,11... | collective-permute-start | bytes 7299080 | tf_op jit(solution)/shard_map/ppermute | solution.py:159
  34.5 0.1 broadcast_in_dim.12
  34.6 17.4 %all_to_all.36 = bf16[8,48,1024]{2,1,0:T(8,128)(2,1)S(1)} all-to-all(bf16[8,48,1024]{2,1,0:T(8,128)(2,1)S(1)} %bitcast.18), channel_id=1, replica_groups=mesh['x'=4,'z'=16,'y'=4,'core'=2] {'x','core'}, dimensions={0} | all-to-all | bytes 1572864 | tf_op jit(solution)/shard_map/all_to_all | solution.py:161
  52.1 0.1 pad_add_fusion.place_ref
  52.1 0.0 copy-start.3
  52.2 0.0 collective-permute-done.other_ref
  52.2 0.0 copy-done
  52.2 2.2 %shard_map.67 = f32[4,48,1188]{2,1,0:T(8,128)S(1)} custom-call(s32[3]{0:T(128)S(1)} %pad_add_fusion.place_ref, bf16[4,2,48,1024]{3,2,1,0:T(8,128)(2,1)S(1)} %bitcast.10, bf16[1188,1024]{1,0:T(8,128)(2,1)S(1)} %copy-done, bf16[1188,1024]{1,0:T(8,128)(2,1)S(1)} %collective-permute-done.other_ref), custom_call_target="tpu_custom_call" | custom-call | flops 5652480 | bytes 5652480 | tf_op jit(solution)/shard_map/pallas_call | solution.py:24
  54.4 0.0 copy-start.4
  54.4 18.3 %all_to_all.37.parts_ref = f32[4,48,1188]{2,1,0:T(8,128)S(1)} all-to-all(f32[4,48,1188]{2,1,0:T(8,128)S(1)} %shard_map.67), channel_id=1, replica_groups=mesh['x'=4,'z'=16,'y'=4,'core'=2] {'y'}, dimensions={0} | all-to-all | bytes 1824768 | tf_op jit(solution)/shard_map/all_to_all | solution.py:171
  72.7 0.0 copy-done.3
  72.7 0.8 shard_map.68
  73.5 19.8 %all_to_all.38.stats_ref = f32[64,1,128]{2,1,0:T(1,128)S(1)} all-to-all(f32[64,1,128]{2,1,0:T(1,128)S(1)} %get-tuple-element.41), channel_id=1, replica_groups=mesh['x'=4,'z'=16,'y'=4,'core'=2] {'x','z'}, dimensions={0} | all-to-all | bytes 65536 | tf_op jit(solution)/shard_map/all_to_all | solution.py:175
  93.3 0.0 copy-done.4
  93.3 1.3 shard_map.69
  94.6 10.3 %all_to_all.39.grad_ref = bf16[4,48,1188]{2,1,0:T(8,128)(2,1)S(1)} all-to-all(bf16[4,48,1188]{2,1,0:T(8,128)(2,1)S(1)} %get-tuple-element.45), channel_id=1, replica_groups=mesh['x'=4,'z'=16,'y'=4,'core'=2] {'y'}, dimensions={0} | all-to-all | bytes 912384 | tf_op jit(solution)/shard_map/all_to_all | solution.py:179
  104.9 0.0 copy-start.1
  104.9 1.7 %shard_map.70 = bf16[4,2,48,1024]{3,2,1,0:T(8,128)(2,1)S(1)} custom-call(s32[3]{0:T(128)S(1)} %pad_add_fusion.place_ref, bf16[4,48,1188]{2,1,0:T(8,128)(2,1)S(1)} %all_to_all.39.grad_ref, bf16[1188,1024]{1,0:T(8,128)(2,1)S(1)} %copy-done, bf16[1188,1024]{1,0:T(8,128)(2,1)S(1)} %collective-permute-done.other_ref), custom_call_target="tpu_custom_call" | custom-call | flops 5322240 | bytes 5322240 | tf_op jit(solution)/shard_map/pallas_call | solution.py:24
  106.7 0.0 copy-done.1
  106.7 0.0 copy-start.2
  106.7 16.1 %all_to_all.40 = bf16[8,48,1024]{2,1,0:T(8,128)(2,1)S(1)} all-to-all(bf16[8,48,1024]{2,1,0:T(8,128)(2,1)S(1)} %bitcast.13), channel_id=1, replica_groups=mesh['x'=4,'z'=16,'y'=4,'core'=2] {'x','core'}, dimensions={0} | all-to-all | bytes 1572864 | tf_op jit(solution)/shard_map/all_to_all | solution.py:183
  122.7 1.4 shard_map.71
  124.1 4.7 %all-to-all-start.6 = ((bf16[16,2,3072]{2,1,0:T(2,128)(2,1)}), bf16[16,2,3072]{2,1,0:T(2,128)(2,1)S(1)}, u32[]{:S(2)}, u32[]{:S(2)}) async-start(bf16[16,2,3072]{2,1,0:T(2,128)(2,1)} %shard_map.71), calls=%async_computation.6 | async-start | bytes 393216 | tf_op jit(solution)/shard_map/all_to_all | solution.py:187
  128.8 0.0 copy-done.2
  128.8 1.9 %collective-permute-start.2 = (bf16[4,48,1188]{2,1,0:T(8,128)(2,1)S(1)}, bf16[4,48,1188]{2,1,0:T(8,128)(2,1)S(1)}, u32[]{:S(2)}, u32[]{:S(2)}) collective-permute-start(bf16[4,48,1188]{2,1,0:T(8,128)(2,1)S(1)} %copy-done.2), channel_id=1, source_target_pairs={{0,1},{1,0},{2,3},{3,2},{4,5},{5,4},{6,7},{7,6},{8,9},{9,8},{10,11... | collective-permute-start | bytes 1368584 | tf_op jit(solution)/shard_map/ppermute | solution.py:190
  130.8 2.4 %collective-permute-start.1 = (bf16[4,1,48,1024]{3,2,1,0:T(8,128)(2,1)S(1)}, bf16[4,1,48,1024]{3,2,1,0:T(8,128)(2,1)S(1)}, u32[]{:S(2)}, u32[]{:S(2)}) collective-permute-start(bf16[4,1,48,1024]{3,2,1,0:T(8,128)(2,1)S(1)} %constant_dynamic-slice_fusion), channel_id=1, source_target_pairs={{0,1},{1,0},{2,3},{3,2},{4,5},{5,4},{6,7},{7,6},{8,9},{9,8},{10,11... | collective-permute-start | bytes 1179656 | tf_op jit(solution)/shard_map/ppermute | solution.py:192
  133.2 1.3 collective-permute-done.1.rest_rows_ref
  134.5 0.0 collective-permute-done.2.rest_grad_ref
  134.5 3.4 %shard_map.72 = bf16[1188,1024]{1,0:T(8,128)(2,1)} custom-call(s32[3]{0:T(128)S(1)} %pad_add_fusion.place_ref, bf16[4,2,48,1024]{3,2,1,0:T(8,128)(2,1)S(1)} %bitcast.12, bf16[4,48,1188]{2,1,0:T(8,128)(2,1)S(1)} %copy-done.2, bf16[4,1,48,1024]{3,2,1,0:T(8,128)(2,1)S(1)} %collective-permute-done.1.rest_rows_ref, ...), custom_call_target="tpu_custom_call" | custom-call | flops 1 | bytes 1 | tf_op jit(solution)/shard_map/pallas_call | solution.py:24
  138.0 6.7 %all-to-all-done.6 = bf16[16,2,3072]{2,1,0:T(2,128)(2,1)S(1)} async-done(((bf16[16,2,3072]{2,1,0:T(2,128)(2,1)}), bf16[16,2,3072]{2,1,0:T(2,128)(2,1)S(1)}, u32[]{:S(2)}, u32[]{:S(2)}) %all-to-all-start.6) | async-done | bytes 196640 | tf_op jit(solution)/shard_map/all_to_all | solution.py:187
  144.6 0.2 reduce_sum.12
  144.8 0.6 reshape.38
  (1 shorter events, 0.0 us)
Async XLA Ops:
  0.6 51.5 %copy-start = (bf16[1188,1024]{1,0:T(8,128)(2,1)S(1)}, bf16[1188,1024]{1,0:T(8,128)(2,1)}, u32[]{:S(2)}) copy-start(bf16[1188,1024]{1,0:T(8,128)(2,1)} %head_ref.1) | copy-start | bytes 7299076
  32.6 19.6 %collective-permute-start = (bf16[1188,1024]{1,0:T(8,128)(2,1)}, bf16[1188,1024]{1,0:T(8,128)(2,1)S(1)}, u32[]{:S(2)}, u32[]{:S(2)}) collective-permute-start(bf16[1188,1024]{1,0:T(8,128)(2,1)} %head_ref.1), channel_id=1, source_target_pairs={{0,1},{1,0},{2,3},{3,2},{4,5},{5,4},{6,7},{7,6},{8,9},{9,8},{10,11... | collective-permute-start | bytes 7299080 | tf_op jit(solution)/shard_map/ppermute | solution.py:159
  52.1 20.5 %copy-start.3 = (s32[384]{0:T(512)S(1)}, s32[384]{0:T(512)}, u32[]{:S(2)}) copy-start(s32[384]{0:T(512)} %param.6) | copy-start | bytes 4612
  54.4 38.9 %copy-start.4 = (f32[384]{0:T(512)S(1)}, f32[384]{0:T(512)}, u32[]{:S(2)}) copy-start(f32[384]{0:T(512)} %param.7) | copy-start | bytes 4612
  104.9 1.8 %copy-start.1 = (bf16[4,48,1188]{2,1,0:T(8,128)(2,1)}, bf16[4,48,1188]{2,1,0:T(8,128)(2,1)S(1)}, u32[]{:S(2)}) copy-start(bf16[4,48,1188]{2,1,0:T(8,128)(2,1)S(1)} %all_to_all.39.grad_ref) | copy-start | bytes 1368580
  106.7 22.1 %copy-start.2 = (bf16[4,48,1188]{2,1,0:T(8,128)(2,1)S(1)}, bf16[4,48,1188]{2,1,0:T(8,128)(2,1)}, u32[]{:S(2)}) copy-start(bf16[4,48,1188]{2,1,0:T(8,128)(2,1)} %copy-done.1) | copy-start | bytes 1368580
  124.1 20.5 %all-to-all-start.6 = ((bf16[16,2,3072]{2,1,0:T(2,128)(2,1)}), bf16[16,2,3072]{2,1,0:T(2,128)(2,1)S(1)}, u32[]{:S(2)}, u32[]{:S(2)}) async-start(bf16[16,2,3072]{2,1,0:T(2,128)(2,1)} %shard_map.71), calls=%async_computation.6 | async-start | bytes 393216 | tf_op jit(solution)/shard_map/all_to_all | solution.py:187
  128.8 5.7 %collective-permute-start.2 = (bf16[4,48,1188]{2,1,0:T(8,128)(2,1)S(1)}, bf16[4,48,1188]{2,1,0:T(8,128)(2,1)S(1)}, u32[]{:S(2)}, u32[]{:S(2)}) collective-permute-start(bf16[4,48,1188]{2,1,0:T(8,128)(2,1)S(1)} %copy-done.2), channel_id=1, source_target_pairs={{0,1},{1,0},{2,3},{3,2},{4,5},{5,4},{6,7},{7,6},{8,9},{9,8},{10,11... | collective-permute-start | bytes 1368584 | tf_op jit(solution)/shard_map/ppermute | solution.py:190
  130.8 3.7 %collective-permute-start.1 = (bf16[4,1,48,1024]{3,2,1,0:T(8,128)(2,1)S(1)}, bf16[4,1,48,1024]{3,2,1,0:T(8,128)(2,1)S(1)}, u32[]{:S(2)}, u32[]{:S(2)}) collective-permute-start(bf16[4,1,48,1024]{3,2,1,0:T(8,128)(2,1)S(1)} %constant_dynamic-slice_fusion), channel_id=1, source_target_pairs={{0,1},{1,0},{2,3},{3,2},{4,5},{5,4},{6,7},{7,6},{8,9},{9,8},{10,11... | collective-permute-start | bytes 1179656 | tf_op jit(solution)/shard_map/ppermute | solution.py:192

commit v9 on v8

v9 whole, which is shorter than its diff:
```python
import functools

import jax
import jax.numpy as jnp
from jax import lax
from jax.experimental import pallas as pl
from jax.experimental.pallas import tpu as pltpu
from jax.sharding import Mesh, PartitionSpec as P

X, ZH, ZL, Y, C = 4, 8, 2, 4, 2
VOCAB_AXES = ("x", "zh", "zl")
NEAR_AXES = ("x", "zl", "core")
ROW_AXES = ("y", "core")
SWAP = [(0, 1), (1, 0)]
LANES = 128
PACK_COST = 2**26
TILE = 256
BF16, F32 = jnp.bfloat16, jnp.float32
IN_VMEM = pl.BlockSpec(memory_space=pltpu.VMEM)
IN_ANY = pl.BlockSpec(memory_space=pl.ANY)
IN_SMEM = pl.BlockSpec(memory_space=pltpu.SMEM)


def call(kernel, out_shape, place, *operands, cost=None, scratch=(), last=IN_VMEM):
    many = isinstance(out_shape, list)
    moved = cost or sum(a.size * a.dtype.itemsize for a in operands)
    return pl.pallas_call(
        kernel,
        out_shape=out_shape,
        in_specs=[IN_SMEM] + [IN_VMEM] * (len(operands) - 1) + [last],
        out_specs=[IN_VMEM] * len(out_shape) if many else IN_VMEM,
        scratch_shapes=scratch,
        cost_estimate=pl.CostEstimate(flops=moved, bytes_accessed=moved, transcendentals=0),
        compiler_params=pltpu.CompilerParams(vmem_limit_bytes=8 * 2**20),
    )(place, *operands)


def gather_over(block, axis):
    size = lax.axis_size(axis)
    copies = jnp.broadcast_to(block[None], (size,) + block.shape)
    return lax.all_to_all(copies, axis, 0, 0)


def to_lanes(column, position):
    lane = lax.broadcasted_iota(jnp.int32, (column.shape[0], LANES), 1)
    return jnp.sum(jnp.where(position == lane, column, 0.0), axis=0, keepdims=True)


def to_column(lanes, position):
    lane = lax.broadcasted_iota(jnp.int32, (position.shape[0], LANES), 1)
    found = jnp.zeros(lane.shape, lanes.dtype)
    for k in range(lanes.shape[0]):
        found = jnp.where(position == lane + k * LANES, lanes[k : k + 1], found)
    return jnp.sum(found, axis=1, keepdims=True)


def row_iota(rows):
    return lax.broadcasted_iota(jnp.int32, (rows, 1), 0)


def token_position(rows):
    block = rows * C // (ZH * ZL)
    row = row_iota(rows)
    zl, rest = row // (rows // ZL), row % (rows // ZL)
    return rest // block * (ZL * block) + zl * block + rest % block


def target_mask(place_ref, targets_ref, shape):
    column = to_column(targets_ref[...], token_position(shape[0]) + place_ref[1]) - place_ref[2]
    return lax.broadcasted_iota(jnp.int32, shape, 1) == column


def spans(length):
    return [pl.ds(first, min(TILE, length - first)) for first in range(0, length, TILE)]


def logits_kernel(place_ref, rows_ref, head_ref, other_ref, out_ref, kept_ref, sem):
    keep = pltpu.make_async_copy(other_ref, kept_ref, sem)
    keep.start()
    mine = place_ref[0]

    def tile(c, part_ref, span):
        rows = rows_ref[:, :, pl.ds(c, 1)].reshape(-1, rows_ref.shape[-1])
        product = lax.dot_general(rows, part_ref[span, :], (((1,), (1,)), ((), ())), preferred_element_type=F32)
        return product.reshape(out_ref.shape[:2] + (span.size,))

    for span in spans(head_ref.shape[0]):
        out_ref[:, :, span] = tile(mine, head_ref, span)
    keep.wait()
    for span in spans(head_ref.shape[0]):
        out_ref[:, :, span] += tile(C - 1 - mine, kept_ref, span)


def partial_kernel(place_ref, grad_ref, head_ref, other_ref, out_ref):
    mine = place_ref[0]
    _, _, _, rows, slice_width = out_ref.shape
    grad = grad_ref[...].reshape(X * ZL * rows, -1)
    for c, part_ref in ((mine, head_ref), (C - 1 - mine, other_ref)):
        for span in spans(slice_width):
            tile = jnp.dot(grad, part_ref[:, span], preferred_element_type=F32).astype(BF16)
            out_ref[:, :, pl.ds(c, 1), :, span] = tile.reshape(X, ZL, 1, rows, span.size)


def statistics_kernel(place_ref, parts_ref, targets_ref, logits_ref, stats_ref):
    logits = parts_ref[0]
    for y in range(1, Y):
        logits = logits + parts_ref[y]
    logits_ref[...] = logits
    top = jnp.max(logits, axis=1, keepdims=True)
    total = jnp.sum(jnp.exp(logits - top), axis=1, keepdims=True)
    mask = target_mask(place_ref, targets_ref, logits.shape)
    target_logit = jnp.sum(jnp.where(mask, logits, 0.0), axis=1, keepdims=True)
    row = row_iota(logits.shape[0])
    row = to_lanes(top + jnp.log(total), row) + to_lanes(target_logit, row + LANES // 2)
    stats_ref[...] = jnp.broadcast_to(row[None], stats_ref.shape)


def softmax_kernel(place_ref, stats_ref, logits_ref, targets_ref, upstream_ref, loss_ref, grad_ref):
    logits = logits_ref[...]
    rows = logits.shape[0]
    stats = stats_ref[:, 0, :]
    top = jnp.max(stats, axis=0, keepdims=True)
    row = row_iota(rows)
    lse = to_column(top + jnp.log(jnp.sum(jnp.exp(stats - top), axis=0, keepdims=True)), row)
    target_logit = to_column(jnp.sum(stats, axis=0, keepdims=True), row + LANES // 2)
    position = token_position(rows)
    loss_ref[...] = to_lanes(lse - target_logit, position)[:, :rows]
    weight = to_column(upstream_ref[...], position + place_ref[1])
    mask = target_mask(place_ref, targets_ref, logits.shape)
    probability = jnp.exp(logits - lse)
    grad = ((probability - jnp.where(mask, 1.0, 0.0)) * weight).astype(BF16)
    grad_ref[...] = jnp.broadcast_to(grad[None], grad_ref.shape)


def over_x_kernel(place_ref, parts_ref, out_ref):
    blocks, pieces, rows, _ = out_ref.shape
    per_half = blocks // C
    for half in range(C):
        total = 0.0
        for x in range(X):
            for zl in range(ZL):
                total = total + parts_ref[x, zl, half].astype(F32)
        for k in range(per_half * pieces):
            piece = total[k * rows : (k + 1) * rows].astype(BF16)
            out_ref[half * per_half + k // pieces, k % pieces] = piece


def pack_kernel(place_ref, rows_ref, grad_ref, out_ref):
    width, slice_width = grad_ref.shape[-1], rows_ref.shape[-1]
    out_ref[:, :, :width] = grad_ref[...]
    rows = rows_ref[:, :, pl.ds(C - 1 - place_ref[0], 1)]
    out_ref[:, :, out_ref.shape[-1] - slice_width :] = rows.reshape(Y, -1, slice_width)


def pick_kernel(place_ref, rows_ref, out_ref):
    out_ref[...] = rows_ref[:, :, pl.ds(place_ref[0], 1)].reshape(out_ref.shape)


def head_kernel(place_ref, rows_ref, grad_ref, rest_ref, out_ref):
    width, slice_width = out_ref.shape
    rows = rows_ref[...]
    rest_rows = rest_ref[:, :, rest_ref.shape[-1] - slice_width :].reshape(-1, slice_width)

    def dot(grad_ref, span, rows):
        grad = grad_ref[:, :, span].reshape(-1, span.size)
        return lax.dot_general(grad, rows, (((0,), (0,)), ((), ())), preferred_element_type=F32)

    for span in spans(width):
        out_ref[span, :] = (dot(grad_ref, span, rows) + dot(rest_ref, span, rest_rows)).astype(BF16)


def per_device(hidden, head, targets, upstream):
    width, slice_width = head.shape
    token_count = targets.shape[0]
    own = token_count // (Y * C)
    near = (X, ZL, C, own // ZL, slice_width)
    barrier = lax.optimization_barrier

    core = lax.axis_index("core")
    row_first = lax.axis_index(ROW_AXES) * own
    first_column = lax.axis_index(VOCAB_AXES) * width
    hidden, core, row_first, first_column = barrier((hidden, core, row_first, first_column))
    by_z = gather_over(hidden.reshape(-1, 2, slice_width), "zh").reshape(near[2:])

    by_z, head = barrier((by_z, head))
    head_other = lax.ppermute(head, "core", SWAP)
    copies = jnp.broadcast_to(by_z, near).reshape(-1, *near[3:])
    by_x = lax.all_to_all(copies, NEAR_AXES, 0, 0).reshape(near)

    by_x, targets, upstream, core, row_first, first_column = barrier(
        (by_x, targets, upstream, core, row_first, first_column)
    )
    place = jnp.stack([core, row_first, first_column])
    targets, upstream = targets.reshape(-1, LANES), upstream.reshape(-1, LANES)
    out = [jax.ShapeDtypeStruct((Y, own, width), F32), jax.ShapeDtypeStruct(head.shape, BF16)]
    sem = [pltpu.SemaphoreType.DMA]
    chip_logits, head_other = call(logits_kernel, out, place, by_x, head, head_other, scratch=sem, last=IN_ANY)
    chip_logits, targets, upstream = barrier((chip_logits, targets, upstream))
    parts = lax.all_to_all(chip_logits, "y", 0, 0)

    out = [jax.ShapeDtypeStruct((own, width), F32), jax.ShapeDtypeStruct((X * ZH * ZL, 1, LANES), F32)]
    logits, stats = call(statistics_kernel, out, place, parts, targets)
    stats = lax.all_to_all(stats, VOCAB_AXES, 0, 0)
    out = [jax.ShapeDtypeStruct((1, own), F32), jax.ShapeDtypeStruct((Y, own, width), BF16)]
    token_loss, grad_rows = call(softmax_kernel, out, place, stats, logits, targets, upstream)

    grad_half = lax.all_to_all(grad_rows, "y", 0, 0)

    partial = call(partial_kernel, jax.ShapeDtypeStruct(near, BF16), place, grad_half, head, head_other)
    padded = -(-width // LANES) * LANES
    out = jax.ShapeDtypeStruct((Y, own, padded + slice_width), BF16)
    rest = call(pack_kernel, out, place, by_x, grad_half, cost=PACK_COST)
    rest = lax.ppermute(rest, "core", SWAP)
    over_x = lax.all_to_all(partial.reshape(-1, *near[3:]), NEAR_AXES, 0, 0).reshape(near)
    out = jax.ShapeDtypeStruct((ZH, hidden.shape[0] // 2, 2, slice_width), BF16)
    over_x = call(over_x_kernel, out, place, over_x)
    over_x, by_x, core, grad_half, place = barrier((over_x, by_x, core, grad_half, place))
    over_z = lax.all_to_all(over_x, "zh", 0, 0)

    out = jax.ShapeDtypeStruct((Y * own, slice_width), BF16)
    rows = call(pick_kernel, out, place, by_x, cost=PACK_COST)
    out = jax.ShapeDtypeStruct((width, slice_width), BF16)
    grad_head = call(head_kernel, out, place, rows, grad_half, rest, cost=1)
    over_z, grad_head = barrier((over_z, grad_head))
    grad_hidden = jnp.sum(over_z.astype(F32), axis=0).astype(BF16).reshape(hidden.shape)
    return token_loss[0], grad_hidden, grad_head


def solution(mesh):
    torus = Mesh(mesh.devices.reshape(X, ZH, ZL, Y, C), VOCAB_AXES + ROW_AXES)
    return jax.shard_map(
        per_device,
        mesh=torus,
        in_specs=(P(VOCAB_AXES, ROW_AXES), P(VOCAB_AXES, ROW_AXES), P(), P()),
        out_specs=(P(ROW_AXES), P(VOCAB_AXES, ROW_AXES), P(VOCAB_AXES, ROW_AXES)),
        check_vma=False,
    )
```

time: 146 us -> 145 us (level)
  the two profiles are of different devices: /device:TPU:32 before, /device:TPU:8 now
where the time goes in v9:
time: 145 us; the launch traced here: 144 us
  blocking collectives  75.8 us (52%)
  waiting for transfers between devices  30.9 us (21%)
  starting transfers between devices  17.1 us (12%)
  Pallas kernels  15.2 us (10%)
  local copies, waits for them, and re-layouts  4.49 us (3%)
    all_to_all x1, blocking collectives, gather_over(): return lax.all_to_all(copies, axis, 0, 0)  29.8 us
    all_to_all x1, blocking collectives, per_device(): stats = lax.all_to_all(stats, VOCAB_AXES, 0, 0)  18.2 us
    all_to_all x1, blocking collectives, per_device(): parts = lax.all_to_all(chip_logits, 'y', 0, 0)  17.4 us
    pallas_call x8, Pallas kernels, call(): pl.pallas_call(kernel, out_shape=out_shape, in_specs=[IN_SMEM] + [IN_VMEM...  15.2 us
    all_to_all x1, waiting for transfers between devices, per_device(): by_x = lax.all_to_all(copies, NEAR_AXES, 0, 0).reshape(near)  11.4 us
    all_to_all x1, waiting for transfers between devices, per_device(): over_z = lax.all_to_all(over_x, 'zh', 0, 0)  10.4 us
    all_to_all x1, blocking collectives, per_device(): grad_half = lax.all_to_all(grad_rows, 'y', 0, 0)  10.3 us
    all_to_all x1, waiting for transfers between devices, per_device(): lax.all_to_all(partial.reshape(-1, *near[3:]), NEAR_AXES, 0, 0)  9.09 us
  transfers between devices with their start and end apart: 5, of which 3 were waited for; matrix products, arithmetic and copies ran while one was open for 0% of the time, Pallas kernels for 6%

profile of v9, /device:TPU:8, one launch (start us, length us, event | category | flops | bytes accessed | tf_op | source)
XLA Modules:
  0.0 144.5 jit_solution(4751944364120540823)
XLA Ops:
  0.6 0.0 copy-start
  0.7 0.9 broadcast_in_dim.10
  1.5 0.1 broadcast_in_dim.11
  1.6 29.8 %all_to_all.35 = bf16[8,3,2,1024]{3,2,1,0:T(2,128)(2,1)S(1)} all-to-all(bf16[8,3,2,1024]{3,2,1,0:T(2,128)(2,1)S(1)} %broadcast_in_dim.11), channel_id=1, replica_groups=mesh['x'=4,'zh'=8,'zl'=2,'y'=4,'core'=2] {'zh'}, dimensions={0} | all-to-all | bytes 196608 | tf_op jit(solution)/shard_map/all_to_all | solution.py:41
  31.5 1.0 broadcast_in_dim.12
  32.4 5.0 %all-to-all-start.1 = ((bf16[16,24,1024]{2,1,0:T(8,128)(2,1)}), bf16[16,24,1024]{2,1,0:T(8,128)(2,1)S(1)}, u32[]{:S(2)}, u32[]{:S(2)}) async-start(bf16[16,24,1024]{2,1,0:T(8,128)(2,1)} %bitcast.17), calls=%async_computation.1 | async-start | bytes 1572864 | tf_op jit(solution)/shard_map/all_to_all | solution.py:188
  37.4 0.0 copy-done
  37.4 2.3 %collective-permute-start = (bf16[1188,1024]{1,0:T(8,128)(2,1)S(1)}, bf16[1188,1024]{1,0:T(8,128)(2,1)}, u32[]{:S(2)}, u32[]{:S(2)}) collective-permute-start(bf16[1188,1024]{1,0:T(8,128)(2,1)S(1)} %copy-done), channel_id=1, source_target_pairs={{0,1},{1,0},{2,3},{3,2},{4,5},{5,4},{6,7},{7,6},{8,9},{9,8},{10,11... | collective-permute-start | bytes 7299080 | tf_op jit(solution)/shard_map/ppermute | solution.py:186
  39.8 11.4 %all-to-all-done.1 = bf16[16,24,1024]{2,1,0:T(8,128)(2,1)S(1)} async-done(((bf16[16,24,1024]{2,1,0:T(8,128)(2,1)}), bf16[16,24,1024]{2,1,0:T(8,128)(2,1)S(1)}, u32[]{:S(2)}, u32[]{:S(2)}) %all-to-all-start.1) | async-done | bytes 786464 | tf_op jit(solution)/shard_map/all_to_all | solution.py:188
  51.2 0.1 pad_add_fusion.place_ref
  51.3 0.0 copy-start.5
  51.3 0.0 collective-permute-done.other_ref
  51.3 3.3 %shard_map.67 = (f32[4,48,1188]{2,1,0:T(8,128)S(1)}, bf16[1188,1024]{1,0:T(8,128)(2,1)S(1)}) custom-call(s32[3]{0:T(128)S(1)} %pad_add_fusion.place_ref, bf16[4,2,2,24,1024]{4,3,2,1,0:T(8,128)(2,1)S(1)} %bitcast.10, bf16[1188,1024]{1,0:T(8,128)(2,1)S(1)} %copy-done, bf16[1188,1024]{1,0:T(8,128)(2,1)} %collective-permute-done.other_ref), custom_call_target="tpu_custom_call" | custom-call | flops 5652480 | bytes 5652480 | tf_op jit(solution)/shard_map/pallas_call | solution.py:27
  54.6 0.0 copy-start.6
  54.6 17.4 %all_to_all.36.parts_ref = f32[4,48,1188]{2,1,0:T(8,128)S(1)} all-to-all(f32[4,48,1188]{2,1,0:T(8,128)S(1)} %get-tuple-element.43), channel_id=1, replica_groups=mesh['x'=4,'zh'=8,'zl'=2,'y'=4,'core'=2] {'y'}, dimensions={0} | all-to-all | bytes 1824768 | tf_op jit(solution)/shard_map/all_to_all | solution.py:199
  72.0 0.0 copy-done.5
  72.0 0.8 shard_map.68
  72.9 18.2 %all_to_all.37.stats_ref = f32[64,1,128]{2,1,0:T(1,128)S(1)} all-to-all(f32[64,1,128]{2,1,0:T(1,128)S(1)} %get-tuple-element.45), channel_id=1, replica_groups=mesh['x'=4,'zh'=8,'zl'=2,'y'=4,'core'=2] {'x','zh','zl'}, dimensions={0} | all-to-all | bytes 65536 | tf_op jit(solution)/shard_map/all_to_all | solution.py:203
  91.1 0.0 copy-done.6
  91.1 1.3 shard_map.69
  92.4 10.3 %all_to_all.38.grad_ref = bf16[4,48,1188]{2,1,0:T(8,128)(2,1)S(1)} all-to-all(bf16[4,48,1188]{2,1,0:T(8,128)(2,1)S(1)} %get-tuple-element.49), channel_id=1, replica_groups=mesh['x'=4,'zh'=8,'zl'=2,'y'=4,'core'=2] {'y'}, dimensions={0} | all-to-all | bytes 912384 | tf_op jit(solution)/shard_map/all_to_all | solution.py:207
  102.7 0.0 copy-start.1
  102.7 1.7 %shard_map.70 = bf16[4,2,2,24,1024]{4,3,2,1,0:T(8,128)(2,1)S(1)} custom-call(s32[3]{0:T(128)S(1)} %pad_add_fusion.place_ref, bf16[4,48,1188]{2,1,0:T(8,128)(2,1)S(1)} %all_to_all.38.grad_ref, bf16[1188,1024]{1,0:T(8,128)(2,1)S(1)} %copy-done, bf16[1188,1024]{1,0:T(8,128)(2,1)S(1)} %get-tuple-element.50.other_ref), custom_call_target="tpu_custom_call" | custom-call | flops 5322240 | bytes 5322240 | tf_op jit(solution)/shard_map/pallas_call | solution.py:27
  104.5 0.0 copy-done.1
  104.5 0.0 copy-start.4
  104.5 0.9 copy-done.4
  105.4 4.3 %all-to-all-start.5 = ((bf16[16,24,1024]{2,1,0:T(8,128)(2,1)}), bf16[16,24,1024]{2,1,0:T(8,128)(2,1)}, u32[]{:S(2)}, u32[]{:S(2)}) async-start(bf16[16,24,1024]{2,1,0:T(8,128)(2,1)} %bitcast.13), calls=%async_computation.5 | async-start | bytes 1572864 | tf_op jit(solution)/shard_map/all_to_all | solution.py:214
  109.7 0.0 copy-start.2
  109.7 1.0 copy-done.2
  110.7 0.0 copy-start.3
  110.7 1.5 %shard_map.73 = bf16[4,48,2304]{2,1,0:T(8,128)(2,1)} custom-call(s32[3]{0:T(128)S(1)} %pad_add_fusion.place_ref, bf16[4,2,2,24,1024]{4,3,2,1,0:T(8,128)(2,1)S(1)} %bitcast.11, bf16[4,48,1188]{2,1,0:T(8,128)(2,1)S(1)} %copy-done.2), custom_call_target="tpu_custom_call" | custom-call | flops 67108864 | bytes 67108864 | tf_op jit(solution)/shard_map/pallas_call | solution.py:27
  112.2 2.1 %collective-permute-start.1 = (bf16[4,48,2304]{2,1,0:T(8,128)(2,1)}, bf16[4,48,2304]{2,1,0:T(8,128)(2,1)}, u32[]{:S(2)}, u32[]{:S(2)}) collective-permute-start(bf16[4,48,2304]{2,1,0:T(8,128)(2,1)} %shard_map.73), channel_id=1, source_target_pairs={{0,1},{1,0},{2,3},{3,2},{4,5},{5,4},{6,7},{7,6},{8,9},{9,8},{10,11... | collective-permute-start | bytes 2654216 | tf_op jit(solution)/shard_map/ppermute | solution.py:213
  114.3 9.1 %all-to-all-done.5 = bf16[16,24,1024]{2,1,0:T(8,128)(2,1)} async-done(((bf16[16,24,1024]{2,1,0:T(8,128)(2,1)}), bf16[16,24,1024]{2,1,0:T(8,128)(2,1)}, u32[]{:S(2)}, u32[]{:S(2)}) %all-to-all-start.5) | async-done | bytes 786464 | tf_op jit(solution)/shard_map/all_to_all | solution.py:214
  123.4 1.9 %shard_map.71 = bf16[8,3,2,1024]{3,2,1,0:T(2,128)(2,1)} custom-call(s32[3]{0:T(128)S(1)} %pad_add_fusion.place_ref, bf16[4,2,2,24,1024]{4,3,2,1,0:T(8,128)(2,1)} %bitcast.9.parts_ref), custom_call_target="tpu_custom_call" | custom-call | flops 786432 | bytes 786432 | tf_op jit(solution)/shard_map/pallas_call | solution.py:27
  125.3 3.4 %all-to-all-start.6 = ((bf16[8,3,2,1024]{3,2,1,0:T(2,128)(2,1)}), bf16[8,3,2,1024]{3,2,1,0:T(2,128)(2,1)S(1)}, u32[]{:S(2)}, u32[]{:S(2)}) async-start(bf16[8,3,2,1024]{3,2,1,0:T(2,128)(2,1)} %shard_map.71), calls=%async_computation.6 | async-start | bytes 196608 | tf_op jit(solution)/shard_map/all_to_all | solution.py:218
  128.7 0.6 shard_map.72.rows_ref
  129.3 0.0 collective-permute-done.1.rest_ref
  129.3 0.0 copy-done.3
  129.3 4.1 %shard_map.74 = bf16[1188,1024]{1,0:T(8,128)(2,1)} custom-call(s32[3]{0:T(128)S(1)} %pad_add_fusion.place_ref, bf16[192,1024]{1,0:T(8,128)(2,1)S(1)} %shard_map.72.rows_ref, bf16[4,48,1188]{2,1,0:T(8,128)(2,1)S(1)} %copy-done.3, bf16[4,48,2304]{2,1,0:T(8,128)(2,1)} %collective-permute-done.1.rest_ref), custom_call_target="tpu_custom_call" | custom-call | flops 1 | bytes 1 | tf_op jit(solution)/shard_map/pallas_call | solution.py:27
  133.4 10.4 %all-to-all-done.6 = bf16[8,3,2,1024]{3,2,1,0:T(2,128)(2,1)S(1)} async-done(((bf16[8,3,2,1024]{3,2,1,0:T(2,128)(2,1)}), bf16[8,3,2,1024]{3,2,1,0:T(2,128)(2,1)S(1)}, u32[]{:S(2)}, u32[]{:S(2)}) %all-to-all-start.6) | async-done | bytes 98336 | tf_op jit(solution)/shard_map/all_to_all | solution.py:218
  143.8 0.1 reduce_sum.12
  143.8 0.6 reshape.38
  (1 shorter events, 0.0 us)
Async XLA Ops:
  0.6 36.8 %copy-start = (bf16[1188,1024]{1,0:T(8,128)(2,1)S(1)}, bf16[1188,1024]{1,0:T(8,128)(2,1)}, u32[]{:S(2)}) copy-start(bf16[1188,1024]{1,0:T(8,128)(2,1)} %head_ref.1) | copy-start | bytes 7299076
  32.4 18.8 %all-to-all-start.1 = ((bf16[16,24,1024]{2,1,0:T(8,128)(2,1)}), bf16[16,24,1024]{2,1,0:T(8,128)(2,1)S(1)}, u32[]{:S(2)}, u32[]{:S(2)}) async-start(bf16[16,24,1024]{2,1,0:T(8,128)(2,1)} %bitcast.17), calls=%async_computation.1 | async-start | bytes 1572864 | tf_op jit(solution)/shard_map/all_to_all | solution.py:188
  37.4 13.8 %collective-permute-start = (bf16[1188,1024]{1,0:T(8,128)(2,1)S(1)}, bf16[1188,1024]{1,0:T(8,128)(2,1)}, u32[]{:S(2)}, u32[]{:S(2)}) collective-permute-start(bf16[1188,1024]{1,0:T(8,128)(2,1)S(1)} %copy-done), channel_id=1, source_target_pairs={{0,1},{1,0},{2,3},{3,2},{4,5},{5,4},{6,7},{7,6},{8,9},{9,8},{10,11... | collective-permute-start | bytes 7299080 | tf_op jit(solution)/shard_map/ppermute | solution.py:186
  51.3 20.8 %copy-start.5 = (s32[384]{0:T(512)S(1)}, s32[384]{0:T(512)}, u32[]{:S(2)}) copy-start(s32[384]{0:T(512)} %param.6) | copy-start | bytes 4612
  54.6 36.5 %copy-start.6 = (f32[384]{0:T(512)S(1)}, f32[384]{0:T(512)}, u32[]{:S(2)}) copy-start(f32[384]{0:T(512)} %param.7) | copy-start | bytes 4612
  102.7 1.7 %copy-start.1 = (bf16[4,48,1188]{2,1,0:T(8,128)(2,1)}, bf16[4,48,1188]{2,1,0:T(8,128)(2,1)S(1)}, u32[]{:S(2)}) copy-start(bf16[4,48,1188]{2,1,0:T(8,128)(2,1)S(1)} %all_to_all.38.grad_ref) | copy-start | bytes 1368580
  104.5 0.9 copy-start.4
  105.4 18.1 %all-to-all-start.5 = ((bf16[16,24,1024]{2,1,0:T(8,128)(2,1)}), bf16[16,24,1024]{2,1,0:T(8,128)(2,1)}, u32[]{:S(2)}, u32[]{:S(2)}) async-start(bf16[16,24,1024]{2,1,0:T(8,128)(2,1)} %bitcast.13), calls=%async_computation.5 | async-start | bytes 1572864 | tf_op jit(solution)/shard_map/all_to_all | solution.py:214
  109.7 1.0 copy-start.2
  110.7 18.6 %copy-start.3 = (bf16[4,48,1188]{2,1,0:T(8,128)(2,1)S(1)}, bf16[4,48,1188]{2,1,0:T(8,128)(2,1)}, u32[]{:S(2)}) copy-start(bf16[4,48,1188]{2,1,0:T(8,128)(2,1)} %copy-done.1) | copy-start | bytes 1368580
  112.2 17.1 %collective-permute-start.1 = (bf16[4,48,2304]{2,1,0:T(8,128)(2,1)}, bf16[4,48,2304]{2,1,0:T(8,128)(2,1)}, u32[]{:S(2)}, u32[]{:S(2)}) collective-permute-start(bf16[4,48,2304]{2,1,0:T(8,128)(2,1)} %shard_map.73), channel_id=1, source_target_pairs={{0,1},{1,0},{2,3},{3,2},{4,5},{5,4},{6,7},{7,6},{8,9},{9,8},{10,11... | collective-permute-start | bytes 2654216 | tf_op jit(solution)/shard_map/ppermute | solution.py:213
  125.3 18.4 %all-to-all-start.6 = ((bf16[8,3,2,1024]{3,2,1,0:T(2,128)(2,1)}), bf16[8,3,2,1024]{3,2,1,0:T(2,128)(2,1)S(1)}, u32[]{:S(2)}, u32[]{:S(2)}) async-start(bf16[8,3,2,1024]{3,2,1,0:T(2,128)(2,1)} %shard_map.71), calls=%async_computation.6 | async-start | bytes 196608 | tf_op jit(solution)/shard_map/all_to_all | solution.py:218

commit v10 on v9

--- a/solution.py
+++ b/solution.py
@@ -21,15 +21,16 @@
 IN_SMEM = pl.BlockSpec(memory_space=pltpu.SMEM)
 
 
-def call(kernel, out_shape, place, *operands, cost=None, scratch=(), last=IN_VMEM):
+def call(kernel, out_shape, place, *operands, cost=None, scratch=(), last=IN_VMEM, result=IN_VMEM, aliases=None):
     many = isinstance(out_shape, list)
     moved = cost or sum(a.size * a.dtype.itemsize for a in operands)
     return pl.pallas_call(
         kernel,
         out_shape=out_shape,
         in_specs=[IN_SMEM] + [IN_VMEM] * (len(operands) - 1) + [last],
-        out_specs=[IN_VMEM] * len(out_shape) if many else IN_VMEM,
+        out_specs=[IN_VMEM] * len(out_shape) if many else result,
         scratch_shapes=scratch,
+        input_output_aliases=aliases or {},
         cost_estimate=pl.CostEstimate(flops=moved, bytes_accessed=moved, transcendentals=0),
         compiler_params=pltpu.CompilerParams(vmem_limit_bytes=8 * 2**20),
     )(place, *operands)
@@ -91,14 +92,19 @@
         out_ref[:, :, span] += tile(C - 1 - mine, kept_ref, span)
 
 
-def partial_kernel(place_ref, grad_ref, head_ref, other_ref, out_ref):
+def partial_kernel(place_ref, grad_ref, head_ref, other_ref, spent_ref, out_ref, held_ref, sems):
     mine = place_ref[0]
     _, _, _, rows, slice_width = out_ref.shape
     grad = grad_ref[...].reshape(X * ZL * rows, -1)
-    for c, part_ref in ((mine, head_ref), (C - 1 - mine, other_ref)):
+    copies = []
+    for k, (c, part_ref) in enumerate(((mine, head_ref), (C - 1 - mine, other_ref))):
         for span in spans(slice_width):
             tile = jnp.dot(grad, part_ref[:, span], preferred_element_type=F32).astype(BF16)
-            out_ref[:, :, pl.ds(c, 1), :, span] = tile.reshape(X, ZL, 1, rows, span.size)
+            held_ref[k, :, :, :, span] = tile.reshape(X, ZL, rows, span.size)
+        copies.append(pltpu.make_async_copy(held_ref.at[k], out_ref.at[:, :, c], sems.at[k]))
+        copies[-1].start()
+    for copy in copies:
+        copy.wait()
 
 
 def statistics_kernel(place_ref, parts_ref, targets_ref, logits_ref, stats_ref):
@@ -206,7 +212,12 @@
 
     grad_half = lax.all_to_all(grad_rows, "y", 0, 0)
 
-    partial = call(partial_kernel, jax.ShapeDtypeStruct(near, BF16), place, grad_half, head, head_other)
+    held = [pltpu.VMEM((C, X, ZL, *near[3:]), BF16), pltpu.SemaphoreType.DMA((C,))]
+    out = jax.ShapeDtypeStruct(near, BF16)
+    partial = call(
+        partial_kernel, out, place, grad_half, head, head_other, copies.reshape(near),
+        scratch=held, last=IN_ANY, result=IN_ANY, aliases={4: 0},
+    )
     padded = -(-width // LANES) * LANES
     out = jax.ShapeDtypeStruct((Y, own, padded + slice_width), BF16)
     rest = call(pack_kernel, out, place, by_x, grad_half, cost=PACK_COST)

time: 145 us -> 144 us (level)
  transfers between devices with their start and end apart: 5 -> 5, of which waited for: 3 -> 3; matrix products, arithmetic and copies ran while one was open for 0% -> 0% of each run, Pallas kernels for 6% -> 5%
where the time goes in v10:
time: 144 us; the launch traced here: 143 us
  blocking collectives  75.8 us (53%)
  waiting for transfers between devices  31.4 us (22%)
  starting transfers between devices  16.5 us (11%)
  Pallas kernels  14.8 us (10%)
  local copies, waits for them, and re-layouts  3.62 us (3%)
    all_to_all x1, blocking collectives, gather_over(): return lax.all_to_all(copies, axis, 0, 0)  29.8 us
    all_to_all x1, blocking collectives, per_device(): stats = lax.all_to_all(stats, VOCAB_AXES, 0, 0)  18.2 us
    all_to_all x1, blocking collectives, per_device(): parts = lax.all_to_all(chip_logits, 'y', 0, 0)  17.4 us
    pallas_call x8, Pallas kernels, call(): pl.pallas_call(kernel, out_shape=out_shape, in_specs=[IN_SMEM] + [IN_VMEM...  14.8 us
    all_to_all x1, waiting for transfers between devices, per_device(): by_x = lax.all_to_all(copies, NEAR_AXES, 0, 0).reshape(near)  11.4 us
    all_to_all x1, waiting for transfers between devices, per_device(): over_z = lax.all_to_all(over_x, 'zh', 0, 0)  11 us
    all_to_all x1, blocking collectives, per_device(): grad_half = lax.all_to_all(grad_rows, 'y', 0, 0)  10.3 us
    all_to_all x1, waiting for transfers between devices, per_device(): lax.all_to_all(partial.reshape(-1, *near[3:]), NEAR_AXES, 0, 0)  8.99 us
  transfers between devices with their start and end apart: 5, of which 3 were waited for; matrix products, arithmetic and copies ran while one was open for 0% of the time, Pallas kernels for 5%

profile of v10, /device:TPU:8, one launch (start us, length us, event | category | flops | bytes accessed | tf_op | source)
XLA Modules:
  0.0 143.1 jit_solution(12231191639384664802)
XLA Ops:
  0.6 0.0 copy-start
  0.7 0.9 broadcast_in_dim.10
  1.5 0.1 broadcast_in_dim.11
  1.6 29.8 %all_to_all.35 = bf16[8,3,2,1024]{3,2,1,0:T(2,128)(2,1)S(1)} all-to-all(bf16[8,3,2,1024]{3,2,1,0:T(2,128)(2,1)S(1)} %broadcast_in_dim.11), channel_id=1, replica_groups=mesh['x'=4,'zh'=8,'zl'=2,'y'=4,'core'=2] {'zh'}, dimensions={0} | all-to-all | bytes 196608 | tf_op jit(solution)/shard_map/all_to_all | solution.py:42
  31.5 1.0 broadcast_in_dim.12.spent_ref
  32.4 5.0 %all-to-all-start.1 = ((bf16[16,24,1024]{2,1,0:T(8,128)(2,1)}), bf16[16,24,1024]{2,1,0:T(8,128)(2,1)S(1)}, u32[]{:S(2)}, u32[]{:S(2)}) async-start(bf16[16,24,1024]{2,1,0:T(8,128)(2,1)} %bitcast), calls=%async_computation.1 | async-start | bytes 1572864 | tf_op jit(solution)/shard_map/all_to_all | solution.py:194
  37.4 0.0 copy-done
  37.4 2.3 %collective-permute-start = (bf16[1188,1024]{1,0:T(8,128)(2,1)S(1)}, bf16[1188,1024]{1,0:T(8,128)(2,1)}, u32[]{:S(2)}, u32[]{:S(2)}) collective-permute-start(bf16[1188,1024]{1,0:T(8,128)(2,1)S(1)} %copy-done), channel_id=1, source_target_pairs={{0,1},{1,0},{2,3},{3,2},{4,5},{5,4},{6,7},{7,6},{8,9},{9,8},{10,11... | collective-permute-start | bytes 7299080 | tf_op jit(solution)/shard_map/ppermute | solution.py:192
  39.8 11.4 %all-to-all-done.1 = bf16[16,24,1024]{2,1,0:T(8,128)(2,1)S(1)} async-done(((bf16[16,24,1024]{2,1,0:T(8,128)(2,1)}), bf16[16,24,1024]{2,1,0:T(8,128)(2,1)S(1)}, u32[]{:S(2)}, u32[]{:S(2)}) %all-to-all-start.1) | async-done | bytes 786464 | tf_op jit(solution)/shard_map/all_to_all | solution.py:194
  51.2 0.1 pad_add_fusion.place_ref
  51.3 0.0 copy-start.4
  51.3 0.0 collective-permute-done.other_ref
  51.3 3.3 %shard_map.67 = (f32[4,48,1188]{2,1,0:T(8,128)S(1)}, bf16[1188,1024]{1,0:T(8,128)(2,1)S(1)}) custom-call(s32[3]{0:T(128)S(1)} %pad_add_fusion.place_ref, bf16[4,2,2,24,1024]{4,3,2,1,0:T(8,128)(2,1)S(1)} %bitcast.10, bf16[1188,1024]{1,0:T(8,128)(2,1)S(1)} %copy-done, bf16[1188,1024]{1,0:T(8,128)(2,1)} %collective-permute-done.other_ref), custom_call_target="tpu_custom_call" | custom-call | flops 5652480 | bytes 5652480 | tf_op jit(solution)/shard_map/pallas_call | solution.py:27
  54.6 0.0 copy-start.5
  54.6 17.4 %all_to_all.36.parts_ref = f32[4,48,1188]{2,1,0:T(8,128)S(1)} all-to-all(f32[4,48,1188]{2,1,0:T(8,128)S(1)} %get-tuple-element.43), channel_id=1, replica_groups=mesh['x'=4,'zh'=8,'zl'=2,'y'=4,'core'=2] {'y'}, dimensions={0} | all-to-all | bytes 1824768 | tf_op jit(solution)/shard_map/all_to_all | solution.py:205
  72.0 0.0 copy-done.4
  72.0 0.8 shard_map.68
  72.9 18.2 %all_to_all.37.stats_ref = f32[64,1,128]{2,1,0:T(1,128)S(1)} all-to-all(f32[64,1,128]{2,1,0:T(1,128)S(1)} %get-tuple-element.45), channel_id=1, replica_groups=mesh['x'=4,'zh'=8,'zl'=2,'y'=4,'core'=2] {'x','zh','zl'}, dimensions={0} | all-to-all | bytes 65536 | tf_op jit(solution)/shard_map/all_to_all | solution.py:209
  91.1 0.0 copy-done.5
  91.1 1.3 shard_map.69
  92.4 10.3 %all_to_all.38.grad_ref = bf16[4,48,1188]{2,1,0:T(8,128)(2,1)S(1)} all-to-all(bf16[4,48,1188]{2,1,0:T(8,128)(2,1)S(1)} %get-tuple-element.49), channel_id=1, replica_groups=mesh['x'=4,'zh'=8,'zl'=2,'y'=4,'core'=2] {'y'}, dimensions={0} | all-to-all | bytes 912384 | tf_op jit(solution)/shard_map/all_to_all | solution.py:213
  102.7 0.0 copy-start.1
  102.7 2.6 %shard_map.70 = bf16[4,2,2,24,1024]{4,3,2,1,0:T(8,128)(2,1)} custom-call(s32[3]{0:T(128)S(1)} %pad_add_fusion.place_ref, bf16[4,48,1188]{2,1,0:T(8,128)(2,1)S(1)} %all_to_all.38.grad_ref, bf16[1188,1024]{1,0:T(8,128)(2,1)S(1)} %copy-done, bf16[1188,1024]{1,0:T(8,128)(2,1)S(1)} %get-tuple-element.50.other_ref, ...), custom_call_target="tpu_custom_call", output_to_operand_aliasing={{}: (4, {})} | custom-call | flops 6108672 | bytes 6108672 | tf_op jit(solution)/shard_map/pallas_call | solution.py:27
  105.3 0.0 copy-done.1
  105.3 3.6 %all-to-all-start.5 = ((bf16[16,24,1024]{2,1,0:T(8,128)(2,1)}), bf16[16,24,1024]{2,1,0:T(8,128)(2,1)S(1)}, u32[]{:S(2)}, u32[]{:S(2)}) async-start(bf16[16,24,1024]{2,1,0:T(8,128)(2,1)} %bitcast.8), calls=%async_computation.5 | async-start | bytes 1572864 | tf_op jit(solution)/shard_map/all_to_all | solution.py:225
  108.9 0.0 copy-start.2
  108.9 1.0 copy-done.2
  110.0 0.0 copy-start.3
  110.0 1.5 %shard_map.73 = bf16[4,48,2304]{2,1,0:T(8,128)(2,1)} custom-call(s32[3]{0:T(128)S(1)} %pad_add_fusion.place_ref, bf16[4,2,2,24,1024]{4,3,2,1,0:T(8,128)(2,1)S(1)} %bitcast.11, bf16[4,48,1188]{2,1,0:T(8,128)(2,1)S(1)} %copy-done.2), custom_call_target="tpu_custom_call" | custom-call | flops 67108864 | bytes 67108864 | tf_op jit(solution)/shard_map/pallas_call | solution.py:27
  111.5 2.2 %collective-permute-start.1 = (bf16[4,48,2304]{2,1,0:T(8,128)(2,1)}, bf16[4,48,2304]{2,1,0:T(8,128)(2,1)S(1)}, u32[]{:S(2)}, u32[]{:S(2)}) collective-permute-start(bf16[4,48,2304]{2,1,0:T(8,128)(2,1)} %shard_map.73), channel_id=1, source_target_pairs={{0,1},{1,0},{2,3},{3,2},{4,5},{5,4},{6,7},{7,6},{8,9},{9,8},{10,11... | collective-permute-start | bytes 2654216 | tf_op jit(solution)/shard_map/ppermute | solution.py:224
  113.7 9.0 %all-to-all-done.5 = bf16[16,24,1024]{2,1,0:T(8,128)(2,1)S(1)} async-done(((bf16[16,24,1024]{2,1,0:T(8,128)(2,1)}), bf16[16,24,1024]{2,1,0:T(8,128)(2,1)S(1)}, u32[]{:S(2)}, u32[]{:S(2)}) %all-to-all-start.5) | async-done | bytes 786464 | tf_op jit(solution)/shard_map/all_to_all | solution.py:225
  122.7 1.3 shard_map.71
  123.9 3.4 %all-to-all-start.6 = ((bf16[8,3,2,1024]{3,2,1,0:T(2,128)(2,1)}), bf16[8,3,2,1024]{3,2,1,0:T(2,128)(2,1)S(1)}, u32[]{:S(2)}, u32[]{:S(2)}) async-start(bf16[8,3,2,1024]{3,2,1,0:T(2,128)(2,1)} %shard_map.71), calls=%async_computation.6 | async-start | bytes 196608 | tf_op jit(solution)/shard_map/all_to_all | solution.py:229
  127.3 0.6 shard_map.72.rows_ref
  127.9 0.0 collective-permute-done.1.rest_ref
  127.9 0.0 copy-done.3
  127.9 3.4 %shard_map.74 = bf16[1188,1024]{1,0:T(8,128)(2,1)} custom-call(s32[3]{0:T(128)S(1)} %pad_add_fusion.place_ref, bf16[192,1024]{1,0:T(8,128)(2,1)S(1)} %shard_map.72.rows_ref, bf16[4,48,1188]{2,1,0:T(8,128)(2,1)S(1)} %copy-done.3, bf16[4,48,2304]{2,1,0:T(8,128)(2,1)S(1)} %collective-permute-done.1.rest_ref), custom_call_target="tpu_custom_call" | custom-call | flops 1 | bytes 1 | tf_op jit(solution)/shard_map/pallas_call | solution.py:27
  131.3 11.0 %all-to-all-done.6 = bf16[8,3,2,1024]{3,2,1,0:T(2,128)(2,1)S(1)} async-done(((bf16[8,3,2,1024]{3,2,1,0:T(2,128)(2,1)}), bf16[8,3,2,1024]{3,2,1,0:T(2,128)(2,1)S(1)}, u32[]{:S(2)}, u32[]{:S(2)}) %all-to-all-start.6) | async-done | bytes 98336 | tf_op jit(solution)/shard_map/all_to_all | solution.py:229
  142.4 0.1 reduce_sum.12
  142.5 0.6 reshape.38
  (1 shorter events, 0.0 us)
Async XLA Ops:
  0.6 36.8 %copy-start = (bf16[1188,1024]{1,0:T(8,128)(2,1)S(1)}, bf16[1188,1024]{1,0:T(8,128)(2,1)}, u32[]{:S(2)}) copy-start(bf16[1188,1024]{1,0:T(8,128)(2,1)} %head_ref.1) | copy-start | bytes 7299076
  32.4 18.8 %all-to-all-start.1 = ((bf16[16,24,1024]{2,1,0:T(8,128)(2,1)}), bf16[16,24,1024]{2,1,0:T(8,128)(2,1)S(1)}, u32[]{:S(2)}, u32[]{:S(2)}) async-start(bf16[16,24,1024]{2,1,0:T(8,128)(2,1)} %bitcast), calls=%async_computation.1 | async-start | bytes 1572864 | tf_op jit(solution)/shard_map/all_to_all | solution.py:194
  37.4 13.8 %collective-permute-start = (bf16[1188,1024]{1,0:T(8,128)(2,1)S(1)}, bf16[1188,1024]{1,0:T(8,128)(2,1)}, u32[]{:S(2)}, u32[]{:S(2)}) collective-permute-start(bf16[1188,1024]{1,0:T(8,128)(2,1)S(1)} %copy-done), channel_id=1, source_target_pairs={{0,1},{1,0},{2,3},{3,2},{4,5},{5,4},{6,7},{7,6},{8,9},{9,8},{10,11... | collective-permute-start | bytes 7299080 | tf_op jit(solution)/shard_map/ppermute | solution.py:192
  51.3 20.8 %copy-start.4 = (s32[384]{0:T(512)S(1)}, s32[384]{0:T(512)}, u32[]{:S(2)}) copy-start(s32[384]{0:T(512)} %param.6) | copy-start | bytes 4612
  54.6 36.5 %copy-start.5 = (f32[384]{0:T(512)S(1)}, f32[384]{0:T(512)}, u32[]{:S(2)}) copy-start(f32[384]{0:T(512)} %param.7) | copy-start | bytes 4612
  102.7 2.6 %copy-start.1 = (bf16[4,48,1188]{2,1,0:T(8,128)(2,1)}, bf16[4,48,1188]{2,1,0:T(8,128)(2,1)S(1)}, u32[]{:S(2)}) copy-start(bf16[4,48,1188]{2,1,0:T(8,128)(2,1)S(1)} %all_to_all.38.grad_ref) | copy-start | bytes 1368580
  105.3 17.4 %all-to-all-start.5 = ((bf16[16,24,1024]{2,1,0:T(8,128)(2,1)}), bf16[16,24,1024]{2,1,0:T(8,128)(2,1)S(1)}, u32[]{:S(2)}, u32[]{:S(2)}) async-start(bf16[16,24,1024]{2,1,0:T(8,128)(2,1)} %bitcast.8), calls=%async_computation.5 | async-start | bytes 1572864 | tf_op jit(solution)/shard_map/all_to_all | solution.py:225
  108.9 1.0 copy-start.2
  110.0 17.9 %copy-start.3 = (bf16[4,48,1188]{2,1,0:T(8,128)(2,1)S(1)}, bf16[4,48,1188]{2,1,0:T(8,128)(2,1)}, u32[]{:S(2)}) copy-start(bf16[4,48,1188]{2,1,0:T(8,128)(2,1)} %copy-done.1) | copy-start | bytes 1368580
  111.5 16.4 %collective-permute-start.1 = (bf16[4,48,2304]{2,1,0:T(8,128)(2,1)}, bf16[4,48,2304]{2,1,0:T(8,128)(2,1)S(1)}, u32[]{:S(2)}, u32[]{:S(2)}) collective-permute-start(bf16[4,48,2304]{2,1,0:T(8,128)(2,1)} %shard_map.73), channel_id=1, source_target_pairs={{0,1},{1,0},{2,3},{3,2},{4,5},{5,4},{6,7},{7,6},{8,9},{9,8},{10,11... | collective-permute-start | bytes 2654216 | tf_op jit(solution)/shard_map/ppermute | solution.py:224
  123.9 18.4 %all-to-all-start.6 = ((bf16[8,3,2,1024]{3,2,1,0:T(2,128)(2,1)}), bf16[8,3,2,1024]{3,2,1,0:T(2,128)(2,1)S(1)}, u32[]{:S(2)}, u32[]{:S(2)}) async-start(bf16[8,3,2,1024]{3,2,1,0:T(2,128)(2,1)} %shard_map.71), calls=%async_computation.6 | async-start | bytes 196608 | tf_op jit(solution)/shard_map/all_to_all | solution.py:229

commit v11 on v10

--- a/solution.py
+++ b/solution.py
@@ -80,16 +80,22 @@
     keep.start()
     mine = place_ref[0]
 
+    width = head_ref.shape[0]
+
     def tile(c, part_ref, span):
         rows = rows_ref[:, :, pl.ds(c, 1)].reshape(-1, rows_ref.shape[-1])
         product = lax.dot_general(rows, part_ref[span, :], (((1,), (1,)), ((), ())), preferred_element_type=F32)
-        return product.reshape(out_ref.shape[:2] + (span.size,))
-
-    for span in spans(head_ref.shape[0]):
-        out_ref[:, :, span] = tile(mine, head_ref, span)
+        return product.reshape(Y, ZL, -1, span.size)
+
+    for span in spans(width):
+        product = tile(mine, head_ref, span)
+        for zl in range(ZL):
+            out_ref[:, :, pl.ds(zl * width + span.start, span.size)] = product[:, zl]
     keep.wait()
-    for span in spans(head_ref.shape[0]):
-        out_ref[:, :, span] += tile(C - 1 - mine, kept_ref, span)
+    for span in spans(width):
+        product = tile(C - 1 - mine, kept_ref, span)
+        for zl in range(ZL):
+            out_ref[:, :, pl.ds(zl * width + span.start, span.size)] += product[:, zl]
 
 
 def partial_kernel(place_ref, grad_ref, head_ref, other_ref, spent_ref, out_ref, held_ref, sems):
@@ -111,6 +117,8 @@
     logits = parts_ref[0]
     for y in range(1, Y):
         logits = logits + parts_ref[y]
+    width = logits_ref.shape[1]
+    logits = jnp.concatenate([logits[:, zl * width : (zl + 1) * width] for zl in range(ZL)], axis=0)
     logits_ref[...] = logits
     top = jnp.max(logits, axis=1, keepdims=True)
     total = jnp.sum(jnp.exp(logits - top), axis=1, keepdims=True)
@@ -198,7 +206,7 @@
     )
     place = jnp.stack([core, row_first, first_column])
     targets, upstream = targets.reshape(-1, LANES), upstream.reshape(-1, LANES)
-    out = [jax.ShapeDtypeStruct((Y, own, width), F32), jax.ShapeDtypeStruct(head.shape, BF16)]
+    out = [jax.ShapeDtypeStruct((Y, own // ZL, ZL * width), F32), jax.ShapeDtypeStruct(head.shape, BF16)]
     sem = [pltpu.SemaphoreType.DMA]
     chip_logits, head_other = call(logits_kernel, out, place, by_x, head, head_other, scratch=sem, last=IN_ANY)
     chip_logits, targets, upstream = barrier((chip_logits, targets, upstream))

time: 144 us -> 143 us (level)
  no operation moved by 1% of the time
where the time goes in v11:
time: 143 us
  blocking collectives  75.3 us (53%)
  waiting for transfers between devices  31.4 us (22%)
  starting transfers between devices  16.5 us (12%)
  Pallas kernels  14.9 us (10%)
  local copies, waits for them, and re-layouts  3.62 us (3%)
    all_to_all x1, blocking collectives, gather_over(): return lax.all_to_all(copies, axis, 0, 0)  29.8 us
    all_to_all x1, blocking collectives, per_device(): stats = lax.all_to_all(stats, VOCAB_AXES, 0, 0)  18.2 us
    all_to_all x1, blocking collectives, per_device(): parts = lax.all_to_all(chip_logits, 'y', 0, 0)  16.9 us
    pallas_call x8, Pallas kernels, call(): pl.pallas_call(kernel, out_shape=out_shape, in_specs=[IN_SMEM] + [IN_VMEM...  14.9 us
    all_to_all x1, waiting for transfers between devices, per_device(): by_x = lax.all_to_all(copies, NEAR_AXES, 0, 0).reshape(near)  11.4 us
    all_to_all x1, waiting for transfers between devices, per_device(): over_z = lax.all_to_all(over_x, 'zh', 0, 0)  11 us
    all_to_all x1, blocking collectives, per_device(): grad_half = lax.all_to_all(grad_rows, 'y', 0, 0)  10.3 us
    all_to_all x1, waiting for transfers between devices, per_device(): lax.all_to_all(partial.reshape(-1, *near[3:]), NEAR_AXES, 0, 0)  8.99 us
  transfers between devices with their start and end apart: 5, of which 3 were waited for; matrix products, arithmetic and copies ran while one was open for 0% of the time, Pallas kernels for 5%

profile of v11, /device:TPU:8, one launch (start us, length us, event | category | flops | bytes accessed | tf_op | source)
XLA Modules:
  0.0 142.7 jit_solution(15353083140718423601)
XLA Ops:
  0.6 0.0 copy-start
  0.7 0.9 broadcast_in_dim.10
  1.5 0.1 broadcast_in_dim.11
  1.6 29.8 %all_to_all.35 = bf16[8,3,2,1024]{3,2,1,0:T(2,128)(2,1)S(1)} all-to-all(bf16[8,3,2,1024]{3,2,1,0:T(2,128)(2,1)S(1)} %broadcast_in_dim.11), channel_id=1, replica_groups=mesh['x'=4,'zh'=8,'zl'=2,'y'=4,'core'=2] {'zh'}, dimensions={0} | all-to-all | bytes 196608 | tf_op jit(solution)/shard_map/all_to_all | solution.py:42
  31.5 1.0 broadcast_in_dim.12.spent_ref
  32.4 5.0 %all-to-all-start.1 = ((bf16[16,24,1024]{2,1,0:T(8,128)(2,1)}), bf16[16,24,1024]{2,1,0:T(8,128)(2,1)S(1)}, u32[]{:S(2)}, u32[]{:S(2)}) async-start(bf16[16,24,1024]{2,1,0:T(8,128)(2,1)} %bitcast), calls=%async_computation.1 | async-start | bytes 1572864 | tf_op jit(solution)/shard_map/all_to_all | solution.py:202
  37.4 0.0 copy-done
  37.4 2.3 %collective-permute-start = (bf16[1188,1024]{1,0:T(8,128)(2,1)S(1)}, bf16[1188,1024]{1,0:T(8,128)(2,1)}, u32[]{:S(2)}, u32[]{:S(2)}) collective-permute-start(bf16[1188,1024]{1,0:T(8,128)(2,1)S(1)} %copy-done), channel_id=1, source_target_pairs={{0,1},{1,0},{2,3},{3,2},{4,5},{5,4},{6,7},{7,6},{8,9},{9,8},{10,11... | collective-permute-start | bytes 7299080 | tf_op jit(solution)/shard_map/ppermute | solution.py:200
  39.8 11.4 %all-to-all-done.1 = bf16[16,24,1024]{2,1,0:T(8,128)(2,1)S(1)} async-done(((bf16[16,24,1024]{2,1,0:T(8,128)(2,1)}), bf16[16,24,1024]{2,1,0:T(8,128)(2,1)S(1)}, u32[]{:S(2)}, u32[]{:S(2)}) %all-to-all-start.1) | async-done | bytes 786464 | tf_op jit(solution)/shard_map/all_to_all | solution.py:202
  51.2 0.1 pad_add_fusion.place_ref
  51.3 0.0 copy-start.4
  51.3 0.0 collective-permute-done.other_ref
  51.3 3.4 %shard_map.67 = (f32[4,24,2376]{2,1,0:T(8,128)S(1)}, bf16[1188,1024]{1,0:T(8,128)(2,1)S(1)}) custom-call(s32[3]{0:T(128)S(1)} %pad_add_fusion.place_ref, bf16[4,2,2,24,1024]{4,3,2,1,0:T(8,128)(2,1)S(1)} %bitcast.10, bf16[1188,1024]{1,0:T(8,128)(2,1)S(1)} %copy-done, bf16[1188,1024]{1,0:T(8,128)(2,1)} %collective-permute-done.other_ref), custom_call_target="tpu_custom_call" | custom-call | flops 5652480 | bytes 5652480 | tf_op jit(solution)/shard_map/pallas_call | solution.py:27
  54.7 0.0 copy-start.5
  54.7 16.9 %all_to_all.36.parts_ref = f32[4,24,2376]{2,1,0:T(8,128)S(1)} all-to-all(f32[4,24,2376]{2,1,0:T(8,128)S(1)} %get-tuple-element.43), channel_id=1, replica_groups=mesh['x'=4,'zh'=8,'zl'=2,'y'=4,'core'=2] {'y'}, dimensions={0} | all-to-all | bytes 1824768 | tf_op jit(solution)/shard_map/all_to_all | solution.py:213
  71.6 0.0 copy-done.4
  71.6 0.9 shard_map.68
  72.5 18.2 %all_to_all.37.stats_ref = f32[64,1,128]{2,1,0:T(1,128)S(1)} all-to-all(f32[64,1,128]{2,1,0:T(1,128)S(1)} %get-tuple-element.45), channel_id=1, replica_groups=mesh['x'=4,'zh'=8,'zl'=2,'y'=4,'core'=2] {'x','zh','zl'}, dimensions={0} | all-to-all | bytes 65536 | tf_op jit(solution)/shard_map/all_to_all | solution.py:217
  90.7 0.0 copy-done.5
  90.7 1.3 shard_map.69
  92.0 10.3 %all_to_all.38.grad_ref = bf16[4,48,1188]{2,1,0:T(8,128)(2,1)S(1)} all-to-all(bf16[4,48,1188]{2,1,0:T(8,128)(2,1)S(1)} %get-tuple-element.49), channel_id=1, replica_groups=mesh['x'=4,'zh'=8,'zl'=2,'y'=4,'core'=2] {'y'}, dimensions={0} | all-to-all | bytes 912384 | tf_op jit(solution)/shard_map/all_to_all | solution.py:221
  102.3 0.0 copy-start.1
  102.3 2.6 %shard_map.70 = bf16[4,2,2,24,1024]{4,3,2,1,0:T(8,128)(2,1)} custom-call(s32[3]{0:T(128)S(1)} %pad_add_fusion.place_ref, bf16[4,48,1188]{2,1,0:T(8,128)(2,1)S(1)} %all_to_all.38.grad_ref, bf16[1188,1024]{1,0:T(8,128)(2,1)S(1)} %copy-done, bf16[1188,1024]{1,0:T(8,128)(2,1)S(1)} %get-tuple-element.50.other_ref, ...), custom_call_target="tpu_custom_call", output_to_operand_aliasing={{}: (4, {})} | custom-call | flops 6108672 | bytes 6108672 | tf_op jit(solution)/shard_map/pallas_call | solution.py:27
  104.9 0.0 copy-done.1
  104.9 3.6 %all-to-all-start.5 = ((bf16[16,24,1024]{2,1,0:T(8,128)(2,1)}), bf16[16,24,1024]{2,1,0:T(8,128)(2,1)S(1)}, u32[]{:S(2)}, u32[]{:S(2)}) async-start(bf16[16,24,1024]{2,1,0:T(8,128)(2,1)} %bitcast.8), calls=%async_computation.5 | async-start | bytes 1572864 | tf_op jit(solution)/shard_map/all_to_all | solution.py:233
  108.5 0.0 copy-start.2
  108.5 1.0 copy-done.2
  109.6 0.0 copy-start.3
  109.6 1.5 %shard_map.73 = bf16[4,48,2304]{2,1,0:T(8,128)(2,1)} custom-call(s32[3]{0:T(128)S(1)} %pad_add_fusion.place_ref, bf16[4,2,2,24,1024]{4,3,2,1,0:T(8,128)(2,1)S(1)} %bitcast.11, bf16[4,48,1188]{2,1,0:T(8,128)(2,1)S(1)} %copy-done.2), custom_call_target="tpu_custom_call" | custom-call | flops 67108864 | bytes 67108864 | tf_op jit(solution)/shard_map/pallas_call | solution.py:27
  111.1 2.2 %collective-permute-start.1 = (bf16[4,48,2304]{2,1,0:T(8,128)(2,1)}, bf16[4,48,2304]{2,1,0:T(8,128)(2,1)S(1)}, u32[]{:S(2)}, u32[]{:S(2)}) collective-permute-start(bf16[4,48,2304]{2,1,0:T(8,128)(2,1)} %shard_map.73), channel_id=1, source_target_pairs={{0,1},{1,0},{2,3},{3,2},{4,5},{5,4},{6,7},{7,6},{8,9},{9,8},{10,11... | collective-permute-start | bytes 2654216 | tf_op jit(solution)/shard_map/ppermute | solution.py:232
  113.3 9.0 %all-to-all-done.5 = bf16[16,24,1024]{2,1,0:T(8,128)(2,1)S(1)} async-done(((bf16[16,24,1024]{2,1,0:T(8,128)(2,1)}), bf16[16,24,1024]{2,1,0:T(8,128)(2,1)S(1)}, u32[]{:S(2)}, u32[]{:S(2)}) %all-to-all-start.5) | async-done | bytes 786464 | tf_op jit(solution)/shard_map/all_to_all | solution.py:233
  122.3 1.3 shard_map.71
  123.5 3.4 %all-to-all-start.6 = ((bf16[8,3,2,1024]{3,2,1,0:T(2,128)(2,1)}), bf16[8,3,2,1024]{3,2,1,0:T(2,128)(2,1)S(1)}, u32[]{:S(2)}, u32[]{:S(2)}) async-start(bf16[8,3,2,1024]{3,2,1,0:T(2,128)(2,1)} %shard_map.71), calls=%async_computation.6 | async-start | bytes 196608 | tf_op jit(solution)/shard_map/all_to_all | solution.py:237
  126.9 0.6 shard_map.72.rows_ref
  127.5 0.0 collective-permute-done.1.rest_ref
  127.5 0.0 copy-done.3
  127.5 3.4 %shard_map.74 = bf16[1188,1024]{1,0:T(8,128)(2,1)} custom-call(s32[3]{0:T(128)S(1)} %pad_add_fusion.place_ref, bf16[192,1024]{1,0:T(8,128)(2,1)S(1)} %shard_map.72.rows_ref, bf16[4,48,1188]{2,1,0:T(8,128)(2,1)S(1)} %copy-done.3, bf16[4,48,2304]{2,1,0:T(8,128)(2,1)S(1)} %collective-permute-done.1.rest_ref), custom_call_target="tpu_custom_call" | custom-call | flops 1 | bytes 1 | tf_op jit(solution)/shard_map/pallas_call | solution.py:27
  131.0 11.0 %all-to-all-done.6 = bf16[8,3,2,1024]{3,2,1,0:T(2,128)(2,1)S(1)} async-done(((bf16[8,3,2,1024]{3,2,1,0:T(2,128)(2,1)}), bf16[8,3,2,1024]{3,2,1,0:T(2,128)(2,1)S(1)}, u32[]{:S(2)}, u32[]{:S(2)}) %all-to-all-start.6) | async-done | bytes 98336 | tf_op jit(solution)/shard_map/all_to_all | solution.py:237
  142.0 0.1 reduce_sum.12
  142.1 0.6 reshape.38
  (1 shorter events, 0.0 us)
Async XLA Ops:
  0.6 36.8 %copy-start = (bf16[1188,1024]{1,0:T(8,128)(2,1)S(1)}, bf16[1188,1024]{1,0:T(8,128)(2,1)}, u32[]{:S(2)}) copy-start(bf16[1188,1024]{1,0:T(8,128)(2,1)} %head_ref.1) | copy-start | bytes 7299076
  32.4 18.8 %all-to-all-start.1 = ((bf16[16,24,1024]{2,1,0:T(8,128)(2,1)}), bf16[16,24,1024]{2,1,0:T(8,128)(2,1)S(1)}, u32[]{:S(2)}, u32[]{:S(2)}) async-start(bf16[16,24,1024]{2,1,0:T(8,128)(2,1)} %bitcast), calls=%async_computation.1 | async-start | bytes 1572864 | tf_op jit(solution)/shard_map/all_to_all | solution.py:202
  37.4 13.8 %collective-permute-start = (bf16[1188,1024]{1,0:T(8,128)(2,1)S(1)}, bf16[1188,1024]{1,0:T(8,128)(2,1)}, u32[]{:S(2)}, u32[]{:S(2)}) collective-permute-start(bf16[1188,1024]{1,0:T(8,128)(2,1)S(1)} %copy-done), channel_id=1, source_target_pairs={{0,1},{1,0},{2,3},{3,2},{4,5},{5,4},{6,7},{7,6},{8,9},{9,8},{10,11... | collective-permute-start | bytes 7299080 | tf_op jit(solution)/shard_map/ppermute | solution.py:200
  51.3 20.3 %copy-start.4 = (s32[384]{0:T(512)S(1)}, s32[384]{0:T(512)}, u32[]{:S(2)}) copy-start(s32[384]{0:T(512)} %param.6) | copy-start | bytes 4612
  54.7 36.0 %copy-start.5 = (f32[384]{0:T(512)S(1)}, f32[384]{0:T(512)}, u32[]{:S(2)}) copy-start(f32[384]{0:T(512)} %param.7) | copy-start | bytes 4612
  102.3 2.6 %copy-start.1 = (bf16[4,48,1188]{2,1,0:T(8,128)(2,1)}, bf16[4,48,1188]{2,1,0:T(8,128)(2,1)S(1)}, u32[]{:S(2)}) copy-start(bf16[4,48,1188]{2,1,0:T(8,128)(2,1)S(1)} %all_to_all.38.grad_ref) | copy-start | bytes 1368580
  104.9 17.4 %all-to-all-start.5 = ((bf16[16,24,1024]{2,1,0:T(8,128)(2,1)}), bf16[16,24,1024]{2,1,0:T(8,128)(2,1)S(1)}, u32[]{:S(2)}, u32[]{:S(2)}) async-start(bf16[16,24,1024]{2,1,0:T(8,128)(2,1)} %bitcast.8), calls=%async_computation.5 | async-start | bytes 1572864 | tf_op jit(solution)/shard_map/all_to_all | solution.py:233
  108.5 1.0 copy-start.2
  109.6 17.9 %copy-start.3 = (bf16[4,48,1188]{2,1,0:T(8,128)(2,1)S(1)}, bf16[4,48,1188]{2,1,0:T(8,128)(2,1)}, u32[]{:S(2)}) copy-start(bf16[4,48,1188]{2,1,0:T(8,128)(2,1)} %copy-done.1) | copy-start | bytes 1368580
  111.1 16.4 %collective-permute-start.1 = (bf16[4,48,2304]{2,1,0:T(8,128)(2,1)}, bf16[4,48,2304]{2,1,0:T(8,128)(2,1)S(1)}, u32[]{:S(2)}, u32[]{:S(2)}) collective-permute-start(bf16[4,48,2304]{2,1,0:T(8,128)(2,1)} %shard_map.73), channel_id=1, source_target_pairs={{0,1},{1,0},{2,3},{3,2},{4,5},{5,4},{6,7},{7,6},{8,9},{9,8},{10,11... | collective-permute-start | bytes 2654216 | tf_op jit(solution)/shard_map/ppermute | solution.py:232
  123.5 18.4 %all-to-all-start.6 = ((bf16[8,3,2,1024]{3,2,1,0:T(2,128)(2,1)}), bf16[8,3,2,1024]{3,2,1,0:T(2,128)(2,1)S(1)}, u32[]{:S(2)}, u32[]{:S(2)}) async-start(bf16[8,3,2,1024]{3,2,1,0:T(2,128)(2,1)} %shard_map.71), calls=%async_computation.6 | async-start | bytes 196608 | tf_op jit(solution)/shard_map/all_to_all | solution.py:237

commit v12 on v11

--- a/solution.py
+++ b/solution.py
@@ -13,6 +13,7 @@
 ROW_AXES = ("y", "core")
 SWAP = [(0, 1), (1, 0)]
 LANES = 128
+SUBLANES = 8
 PACK_COST = 2**26
 TILE = 256
 BF16, F32 = jnp.bfloat16, jnp.float32
@@ -85,17 +86,17 @@
     def tile(c, part_ref, span):
         rows = rows_ref[:, :, pl.ds(c, 1)].reshape(-1, rows_ref.shape[-1])
         product = lax.dot_general(rows, part_ref[span, :], (((1,), (1,)), ((), ())), preferred_element_type=F32)
-        return product.reshape(Y, ZL, -1, span.size)
+        return product.reshape(Y, -1, SUBLANES, span.size)
 
     for span in spans(width):
         product = tile(mine, head_ref, span)
-        for zl in range(ZL):
-            out_ref[:, :, pl.ds(zl * width + span.start, span.size)] = product[:, zl]
+        for k in range(product.shape[1]):
+            out_ref[:, :, pl.ds(k * width + span.start, span.size)] = product[:, k]
     keep.wait()
     for span in spans(width):
         product = tile(C - 1 - mine, kept_ref, span)
-        for zl in range(ZL):
-            out_ref[:, :, pl.ds(zl * width + span.start, span.size)] += product[:, zl]
+        for k in range(product.shape[1]):
+            out_ref[:, :, pl.ds(k * width + span.start, span.size)] += product[:, k]
 
 
 def partial_kernel(place_ref, grad_ref, head_ref, other_ref, spent_ref, out_ref, held_ref, sems):
@@ -118,7 +119,7 @@
     for y in range(1, Y):
         logits = logits + parts_ref[y]
     width = logits_ref.shape[1]
-    logits = jnp.concatenate([logits[:, zl * width : (zl + 1) * width] for zl in range(ZL)], axis=0)
+    logits = jnp.concatenate([logits[:, k : k + width] for k in range(0, logits.shape[1], width)], axis=0)
     logits_ref[...] = logits
     top = jnp.max(logits, axis=1, keepdims=True)
     total = jnp.sum(jnp.exp(logits - top), axis=1, keepdims=True)
@@ -206,7 +207,7 @@
     )
     place = jnp.stack([core, row_first, first_column])
     targets, upstream = targets.reshape(-1, LANES), upstream.reshape(-1, LANES)
-    out = [jax.ShapeDtypeStruct((Y, own // ZL, ZL * width), F32), jax.ShapeDtypeStruct(head.shape, BF16)]
+    out = [jax.ShapeDtypeStruct((Y, SUBLANES, own // SUBLANES * width), F32), jax.ShapeDtypeStruct(head.shape, BF16)]
     sem = [pltpu.SemaphoreType.DMA]
     chip_logits, head_other = call(logits_kernel, out, place, by_x, head, head_other, scratch=sem, last=IN_ANY)
     chip_logits, targets, upstream = barrier((chip_logits, targets, upstream))

time: 143 us -> 143 us (level)
  no operation moved by 1% of the time
where the time goes in v12:
time: 143 us
  blocking collectives  75.1 us (53%)
  waiting for transfers between devices  31.4 us (22%)
  starting transfers between devices  16.5 us (12%)
  Pallas kernels  15 us (10%)
  local copies, waits for them, and re-layouts  3.62 us (3%)
    all_to_all x1, blocking collectives, gather_over(): return lax.all_to_all(copies, axis, 0, 0)  29.8 us
    all_to_all x1, blocking collectives, per_device(): stats = lax.all_to_all(stats, VOCAB_AXES, 0, 0)  18.2 us
    all_to_all x1, blocking collectives, per_device(): parts = lax.all_to_all(chip_logits, 'y', 0, 0)  16.7 us
    pallas_call x8, Pallas kernels, call(): pl.pallas_call(kernel, out_shape=out_shape, in_specs=[IN_SMEM] + [IN_VMEM...  15 us
    all_to_all x1, waiting for transfers between devices, per_device(): by_x = lax.all_to_all(copies, NEAR_AXES, 0, 0).reshape(near)  11.4 us
    all_to_all x1, waiting for transfers between devices, per_device(): over_z = lax.all_to_all(over_x, 'zh', 0, 0)  11 us
    all_to_all x1, blocking collectives, per_device(): grad_half = lax.all_to_all(grad_rows, 'y', 0, 0)  10.3 us
    all_to_all x1, waiting for transfers between devices, per_device(): lax.all_to_all(partial.reshape(-1, *near[3:]), NEAR_AXES, 0, 0)  8.99 us
  transfers between devices with their start and end apart: 5, of which 3 were waited for; matrix products, arithmetic and copies ran while one was open for 0% of the time, Pallas kernels for 5%

profile of v12, /device:TPU:8, one launch (start us, length us, event | category | flops | bytes accessed | tf_op | source)
XLA Modules:
  0.0 142.6 jit_solution(17101697220765981900)
XLA Ops:
  0.6 0.0 copy-start
  0.7 0.9 broadcast_in_dim.10
  1.5 0.1 broadcast_in_dim.11
  1.6 29.8 %all_to_all.35 = bf16[8,3,2,1024]{3,2,1,0:T(2,128)(2,1)S(1)} all-to-all(bf16[8,3,2,1024]{3,2,1,0:T(2,128)(2,1)S(1)} %broadcast_in_dim.11), channel_id=1, replica_groups=mesh['x'=4,'zh'=8,'zl'=2,'y'=4,'core'=2] {'zh'}, dimensions={0} | all-to-all | bytes 196608 | tf_op jit(solution)/shard_map/all_to_all | solution.py:43
  31.5 1.0 broadcast_in_dim.12.spent_ref
  32.4 5.0 %all-to-all-start.1 = ((bf16[16,24,1024]{2,1,0:T(8,128)(2,1)}), bf16[16,24,1024]{2,1,0:T(8,128)(2,1)S(1)}, u32[]{:S(2)}, u32[]{:S(2)}) async-start(bf16[16,24,1024]{2,1,0:T(8,128)(2,1)} %bitcast), calls=%async_computation.1 | async-start | bytes 1572864 | tf_op jit(solution)/shard_map/all_to_all | solution.py:203
  37.4 0.0 copy-done
  37.4 2.3 %collective-permute-start = (bf16[1188,1024]{1,0:T(8,128)(2,1)S(1)}, bf16[1188,1024]{1,0:T(8,128)(2,1)}, u32[]{:S(2)}, u32[]{:S(2)}) collective-permute-start(bf16[1188,1024]{1,0:T(8,128)(2,1)S(1)} %copy-done), channel_id=1, source_target_pairs={{0,1},{1,0},{2,3},{3,2},{4,5},{5,4},{6,7},{7,6},{8,9},{9,8},{10,11... | collective-permute-start | bytes 7299080 | tf_op jit(solution)/shard_map/ppermute | solution.py:201
  39.8 11.4 %all-to-all-done.1 = bf16[16,24,1024]{2,1,0:T(8,128)(2,1)S(1)} async-done(((bf16[16,24,1024]{2,1,0:T(8,128)(2,1)}), bf16[16,24,1024]{2,1,0:T(8,128)(2,1)S(1)}, u32[]{:S(2)}, u32[]{:S(2)}) %all-to-all-start.1) | async-done | bytes 786464 | tf_op jit(solution)/shard_map/all_to_all | solution.py:203
  51.2 0.1 pad_add_fusion.place_ref
  51.3 0.0 copy-start.4
  51.3 0.0 collective-permute-done.other_ref
  51.3 3.4 %shard_map.67 = (f32[4,8,7128]{2,1,0:T(8,128)S(1)}, bf16[1188,1024]{1,0:T(8,128)(2,1)S(1)}) custom-call(s32[3]{0:T(128)S(1)} %pad_add_fusion.place_ref, bf16[4,2,2,24,1024]{4,3,2,1,0:T(8,128)(2,1)S(1)} %bitcast.10, bf16[1188,1024]{1,0:T(8,128)(2,1)S(1)} %copy-done, bf16[1188,1024]{1,0:T(8,128)(2,1)} %collective-permute-done.other_ref), custom_call_target="tpu_custom_call" | custom-call | flops 5652480 | bytes 5652480 | tf_op jit(solution)/shard_map/pallas_call | solution.py:28
  54.7 0.0 copy-start.5
  54.7 16.7 %all_to_all.36.parts_ref = f32[4,8,7128]{2,1,0:T(8,128)S(1)} all-to-all(f32[4,8,7128]{2,1,0:T(8,128)S(1)} %get-tuple-element.43), channel_id=1, replica_groups=mesh['x'=4,'zh'=8,'zl'=2,'y'=4,'core'=2] {'y'}, dimensions={0} | all-to-all | bytes 1824768 | tf_op jit(solution)/shard_map/all_to_all | solution.py:214
  71.5 0.0 copy-done.4
  71.5 0.9 shard_map.68
  72.3 18.2 %all_to_all.37.stats_ref = f32[64,1,128]{2,1,0:T(1,128)S(1)} all-to-all(f32[64,1,128]{2,1,0:T(1,128)S(1)} %get-tuple-element.45), channel_id=1, replica_groups=mesh['x'=4,'zh'=8,'zl'=2,'y'=4,'core'=2] {'x','zh','zl'}, dimensions={0} | all-to-all | bytes 65536 | tf_op jit(solution)/shard_map/all_to_all | solution.py:218
  90.6 0.0 copy-done.5
  90.6 1.3 shard_map.69
  91.9 10.3 %all_to_all.38.grad_ref = bf16[4,48,1188]{2,1,0:T(8,128)(2,1)S(1)} all-to-all(bf16[4,48,1188]{2,1,0:T(8,128)(2,1)S(1)} %get-tuple-element.49), channel_id=1, replica_groups=mesh['x'=4,'zh'=8,'zl'=2,'y'=4,'core'=2] {'y'}, dimensions={0} | all-to-all | bytes 912384 | tf_op jit(solution)/shard_map/all_to_all | solution.py:222
  102.2 0.0 copy-start.1
  102.2 2.6 %shard_map.70 = bf16[4,2,2,24,1024]{4,3,2,1,0:T(8,128)(2,1)} custom-call(s32[3]{0:T(128)S(1)} %pad_add_fusion.place_ref, bf16[4,48,1188]{2,1,0:T(8,128)(2,1)S(1)} %all_to_all.38.grad_ref, bf16[1188,1024]{1,0:T(8,128)(2,1)S(1)} %copy-done, bf16[1188,1024]{1,0:T(8,128)(2,1)S(1)} %get-tuple-element.50.other_ref, ...), custom_call_target="tpu_custom_call", output_to_operand_aliasing={{}: (4, {})} | custom-call | flops 6108672 | bytes 6108672 | tf_op jit(solution)/shard_map/pallas_call | solution.py:28
  104.8 0.0 copy-done.1
  104.8 3.6 %all-to-all-start.5 = ((bf16[16,24,1024]{2,1,0:T(8,128)(2,1)}), bf16[16,24,1024]{2,1,0:T(8,128)(2,1)S(1)}, u32[]{:S(2)}, u32[]{:S(2)}) async-start(bf16[16,24,1024]{2,1,0:T(8,128)(2,1)} %bitcast.8), calls=%async_computation.5 | async-start | bytes 1572864 | tf_op jit(solution)/shard_map/all_to_all | solution.py:234
  108.4 0.0 copy-start.2
  108.4 1.0 copy-done.2
  109.5 0.0 copy-start.3
  109.5 1.5 %shard_map.73 = bf16[4,48,2304]{2,1,0:T(8,128)(2,1)} custom-call(s32[3]{0:T(128)S(1)} %pad_add_fusion.place_ref, bf16[4,2,2,24,1024]{4,3,2,1,0:T(8,128)(2,1)S(1)} %bitcast.11, bf16[4,48,1188]{2,1,0:T(8,128)(2,1)S(1)} %copy-done.2), custom_call_target="tpu_custom_call" | custom-call | flops 67108864 | bytes 67108864 | tf_op jit(solution)/shard_map/pallas_call | solution.py:28
  111.0 2.2 %collective-permute-start.1 = (bf16[4,48,2304]{2,1,0:T(8,128)(2,1)}, bf16[4,48,2304]{2,1,0:T(8,128)(2,1)S(1)}, u32[]{:S(2)}, u32[]{:S(2)}) collective-permute-start(bf16[4,48,2304]{2,1,0:T(8,128)(2,1)} %shard_map.73), channel_id=1, source_target_pairs={{0,1},{1,0},{2,3},{3,2},{4,5},{5,4},{6,7},{7,6},{8,9},{9,8},{10,11... | collective-permute-start | bytes 2654216 | tf_op jit(solution)/shard_map/ppermute | solution.py:233
  113.2 9.0 %all-to-all-done.5 = bf16[16,24,1024]{2,1,0:T(8,128)(2,1)S(1)} async-done(((bf16[16,24,1024]{2,1,0:T(8,128)(2,1)}), bf16[16,24,1024]{2,1,0:T(8,128)(2,1)S(1)}, u32[]{:S(2)}, u32[]{:S(2)}) %all-to-all-start.5) | async-done | bytes 786464 | tf_op jit(solution)/shard_map/all_to_all | solution.py:234
  122.1 1.3 shard_map.71
  123.4 3.4 %all-to-all-start.6 = ((bf16[8,3,2,1024]{3,2,1,0:T(2,128)(2,1)}), bf16[8,3,2,1024]{3,2,1,0:T(2,128)(2,1)S(1)}, u32[]{:S(2)}, u32[]{:S(2)}) async-start(bf16[8,3,2,1024]{3,2,1,0:T(2,128)(2,1)} %shard_map.71), calls=%async_computation.6 | async-start | bytes 196608 | tf_op jit(solution)/shard_map/all_to_all | solution.py:238
  126.8 0.6 shard_map.72.rows_ref
  127.4 0.0 collective-permute-done.1.rest_ref
  127.4 0.0 copy-done.3
  127.4 3.4 %shard_map.74 = bf16[1188,1024]{1,0:T(8,128)(2,1)} custom-call(s32[3]{0:T(128)S(1)} %pad_add_fusion.place_ref, bf16[192,1024]{1,0:T(8,128)(2,1)S(1)} %shard_map.72.rows_ref, bf16[4,48,1188]{2,1,0:T(8,128)(2,1)S(1)} %copy-done.3, bf16[4,48,2304]{2,1,0:T(8,128)(2,1)S(1)} %collective-permute-done.1.rest_ref), custom_call_target="tpu_custom_call" | custom-call | flops 1 | bytes 1 | tf_op jit(solution)/shard_map/pallas_call | solution.py:28
  130.8 11.0 %all-to-all-done.6 = bf16[8,3,2,1024]{3,2,1,0:T(2,128)(2,1)S(1)} async-done(((bf16[8,3,2,1024]{3,2,1,0:T(2,128)(2,1)}), bf16[8,3,2,1024]{3,2,1,0:T(2,128)(2,1)S(1)}, u32[]{:S(2)}, u32[]{:S(2)}) %all-to-all-start.6) | async-done | bytes 98336 | tf_op jit(solution)/shard_map/all_to_all | solution.py:238
  141.9 0.1 reduce_sum.12
  142.0 0.6 reshape.38
  (1 shorter events, 0.0 us)
Async XLA Ops:
  0.6 36.8 %copy-start = (bf16[1188,1024]{1,0:T(8,128)(2,1)S(1)}, bf16[1188,1024]{1,0:T(8,128)(2,1)}, u32[]{:S(2)}) copy-start(bf16[1188,1024]{1,0:T(8,128)(2,1)} %head_ref.1) | copy-start | bytes 7299076
  32.4 18.8 %all-to-all-start.1 = ((bf16[16,24,1024]{2,1,0:T(8,128)(2,1)}), bf16[16,24,1024]{2,1,0:T(8,128)(2,1)S(1)}, u32[]{:S(2)}, u32[]{:S(2)}) async-start(bf16[16,24,1024]{2,1,0:T(8,128)(2,1)} %bitcast), calls=%async_computation.1 | async-start | bytes 1572864 | tf_op jit(solution)/shard_map/all_to_all | solution.py:203
  37.4 13.8 %collective-permute-start = (bf16[1188,1024]{1,0:T(8,128)(2,1)S(1)}, bf16[1188,1024]{1,0:T(8,128)(2,1)}, u32[]{:S(2)}, u32[]{:S(2)}) collective-permute-start(bf16[1188,1024]{1,0:T(8,128)(2,1)S(1)} %copy-done), channel_id=1, source_target_pairs={{0,1},{1,0},{2,3},{3,2},{4,5},{5,4},{6,7},{7,6},{8,9},{9,8},{10,11... | collective-permute-start | bytes 7299080 | tf_op jit(solution)/shard_map/ppermute | solution.py:201
  51.3 20.2 %copy-start.4 = (s32[384]{0:T(512)S(1)}, s32[384]{0:T(512)}, u32[]{:S(2)}) copy-start(s32[384]{0:T(512)} %param.6) | copy-start | bytes 4612
  54.7 35.9 %copy-start.5 = (f32[384]{0:T(512)S(1)}, f32[384]{0:T(512)}, u32[]{:S(2)}) copy-start(f32[384]{0:T(512)} %param.7) | copy-start | bytes 4612
  102.2 2.6 %copy-start.1 = (bf16[4,48,1188]{2,1,0:T(8,128)(2,1)}, bf16[4,48,1188]{2,1,0:T(8,128)(2,1)S(1)}, u32[]{:S(2)}) copy-start(bf16[4,48,1188]{2,1,0:T(8,128)(2,1)S(1)} %all_to_all.38.grad_ref) | copy-start | bytes 1368580
  104.8 17.4 %all-to-all-start.5 = ((bf16[16,24,1024]{2,1,0:T(8,128)(2,1)}), bf16[16,24,1024]{2,1,0:T(8,128)(2,1)S(1)}, u32[]{:S(2)}, u32[]{:S(2)}) async-start(bf16[16,24,1024]{2,1,0:T(8,128)(2,1)} %bitcast.8), calls=%async_computation.5 | async-start | bytes 1572864 | tf_op jit(solution)/shard_map/all_to_all | solution.py:234
  108.4 1.0 copy-start.2
  109.5 17.9 %copy-start.3 = (bf16[4,48,1188]{2,1,0:T(8,128)(2,1)S(1)}, bf16[4,48,1188]{2,1,0:T(8,128)(2,1)}, u32[]{:S(2)}) copy-start(bf16[4,48,1188]{2,1,0:T(8,128)(2,1)} %copy-done.1) | copy-start | bytes 1368580
  111.0 16.4 %collective-permute-start.1 = (bf16[4,48,2304]{2,1,0:T(8,128)(2,1)}, bf16[4,48,2304]{2,1,0:T(8,128)(2,1)S(1)}, u32[]{:S(2)}, u32[]{:S(2)}) collective-permute-start(bf16[4,48,2304]{2,1,0:T(8,128)(2,1)} %shard_map.73), channel_id=1, source_target_pairs={{0,1},{1,0},{2,3},{3,2},{4,5},{5,4},{6,7},{7,6},{8,9},{9,8},{10,11... | collective-permute-start | bytes 2654216 | tf_op jit(solution)/shard_map/ppermute | solution.py:233
  123.4 18.4 %all-to-all-start.6 = ((bf16[8,3,2,1024]{3,2,1,0:T(2,128)(2,1)}), bf16[8,3,2,1024]{3,2,1,0:T(2,128)(2,1)S(1)}, u32[]{:S(2)}, u32[]{:S(2)}) async-start(bf16[8,3,2,1024]{3,2,1,0:T(2,128)(2,1)} %shard_map.71), calls=%async_computation.6 | async-start | bytes 196608 | tf_op jit(solution)/shard_map/all_to_all | solution.py:238
